TPU v7x, 512 devices: a whole 4x4x16 slice. The times are simulated.
512 devices in a mesh: dp: 32 (over z, core), owner: 16 (over x, y).
Axes of the slice: x: 4, y: 4, z: 16, core: 2. Of those that a mesh axis runs over, the one named last changes fastest.
Arguments:
- activations: bfloat16 [32768, 8192], P('dp', 'owner'), may hold values from -20 to 20
- key_cotangent: bfloat16 [32768, 1024], P('dp'), may hold values from -15 to 15
- block_owner: int32 [32], replicated, may hold values from 0 to 15, as said below
- left_root: bfloat16 [64, 512, 512], P('owner', 'dp'), may hold values from -1 to 5, as said below
- right_root: bfloat16 [64, 512, 512], P('owner'), may hold values from -1 to 3, as said below
Outputs:
- step_update: float32 [8192, 1024], P(('owner', 'dp'))
Inputs may be any that keep to these rules, and one draw needn't show every extreme that they name: `block_owner`: each owner index is named by at most 4 blocks, and some owner by exactly 4. `left_root`: each slot's matrix is symmetric. `right_root`: each slot's matrix is symmetric.
All inputs are finite; a program needn't handle non-finite values.
Results may differ from a plain program's by a relative error of at most 0.0065.
Values may be sent and summed in bfloat16 or wider, within the bound.
No kernel may reach another device: no remote copies, remote signals or barrier semaphores. Data moves between devices by JAX's collectives and lax.ppermute only.
A program may use at most 128 MiB of HBM per device.

v0:
```python
import jax
import jax.numpy as jnp
from jax import lax
from jax.sharding import PartitionSpec as P


def shards(activations, key_cotangent, block_owner, left_root, right_root):
    slot_count = left_root.shape[0]
    band_rows = left_root.shape[1]
    block_size = left_root.shape[2]
    columns = key_cotangent.shape[1]
    col_blocks = columns // block_size
    owners = lax.axis_size("owner")
    owner_index = lax.axis_index("owner")
    block_total = block_owner.shape[0]
    block_ids = jnp.arange(block_total, dtype=jnp.int32)
    same_owner = block_owner[:, None] == block_owner[None, :]
    slot_of = jnp.sum(
        (same_owner & (block_ids[None, :] < block_ids[:, None])).astype(jnp.int32), axis=1
    )
    slot_range = jnp.arange(slot_count, dtype=jnp.int32)
    owned_int = (
        (block_owner[None, :] == owner_index) & (slot_of[None, :] == slot_range[:, None])
    ).astype(jnp.int32)
    owned = owned_int.astype(jnp.float32)
    grad_rows = lax.psum_scatter(
        lax.dot_general(
            activations, key_cotangent, (((0,), (0,)), ((), ())), preferred_element_type=jnp.float32
        ),
        "dp",
        scatter_dimension=0,
        tiled=True,
    )
    local_blocks = grad_rows.reshape(band_rows, col_blocks, block_size).transpose(1, 0, 2)
    all_bands = lax.all_gather(
        local_blocks.astype(jnp.bfloat16), "owner", axis=0, tiled=True
    ).astype(local_blocks.dtype)
    slot_grads = jnp.einsum("sb,bfk->sfk", owned, all_bands, precision=lax.Precision.HIGHEST)
    grad_sq = jnp.sum(slot_grads * slot_grads, axis=(1, 2))
    grad_total = lax.psum(grad_sq, "dp")
    grads_low = slot_grads.astype(jnp.bfloat16)
    right_mixed = jnp.einsum(
        "sfk,skj->sfj", grads_low, right_root, preferred_element_type=jnp.float32
    ).astype(jnp.bfloat16)
    precond = jnp.einsum(
        "sfr,srj->sfj",
        left_root,
        lax.all_gather(right_mixed, "dp", axis=1, tiled=True),
        preferred_element_type=jnp.float32,
    )
    pre_sq = jnp.sum(precond * precond, axis=(1, 2))
    pre_total = lax.psum(pre_sq, "dp")
    update = precond * jnp.sqrt(grad_total / (pre_total + 1e-06))[:, None, None]
    every_update = lax.all_gather(update.astype(jnp.bfloat16), "owner", axis=0, tiled=True).astype(
        update.dtype
    )
    global_slot = block_owner * slot_count + slot_of
    mine_slots = lax.dynamic_slice_in_dim(global_slot, owner_index * col_blocks, col_blocks, 0)
    picker = (
        jnp.arange(owners * slot_count, dtype=jnp.int32)[None, :] == mine_slots[:, None]
    ).astype(jnp.float32)
    mine_update = jnp.einsum("cg,gfk->cfk", picker, every_update, precision=lax.Precision.HIGHEST)
    return mine_update.transpose(1, 0, 2).reshape(band_rows, col_blocks * block_size)


def solution(mesh):
    in_specs = (
        P("dp", "owner"),
        P("dp", None),
        P(),
        P("owner", "dp", None),
        P("owner", None, None),
    )
    out_specs = P(("owner", "dp"), None)
    return jax.shard_map(shards, mesh=mesh, in_specs=in_specs, out_specs=out_specs, check_vma=False)
```

profile of v0, /device:TPU:1, one launch (start us, length us, event | category | flops | bytes accessed | tf_op | source)
XLA Modules:
  0.0 336.7 jit_solution(6655749514628272846)
XLA Ops:
  6.5 0.0 copy-start
  6.5 0.0 reduce-scatter.2.cloned.1.call-start
  6.5 1.6 copy-done
  8.1 3.8 %fusion.19 = f32[512,1024]{1,0:T(8,128)} fusion(bf16[1024,512]{1,0:T(8,128)(2,1)} %param.5, bf16[1024,1024]{1,0:T(8,128)(2,1)S(1)} %copy-done), kind=kOutput, calls=%fused_computation.29 | convolution fusion | flops 1073741824 | bytes 5242880 | tf_op jit(solution)/shard_map/dot_general | solution.py:27
  12.0 0.0 copy-start.2
  12.0 0.0 reduce-scatter.2.cloned.1.call-update
  12.0 0.0 copy-start.1
  12.0 0.0 all-gather.3.cloned.1.call-start
  12.1 0.6 copy-done.2
  12.6 0.2 convert_reduce_fusion
  12.8 111.4 %reduce-scatter.2.cloned.1.call-done = f32[16,1024]{1,0:T(8,128)} async-done(((f32[512,1024]{1,0:T(8,128)}), f32[16,1024]{1,0:T(8,128)}) %reduce-scatter.2.cloned.1.call-update) | async-done | bytes 65552 | tf_op jit(solution)/shard_map/reduce_scatter | solution.py:26
  124.2 0.8 convert_element_type.36
  125.0 19.2 %all_gather.9 = bf16[32,16,512]{2,1,0:T(8,128)(2,1)S(1)} all-gather(bf16[2,16,512]{2,1,0:T(8,128)(2,1)S(1)} %bitcast.27), channel_id=1, replica_groups=mesh['dp'=32,'owner'=16] {'owner'}, dimensions={0}, use_global_device_ids=true | all-gather | bytes 557056 | tf_op jit(solution)/shard_map/all_gather | solution.py:35
  144.2 0.7 multiply_reduce_fusion.1
  144.9 2.6 convolution_convert_fusion
  147.5 0.0 all-gather.3.cloned.1.call-update
  147.5 0.0 all-gather.5.cloned.1.call-start
  147.5 76.3 %all-gather.3.cloned.1.call-done = bf16[4,512,512]{2,1,0:T(8,128)(2,1)} async-done(((bf16[4,16,512]{2,1,0:T(8,128)(2,1)}), bf16[4,512,512]{2,1,0:T(8,128)(2,1)}) %all-gather.3.cloned.1.call-update) | async-done | bytes 2097168 | tf_op jit(solution)/shard_map/all_gather | solution.py:48
  223.9 0.0 copy-done.1
  223.9 2.1 multiply_reduce_fusion
  226.0 45.4 %all-reduce = (f32[4]{0:T(128)S(1)}, f32[4]{0:T(128)S(1)}) all-reduce(f32[4]{0:T(128)S(1)} %get-tuple-element.7, f32[4]{0:T(128)S(1)} %get-tuple-element.10), channel_id=1, replica_groups=mesh['dp'=32,'owner'=16] {'dp'}, use_global_device_ids=true, to_apply=%region_3.0 | all-reduce | flops 8 | bytes 64 | tf_op jit(solution)/shard_map/psum | solution.py:40
  271.4 0.7 fusion.4
  272.1 0.0 all-gather.5.cloned.1.call-update
  272.1 0.1 dynamic_slice.3
  272.2 54.8 %all-gather.5.cloned.1.call-done = bf16[64,16,512]{2,1,0:T(8,128)(2,1)} async-done(((bf16[4,16,512]{2,1,0:T(8,128)(2,1)}), bf16[64,16,512]{2,1,0:T(8,128)(2,1)}) %all-gather.5.cloned.1.call-update) | async-done | bytes 1048592 | tf_op jit(solution)/shard_map/all_gather | solution.py:54
  327.1 2.4 fusion
  329.5 0.6 copy.15
  (4 shorter events, 0.0 us)
Async XLA Ops:
  6.5 1.6 copy-start
  6.5 117.6 %reduce-scatter.2.cloned.1.call-start = ((), (), s32[]{:S(2)}) async-start(), calls=%async_computation.1 | async-start | bytes 2162688 | tf_op jit(solution)/shard_map/reduce_scatter | solution.py:26
  12.0 0.7 copy-start.2
  12.0 211.9 %copy-start.1 = (bf16[4,16,512]{2,1,0:T(8,128)(2,1)S(1)}, bf16[4,16,512]{2,1,0:T(8,128)(2,1)}, u32[]{:S(2)}) copy-start(bf16[4,16,512]{2,1,0:T(8,128)(2,1)} %param.8) | copy-start | bytes 196612
  12.0 211.9 %all-gather.3.cloned.1.call-start = ((), (), s32[]{:S(2)}) async-start(), calls=%async_computation.2 | async-start | bytes 2162688 | tf_op jit(solution)/shard_map/all_gather | solution.py:48
  147.5 179.6 %all-gather.5.cloned.1.call-start = ((), (), s32[]{:S(2)}) async-start(), calls=%async_computation.3 | async-start | bytes 1114112 | tf_op jit(solution)/shard_map/all_gather | solution.py:54
Sparse Core Ops, SparseCore 0:
  12.1 112.0 reduce-scatter.1
  147.6 76.2 all-gather.2
  272.2 54.7 all-gather.4
where the time goes:
time: 337 us
  waiting for transfers between devices  243 us (72%)
  blocking collectives  64.6 us (19%)
  between operations  13.1 us (4%)
  matrix products  11.6 us (3%)
    reduce_scatter x1, waiting for transfers between devices, shards(): lax.psum_scatter(lax.dot_general(activations, key_cotangent, (((0,), (0,)...  111 us
    all_gather x1, waiting for transfers between devices, shards(): lax.all_gather(right_mixed, 'dp', axis=1, tiled=True)  76.3 us
    all_gather x1, waiting for transfers between devices, shards(): lax.all_gather(update.astype(jnp.bfloat16), 'owner', axis=0, tiled=True)  54.8 us
    psum x1, blocking collectives, shards(): grad_total = lax.psum(grad_sq, 'dp')  45.4 us
    all_gather x1, blocking collectives, shards(): lax.all_gather(local_blocks.astype(jnp.bfloat16), 'owner', axis=0, tiled=...  19.2 us
  transfers between devices with their start and end apart: 3, of which 3 were waited for; matrix products, arithmetic and copies ran while one was open for 0% of the time, Pallas kernels for 0%

commit v1 on v0

v1 whole, which is shorter than its diff:
```python
import jax
import jax.numpy as jnp
from jax import lax
from jax.experimental import pallas as pl
from jax.experimental.pallas import tpu as pltpu
from jax.sharding import Mesh
from jax.sharding import PartitionSpec as P

BF16 = jnp.bfloat16
F32 = jnp.float32
ROWS_FIRST = (((0,), (0,)), ((), ()))
ANY = pl.BlockSpec(memory_space=pl.ANY)
CORE, ZH, ZL, HOLDER, SLOTS = 0, 1, 2, 3, 4


def call(kernel, place, args, grid, in_specs, out_specs, out_shape, scratch=(), vmem=24):
    return pl.pallas_call(
        kernel,
        grid_spec=pltpu.PrefetchScalarGridSpec(
            num_scalar_prefetch=1, grid=grid, in_specs=in_specs, out_specs=out_specs, scratch_shapes=scratch
        ),
        out_shape=out_shape,
        compiler_params=pltpu.CompilerParams(vmem_limit_bytes=vmem * 1024 * 1024),
    )(place, *args)


def whole(*shape):
    return pl.BlockSpec(shape, lambda i, place: (0,) * len(shape))


def shape_of(shape, dtype):
    return jax.ShapeDtypeStruct(shape, dtype)


def theirs_kernel(place, acts, cots, out, acc):
    step = pl.program_id(0)
    part = lax.dot_general(acts[...], cots[...], ROWS_FIRST, preferred_element_type=F32)

    @pl.when(step == 0)
    def _():
        acc[...] = part

    @pl.when(step > 0)
    def _():
        acc[...] += part

    @pl.when(step == pl.num_programs(0) - 1)
    def _():
        out[...] = acc[...].astype(BF16)


def mine_kernel(place, acts, cots, swapped, own, up, down, across, acc):
    step = pl.program_id(0)
    part = lax.dot_general(acts[...], cots[...], ROWS_FIRST, preferred_element_type=F32)

    @pl.when(step == 0)
    def _():
        acc[...] = part + swapped[...].astype(F32)

    @pl.when(step > 0)
    def _():
        acc[...] += part

    @pl.when(step == pl.num_programs(0) - 1)
    def _():
        for ref, offset in ((own, 0), (up, 1), (down, 3), (across, 2)):
            rows = pl.ds(pl.multiple_of(lax.rem(place[ZL] + offset, 4) * 128, 128), 128)
            ref[...] = acc[rows, :].astype(ref.dtype)


def near_kernel(place, own, a, b, c, keep, up, down, across, acc):
    acc[...] = own[...] + a[...].astype(F32) + b[...].astype(F32) + c[...].astype(F32)
    for ref, offset in ((keep, 0), (up, 1), (down, 3), (across, 2)):
        rows = pl.ds(pl.multiple_of(lax.rem(place[ZH] + offset, 4) * 32, 32), 32)
        ref[...] = acc[rows, :].astype(ref.dtype)


def far_kernel(place, own, a, b, c, left, out):
    out[:, :512] = (own[...] + a[...].astype(F32) + b[...].astype(F32) + c[...].astype(F32)).astype(BF16)
    for j in range(3):
        lanes = pl.ds(pl.multiple_of(lax.rem(place[ZH] + j, 4) * 128, 128), 128)
        for half in range(2):
            out[16 * half : 16 * (half + 1), 512 + 128 * j : 640 + 128 * j] = left[half, 0, :, lanes]


def send_kernel(place, left, right, out, sems):
    copies = []
    for i in range(32):
        slot = place[SLOTS + i]
        copies.append(pltpu.make_async_copy(right.at[slot], out.at[i, pl.ds(0, 64)], sems.at[2 * i]))
        copies.append(pltpu.make_async_copy(left.at[slot], out.at[i, pl.ds(64, 16)], sems.at[2 * i + 1]))
    for copy in copies:
        copy.start()
    for copy in copies:
        copy.wait()


def middle_kernel(place, gathered, right, out):
    grad = gathered[:, :512]
    rows = right[:, 0].reshape(128, 512)
    mixed = lax.dot_general(grad, rows, (((1,), (1,)), ((), ())), preferred_element_type=F32).astype(BF16)
    pieces = [
        jnp.concatenate([mixed[32 * (4 * h + a) : 32 * (4 * h + a + 1)] for h in range(4)], axis=0) for a in range(4)
    ]
    pre_sq = jnp.zeros((), F32)
    for a in range(4):
        acc = jnp.zeros((128, 128), F32)
        for j in range(3):
            left = gathered[128 * a : 128 * (a + 1), 512 + 128 * j : 640 + 128 * j]
            acc += jnp.dot(left, pieces[(a + j) % 4], preferred_element_type=F32)
        b = (a + 3) % 4
        left = gathered[128 * b : 128 * (b + 1), 640:768]
        acc += lax.dot_general(left, pieces[b], ROWS_FIRST, preferred_element_type=F32)
        pre_sq += jnp.sum(acc * acc)

        @pl.when(place[ZH] == a)
        def _():
            out[:, :16, :] = acc.reshape(8, 16, 128)

    wide = grad.astype(F32)
    out[:, 16:20, :] = jnp.full((8, 4, 128), pre_sq, F32)
    out[:, 20:24, :] = jnp.full((8, 4, 128), jnp.sum(wide * wide), F32)


def shards(activations, key_cotangent, block_owner, left_root, right_root):
    core = lax.axis_index("core")
    owner = lax.axis_index("owner")
    zh = lax.axis_index("zh")
    zl = lax.axis_index("zl")

    block_ids = jnp.arange(32, dtype=jnp.int32)
    same_owner = block_owner[:, None] == block_owner[None, :]
    slot_of = jnp.sum((same_owner & (block_ids[None, :] < block_ids[:, None])).astype(jnp.int32), axis=1)
    send_slot = jnp.where(block_owner == owner, slot_of, 0).reshape(16, 2).T.reshape(32)
    holder = lax.dynamic_index_in_dim(block_owner, 2 * owner + core, 0, keepdims=False)
    place = jnp.concatenate([jnp.stack([core, zh, zl, holder]).astype(jnp.int32), send_slot])

    steps = 4
    chunk = 1024 // steps
    acts_spec = pl.BlockSpec((chunk, 512), lambda i, place: (i, 0))
    theirs = call(
        theirs_kernel, place, (activations, key_cotangent), (steps,),
        [acts_spec, pl.BlockSpec((chunk, 512), lambda i, place: (i, 1 - place[CORE]))],
        whole(512, 512), shape_of((512, 512), BF16), [pltpu.VMEM((512, 512), F32)],
    )
    swapped = lax.ppermute(theirs, "core", [(0, 1), (1, 0)])

    _, place_late = lax.optimization_barrier((theirs, place))
    sends = call(
        send_kernel, place_late, (left_root, right_root), (1,),
        [whole(4, 16, 512), pl.BlockSpec((4, 64, 512), lambda i, place: (0, 2 * place[ZL] + place[CORE], 0))],
        ANY, shape_of((32, 80, 512), BF16), [pltpu.SemaphoreType.DMA((64,))],
    )
    factors = lax.all_to_all(sends, ("core", "owner"), 0, 0, tiled=True).reshape(2, 16, 80, 512)

    piece = shape_of((128, 512), BF16)
    own, up, down, across = call(
        mine_kernel, place, (activations, key_cotangent, swapped), (steps,),
        [acts_spec, pl.BlockSpec((chunk, 512), lambda i, place: (i, place[CORE])), whole(512, 512)],
        [whole(128, 512)] * 4, [shape_of((128, 512), F32)] + [piece] * 3, [pltpu.VMEM((512, 512), F32)],
    )

    def shift(x, by):
        return lax.ppermute(x, ("zh", "zl"), [(i, (i + by) % 16) for i in range(16)])

    a, b, c = shift(up, 1), shift(down, -1), shift(across, 2)
    band = shape_of((32, 512), BF16)
    own, up, down, across = call(
        near_kernel, place, (own, a, b, c), (1,), [whole(128, 512)] * 4, [whole(32, 512)] * 4,
        [shape_of((32, 512), F32)] + [band] * 3, [pltpu.VMEM((128, 512), F32)],
    )
    a, b, c = shift(up, 4), shift(down, -4), shift(across, 8)
    left_spec = pl.BlockSpec((2, 1, 16, 512), lambda i, place: (0, place[HOLDER], 4, 0))
    part = call(
        far_kernel, place, (own, a, b, c, factors), (1,), [whole(32, 512)] * 4 + [left_spec],
        whole(32, 896), shape_of((32, 896), BF16),
    )
    gathered = lax.all_gather(part, ("zh", "zl"), axis=0, tiled=True)

    right_spec = pl.BlockSpec((2, 1, 64, 512), lambda i, place: (0, place[HOLDER], 0, 0))
    results = call(
        middle_kernel, place, (gathered, factors), (1,), [whole(512, 896), right_spec],
        whole(8, 24, 128), shape_of((8, 24, 128), F32),
    )
    got = lax.all_to_all(results, ("zl", "core"), 0, 0, tiled=True).reshape(4, 2, 24, 128)
    pre_sq = jnp.sum(got[:, :, 16, 0], axis=0)
    grad_sq = got[0, :, 20, 0]
    scale = jnp.sqrt(grad_sq / (pre_sq + 1e-06))
    update = got[:, :, :16, :] * scale[None, :, None, None]
    return update.transpose(2, 1, 0, 3).reshape(16, 1024)


def solution(mesh):
    split = Mesh(mesh.devices.reshape(4, 4, 2, 16), ("zh", "zl", "core", "owner"))
    dp = ("zh", "zl", "core")
    in_specs = (
        P(dp, "owner"),
        P(dp, None),
        P(),
        P("owner", dp, None),
        P("owner", None, None),
    )
    out_specs = P(("owner",) + dp, None)
    return jax.shard_map(shards, mesh=split, in_specs=in_specs, out_specs=out_specs, check_vma=False)
```

time: 337 us -> 129 us (0.38)
  waiting for transfers between devices: 243 us -> 18.6 us
  starting transfers between devices: 0.09 us -> 40.7 us
  blocking collectives: 64.6 us -> 43.5 us
  Pallas kernels: 0 us -> 13.4 us
  between operations: 13.1 us -> 0.18 us
  matrix products: 11.6 us -> 0 us
  local copies, waits for them, and re-layouts: 2.89 us -> 10.2 us
    all_gather x2 -> x0, waiting for transfers between devices: 131 us -> none  [the longest x1 76.3 us: shards(): lax.all_gather(right_mixed, 'dp', axis=1, tiled=True)]
    reduce_scatter x1 -> x0, waiting for transfers between devices: 111 us -> none  [shards(): lax.psum_scatter(lax.dot_general(activations, key_cotangent, (((0,), (0,)...]
    psum x1 -> x0, blocking collectives: 45.4 us -> none  [shards(): grad_total = lax.psum(grad_sq, 'dp')]
    ppermute x0 -> x7, starting transfers between devices: none -> 30 us  [the longest x6 27.9 us: shift(): lax.ppermute(x, ('zh', 'zl'), [(i, (i + by) % 16) for i in range(16)])]
    ppermute x0 -> x7, waiting for transfers between devices: none -> 18.6 us  [the longest x6 17 us: shift(): lax.ppermute(x, ('zh', 'zl'), [(i, (i + by) % 16) for i in range(16)])]
    all_to_all x0 -> x1, blocking collectives: none -> 18.2 us  [shards(): lax.all_to_all(results, ('zl', 'core'), 0, 0, tiled=True)]
    pallas_call x0 -> x6, Pallas kernels: none -> 13.4 us  [call(): pl.pallas_call(kernel, grid_spec=pltpu.PrefetchScalarGridSpec(num_scalar_...]
    dot_general x5 -> x0, matrix products: 11.6 us -> none  [the longest x1 3.84 us: shards(): lax.dot_general(activations, key_cotangent, (((0,), (0,)), ((), ())), pre...]
  transfers between devices with their start and end apart: 3 -> 8, of which waited for: 3 -> 4; matrix products, arithmetic and copies ran while one was open for 0% -> 0% of each run, Pallas kernels for 0% -> 2%
where the time goes in v1:
time: 129 us; the launch traced here: 128 us
  blocking collectives  43.5 us (34%)
  starting transfers between devices  40.7 us (32%)
  waiting for transfers between devices  18.6 us (14%)
  Pallas kernels  13.4 us (10%)
  local copies, waits for them, and re-layouts  10.2 us (8%)
  other arithmetic  1.76 us (1%)
    ppermute x6, starting transfers between devices, shift(): lax.ppermute(x, ('zh', 'zl'), [(i, (i + by) % 16) for i in range(16)])  27.9 us
    all_gather x1, blocking collectives, shards(): gathered = lax.all_gather(part, ('zh', 'zl'), axis=0, tiled=True)  25.3 us
    all_to_all x1, blocking collectives, shards(): lax.all_to_all(results, ('zl', 'core'), 0, 0, tiled=True)  18.2 us
    ppermute x6, waiting for transfers between devices, shift(): lax.ppermute(x, ('zh', 'zl'), [(i, (i + by) % 16) for i in range(16)])  17 us
    pallas_call x6, Pallas kernels, call(): pl.pallas_call(kernel, grid_spec=pltpu.PrefetchScalarGridSpec(num_scalar_...  13.4 us
    all_to_all x1, starting transfers between devices, shards(): lax.all_to_all(sends, ('core', 'owner'), 0, 0, tiled=True)  10.7 us
    unnamed x15, local copies, waits for them, and re-layouts  7.24 us
  transfers between devices with their start and end apart: 8, of which 4 were waited for; matrix products, arithmetic and copies ran while one was open for 0% of the time, Pallas kernels for 2%

profile of v1, /device:TPU:1, one launch (start us, length us, event | category | flops | bytes accessed | tf_op | source)
XLA Modules:
  0.0 128.4 jit_solution(17568895463989535078)
XLA Ops:
  0.0 0.9 convert_reduce_fusion
  0.9 1.3 dynamic_slice.4
  2.2 0.7 compare_select_fusion
  3.1 0.7 concatenate.3.place
  3.8 1.6 %copy-done.1 = bf16[1024,1024]{1,0:T(8,128)(2,1)S(1)} copy-done((bf16[1024,1024]{1,0:T(8,128)(2,1)S(1)}, bf16[1024,1024]{1,0:T(8,128)(2,1)}, u32[]{:S(2)}) %copy-start.1) | copy-done | bytes 2097176
  5.4 1.2 copy-done.3
  6.6 2.4 %shard_map.55 = bf16[512,512]{1,0:T(8,128)(2,1)S(1)} custom-call(s32[36]{0:T(128)S(1)} %concatenate.3.place, bf16[1024,512]{1,0:T(8,128)(2,1)S(1)} %copy-done.3, bf16[1024,1024]{1,0:T(8,128)(2,1)S(1)} %copy-done.1), custom_call_target="tpu_custom_call" | custom-call | tf_op jit(solution)/shard_map/pallas_call | solution.py:17
  9.1 4.8 %shard_map.58 = bf16[32,80,512]{2,1,0:T(8,128)(2,1)S(1)} custom-call(s32[36]{0:T(128)S(1)} %concatenate.3.place, bf16[4,16,512]{2,1,0:T(8,128)(2,1)S(1)} %copy-done.6, bf16[4,512,512]{2,1,0:T(8,128)(2,1)S(1)} %copy-done.5), custom_call_target="tpu_custom_call" | custom-call | tf_op jit(solution)/shard_map/pallas_call | solution.py:17
  13.9 1.5 %copy-done = bf16[32,80,512]{2,1,0:T(8,128)(2,1)} copy-done((bf16[32,80,512]{2,1,0:T(8,128)(2,1)}, bf16[32,80,512]{2,1,0:T(8,128)(2,1)S(1)}, u32[]{:S(2)}) %copy-start) | copy-done | bytes 2621464
  15.4 10.7 %all-to-all-start = ((bf16[32,80,512]{2,1,0:T(8,128)(2,1)}), bf16[32,80,512]{2,1,0:T(8,128)(2,1)S(1)}, u32[]{:S(2)}, u32[]{:S(2)}) async-start(bf16[32,80,512]{2,1,0:T(8,128)(2,1)} %copy-done), calls=%async_computation | async-start | bytes 5242880 | tf_op jit(solution)/shard_map/all_to_all | solution.py:154
  26.1 2.2 %collective-permute-start = (bf16[512,512]{1,0:T(8,128)(2,1)S(1)}, bf16[512,512]{1,0:T(8,128)(2,1)S(1)}, u32[]{:S(2)}, u32[]{:S(2)}) collective-permute-start(bf16[512,512]{1,0:T(8,128)(2,1)S(1)} %shard_map.55), channel_id=1, source_target_pairs={{0,16},{16,0},{1,17},{17,1},{2,18},{18,2},{3,19},{19,3},{4,20},{20... | collective-permute-start | bytes 1572872 | tf_op jit(solution)/shard_map/ppermute | solution.py:146
  28.2 1.6 %collective-permute-done.swapped = bf16[512,512]{1,0:T(8,128)(2,1)S(1)} collective-permute-done((bf16[512,512]{1,0:T(8,128)(2,1)S(1)}, bf16[512,512]{1,0:T(8,128)(2,1)S(1)}, u32[]{:S(2)}, u32[]{:S(2)}) %collective-permute-start) | collective-permute-done | bytes 524320 | tf_op jit(solution)/shard_map/ppermute | solution.py:146
  29.9 1.6 %copy-done.2 = bf16[1024,1024]{1,0:T(8,128)(2,1)S(1)} copy-done((bf16[1024,1024]{1,0:T(8,128)(2,1)S(1)}, bf16[1024,1024]{1,0:T(8,128)(2,1)}, u32[]{:S(2)}) %copy-start.2) | copy-done | bytes 2097176
  31.5 1.2 copy-done.4
  32.7 2.5 %shard_map.56 = (f32[128,512]{1,0:T(8,128)S(1)}, bf16[128,512]{1,0:T(8,128)(2,1)S(1)}, bf16[128,512]{1,0:T(8,128)(2,1)S(1)}, bf16[128,512]{1,0:T(8,128)(2,1)S(1)}) custom-call(s32[36]{0:T(128)S(1)} %concatenate.3.place, bf16[1024,512]{1,0:T(8,128)(2,1)S(1)} %copy-done.4, bf16[1024,1024]{1,0:T(8,128)(2,1)S(1)} %copy-done.2, ...), custom_call_target="tpu_custom_call" | custom-call | tf_op jit(solution)/shard_map/pallas_call | solution.py:17
  35.2 1.9 %collective-permute-start.1 = (bf16[128,512]{1,0:T(8,128)(2,1)S(1)}, bf16[128,512]{1,0:T(8,128)(2,1)S(1)}, u32[]{:S(2)}, u32[]{:S(2)}) collective-permute-start(bf16[128,512]{1,0:T(8,128)(2,1)S(1)} %get-tuple-element.15), channel_id=1, source_target_pairs={{0,32},{32,64},{64,96},{96,128},{128,160},{160,192},{192,224},{224... | collective-permute-start | bytes 393224 | tf_op jit(solution)/shard_map/ppermute | solution.py:164
  37.1 9.0 %collective-permute-start.2 = (bf16[128,512]{1,0:T(8,128)(2,1)S(1)}, bf16[128,512]{1,0:T(8,128)(2,1)S(1)}, u32[]{:S(2)}, u32[]{:S(2)}) collective-permute-start(bf16[128,512]{1,0:T(8,128)(2,1)S(1)} %get-tuple-element.16), channel_id=1, source_target_pairs={{0,480},{32,0},{64,32},{96,64},{128,96},{160,128},{192,160},{224,1... | collective-permute-start | bytes 393224 | tf_op jit(solution)/shard_map/ppermute | solution.py:164
  46.1 1.9 %collective-permute-start.3 = (bf16[128,512]{1,0:T(8,128)(2,1)S(1)}, bf16[128,512]{1,0:T(8,128)(2,1)S(1)}, u32[]{:S(2)}, u32[]{:S(2)}) collective-permute-start(bf16[128,512]{1,0:T(8,128)(2,1)S(1)} %get-tuple-element.17), channel_id=1, source_target_pairs={{0,64},{32,96},{64,128},{96,160},{128,192},{160,224},{192,256},{22... | collective-permute-start | bytes 393224 | tf_op jit(solution)/shard_map/ppermute | solution.py:164
  48.1 0.7 collective-permute-done.2.b
  48.8 8.7 %collective-permute-done.3.c = bf16[128,512]{1,0:T(8,128)(2,1)S(1)} collective-permute-done((bf16[128,512]{1,0:T(8,128)(2,1)S(1)}, bf16[128,512]{1,0:T(8,128)(2,1)S(1)}, u32[]{:S(2)}, u32[]{:S(2)}) %collective-permute-start.3) | collective-permute-done | bytes 131104 | tf_op jit(solution)/shard_map/ppermute | solution.py:164
  57.5 0.6 shard_map.57
  58.1 1.9 %collective-permute-start.4 = (bf16[32,512]{1,0:T(8,128)(2,1)S(1)}, bf16[32,512]{1,0:T(8,128)(2,1)S(1)}, u32[]{:S(2)}, u32[]{:S(2)}) collective-permute-start(bf16[32,512]{1,0:T(8,128)(2,1)S(1)} %get-tuple-element.19), channel_id=1, source_target_pairs={{0,128},{32,160},{64,192},{96,224},{128,256},{160,288},{192,320},{... | collective-permute-start | bytes 98312 | tf_op jit(solution)/shard_map/ppermute | solution.py:164
  60.1 7.3 %collective-permute-start.5 = (bf16[32,512]{1,0:T(8,128)(2,1)S(1)}, bf16[32,512]{1,0:T(8,128)(2,1)S(1)}, u32[]{:S(2)}, u32[]{:S(2)}) collective-permute-start(bf16[32,512]{1,0:T(8,128)(2,1)S(1)} %get-tuple-element.20), channel_id=1, source_target_pairs={{0,384},{32,416},{64,448},{96,480},{128,0},{160,32},{192,64},{224,... | collective-permute-start | bytes 98312 | tf_op jit(solution)/shard_map/ppermute | solution.py:164
  67.3 5.8 %collective-permute-start.6 = (bf16[32,512]{1,0:T(8,128)(2,1)S(1)}, bf16[32,512]{1,0:T(8,128)(2,1)S(1)}, u32[]{:S(2)}, u32[]{:S(2)}) collective-permute-start(bf16[32,512]{1,0:T(8,128)(2,1)S(1)} %get-tuple-element.21), channel_id=1, source_target_pairs={{0,256},{32,288},{64,320},{96,352},{128,384},{160,416},{192,448},{... | collective-permute-start | bytes 98312 | tf_op jit(solution)/shard_map/ppermute | solution.py:164
  73.2 7.5 %collective-permute-done.6.c = bf16[32,512]{1,0:T(8,128)(2,1)S(1)} collective-permute-done((bf16[32,512]{1,0:T(8,128)(2,1)S(1)}, bf16[32,512]{1,0:T(8,128)(2,1)S(1)}, u32[]{:S(2)}, u32[]{:S(2)}) %collective-permute-start.6) | collective-permute-done | bytes 32800 | tf_op jit(solution)/shard_map/ppermute | solution.py:164
  80.7 0.6 shard_map.59
  81.3 25.3 %all_gather.3.gathered = bf16[512,896]{1,0:T(8,128)(2,1)S(1)} all-gather(bf16[32,896]{1,0:T(8,128)(2,1)S(1)} %shard_map.59), channel_id=1, replica_groups=mesh['zh'=4,'zl'=4,'core'=2,'owner'=16] {'zh','zl'}, dimensions={0}, use_global_device_ids=true | all-gather | bytes 974848 | tf_op jit(solution)/shard_map/all_gather | solution.py:178
  106.6 2.6 %shard_map.60 = f32[8,24,128]{2,1,0:T(8,128)S(1)} custom-call(s32[36]{0:T(128)S(1)} %concatenate.3.place, bf16[512,896]{1,0:T(8,128)(2,1)S(1)} %all_gather.3.gathered, bf16[2,16,80,512]{3,2,1,0:T(8,128)(2,1)S(1)} %bitcast.15), custom_call_target="tpu_custom_call" | custom-call | tf_op jit(solution)/shard_map/pallas_call | solution.py:17
  109.2 18.2 %all_to_all.10 = f32[8,24,128]{2,1,0:T(8,128)S(1)} all-to-all(f32[8,24,128]{2,1,0:T(8,128)S(1)} %shard_map.60), channel_id=1, replica_groups=mesh['zh'=4,'zl'=4,'core'=2,'owner'=16] {'zl','core'}, dimensions={0} | all-to-all | bytes 196608 | tf_op jit(solution)/shard_map/all_to_all | solution.py:185
  127.4 0.1 slice_reduce_fusion
  127.5 0.1 copy.15
  127.7 0.7 reshape.30
  (20 shorter events, 0.4 us)
Async XLA Ops:
  0.0 9.1 %copy-start.6 = (bf16[4,16,512]{2,1,0:T(8,128)(2,1)S(1)}, bf16[4,16,512]{2,1,0:T(8,128)(2,1)}, u32[]{:S(2)}) copy-start(bf16[4,16,512]{2,1,0:T(8,128)(2,1)} %left.1) | copy-start | bytes 196612
  3.8 1.6 %copy-start.1 = (bf16[1024,1024]{1,0:T(8,128)(2,1)S(1)}, bf16[1024,1024]{1,0:T(8,128)(2,1)}, u32[]{:S(2)}) copy-start(bf16[1024,1024]{1,0:T(8,128)(2,1)} %cots.3) | copy-start | bytes 6291460
  5.4 1.2 copy-start.3
  6.6 2.4 %copy-start.5 = (bf16[4,512,512]{2,1,0:T(8,128)(2,1)S(1)}, bf16[4,512,512]{2,1,0:T(8,128)(2,1)}, u32[]{:S(2)}) copy-start(bf16[4,512,512]{2,1,0:T(8,128)(2,1)} %right.1) | copy-start | bytes 6291460
  13.9 1.5 %copy-start = (bf16[32,80,512]{2,1,0:T(8,128)(2,1)}, bf16[32,80,512]{2,1,0:T(8,128)(2,1)S(1)}, u32[]{:S(2)}) copy-start(bf16[32,80,512]{2,1,0:T(8,128)(2,1)S(1)} %shard_map.58) | copy-start | bytes 7864324
  15.4 65.4 %all-to-all-start = ((bf16[32,80,512]{2,1,0:T(8,128)(2,1)}), bf16[32,80,512]{2,1,0:T(8,128)(2,1)S(1)}, u32[]{:S(2)}, u32[]{:S(2)}) async-start(bf16[32,80,512]{2,1,0:T(8,128)(2,1)} %copy-done), calls=%async_computation | async-start | bytes 5242880 | tf_op jit(solution)/shard_map/all_to_all | solution.py:154
  26.1 3.8 %collective-permute-start = (bf16[512,512]{1,0:T(8,128)(2,1)S(1)}, bf16[512,512]{1,0:T(8,128)(2,1)S(1)}, u32[]{:S(2)}, u32[]{:S(2)}) collective-permute-start(bf16[512,512]{1,0:T(8,128)(2,1)S(1)} %shard_map.55), channel_id=1, source_target_pairs={{0,16},{16,0},{1,17},{17,1},{2,18},{18,2},{3,19},{19,3},{4,20},{20... | collective-permute-start | bytes 1572872 | tf_op jit(solution)/shard_map/ppermute | solution.py:146
  29.9 1.6 %copy-start.2 = (bf16[1024,1024]{1,0:T(8,128)(2,1)S(1)}, bf16[1024,1024]{1,0:T(8,128)(2,1)}, u32[]{:S(2)}) copy-start(bf16[1024,1024]{1,0:T(8,128)(2,1)} %cots.3) | copy-start | bytes 6291460
  31.5 1.2 copy-start.4
  35.2 12.9 %collective-permute-start.1 = (bf16[128,512]{1,0:T(8,128)(2,1)S(1)}, bf16[128,512]{1,0:T(8,128)(2,1)S(1)}, u32[]{:S(2)}, u32[]{:S(2)}) collective-permute-start(bf16[128,512]{1,0:T(8,128)(2,1)S(1)} %get-tuple-element.15), channel_id=1, source_target_pairs={{0,32},{32,64},{64,96},{96,128},{128,160},{160,192},{192,224},{224... | collective-permute-start | bytes 393224 | tf_op jit(solution)/shard_map/ppermute | solution.py:164
  37.1 11.7 %collective-permute-start.2 = (bf16[128,512]{1,0:T(8,128)(2,1)S(1)}, bf16[128,512]{1,0:T(8,128)(2,1)S(1)}, u32[]{:S(2)}, u32[]{:S(2)}) collective-permute-start(bf16[128,512]{1,0:T(8,128)(2,1)S(1)} %get-tuple-element.16), channel_id=1, source_target_pairs={{0,480},{32,0},{64,32},{96,64},{128,96},{160,128},{192,160},{224,1... | collective-permute-start | bytes 393224 | tf_op jit(solution)/shard_map/ppermute | solution.py:164
  46.1 11.4 %collective-permute-start.3 = (bf16[128,512]{1,0:T(8,128)(2,1)S(1)}, bf16[128,512]{1,0:T(8,128)(2,1)S(1)}, u32[]{:S(2)}, u32[]{:S(2)}) collective-permute-start(bf16[128,512]{1,0:T(8,128)(2,1)S(1)} %get-tuple-element.17), channel_id=1, source_target_pairs={{0,64},{32,96},{64,128},{96,160},{128,192},{160,224},{192,256},{22... | collective-permute-start | bytes 393224 | tf_op jit(solution)/shard_map/ppermute | solution.py:164
  58.1 15.0 %collective-permute-start.4 = (bf16[32,512]{1,0:T(8,128)(2,1)S(1)}, bf16[32,512]{1,0:T(8,128)(2,1)S(1)}, u32[]{:S(2)}, u32[]{:S(2)}) collective-permute-start(bf16[32,512]{1,0:T(8,128)(2,1)S(1)} %get-tuple-element.19), channel_id=1, source_target_pairs={{0,128},{32,160},{64,192},{96,224},{128,256},{160,288},{192,320},{... | collective-permute-start | bytes 98312 | tf_op jit(solution)/shard_map/ppermute | solution.py:164
  60.1 13.1 %collective-permute-start.5 = (bf16[32,512]{1,0:T(8,128)(2,1)S(1)}, bf16[32,512]{1,0:T(8,128)(2,1)S(1)}, u32[]{:S(2)}, u32[]{:S(2)}) collective-permute-start(bf16[32,512]{1,0:T(8,128)(2,1)S(1)} %get-tuple-element.20), channel_id=1, source_target_pairs={{0,384},{32,416},{64,448},{96,480},{128,0},{160,32},{192,64},{224,... | collective-permute-start | bytes 98312 | tf_op jit(solution)/shard_map/ppermute | solution.py:164
  67.3 13.4 %collective-permute-start.6 = (bf16[32,512]{1,0:T(8,128)(2,1)S(1)}, bf16[32,512]{1,0:T(8,128)(2,1)S(1)}, u32[]{:S(2)}, u32[]{:S(2)}) collective-permute-start(bf16[32,512]{1,0:T(8,128)(2,1)S(1)} %get-tuple-element.21), channel_id=1, source_target_pairs={{0,256},{32,288},{64,320},{96,352},{128,384},{160,416},{192,448},{... | collective-permute-start | bytes 98312 | tf_op jit(solution)/shard_map/ppermute | solution.py:164

commit v2 on v0

v2 whole, which is shorter than its diff:
```python
import jax
import jax.numpy as jnp
from jax import lax
from jax.experimental import pallas as pl
from jax.experimental.pallas import tpu as pltpu
from jax.sharding import Mesh
from jax.sharding import PartitionSpec as P

BF16 = jnp.bfloat16
F32 = jnp.float32
ROWS_FIRST = (((0,), (0,)), ((), ()))
ANY = pl.BlockSpec(memory_space=pl.ANY)


def axis(name):
    return lax.axis_index(name)


def column():
    return axis("core") ^ (axis("zl") & 1)


def block_id():
    return 2 * axis("owner") + column()


def call(kernel, args, grid, in_specs, out_specs, out_shape, scratch=(), prefetch=0, vmem=24, cost=None):
    return pl.pallas_call(
        kernel,
        grid_spec=pltpu.PrefetchScalarGridSpec(
            num_scalar_prefetch=prefetch, grid=grid, in_specs=in_specs, out_specs=out_specs, scratch_shapes=scratch
        ),
        out_shape=out_shape,
        compiler_params=pltpu.CompilerParams(vmem_limit_bytes=vmem * 1024 * 1024),
        cost_estimate=cost,
    )(*args)


WAIT = pl.CostEstimate(flops=60_000_000_000, bytes_accessed=0, transcendentals=0)


def whole(*shape):
    return pl.BlockSpec(shape, lambda i, *_: (0,) * len(shape))


def shape_of(shape, dtype):
    return jax.ShapeDtypeStruct(shape, dtype)


def slots_to_send(owners, slots):
    held = jnp.int32(0)
    for b in range(32):
        hit = owners[b] == axis("owner")
        slots[b] = jnp.where(hit, held, 0)
        held += hit.astype(jnp.int32)


def send_kernel(owners, left, right, left_out, right_out, slots):
    slots_to_send(owners, slots)
    flip = axis("zl") & 1
    for i in range(16):
        right_out[i] = right[slots[2 * i + column()]]
        for core in range(2):
            left_out[16 * core + i] = left[slots[2 * i + (core ^ flip)]]


def split_kernel(mine, swapped, across, up, down, own):
    for ref, offset in ((across, 2), (up, 1), (down, 3), (own, 0)):
        for h in range(4):
            rows = pl.ds(pl.multiple_of(128 * h + 32 * lax.rem(axis("zl") + offset, 4), 32), 32)
            ref[32 * h : 32 * (h + 1)] = (mine[rows, :] + swapped[rows, :].astype(F32)).astype(ref.dtype)


def near_kernel(own, a, b, c, across, up, down, keep, acc):
    acc[...] = own[...] + a[...].astype(F32) + b[...].astype(F32) + c[...].astype(F32)
    for ref, offset in ((across, 2), (up, 1), (down, 3), (keep, 0)):
        rows = pl.ds(pl.multiple_of(lax.rem(axis("zh") + offset, 4) * 32, 32), 32)
        ref[...] = acc[rows, :].astype(ref.dtype)


def far_kernel(owners, own, a, b, c, left, out):
    out[:, :512] = (own[...] + a[...].astype(F32) + b[...].astype(F32) + c[...].astype(F32)).astype(BF16)
    for j in range(3):
        lanes = pl.ds(pl.multiple_of(lax.rem(axis("zh") + j, 4) * 128, 128), 128)
        for half in range(2):
            out[16 * half : 16 * (half + 1), 512 + 128 * j : 640 + 128 * j] = left[half, 0, :, lanes]


def middle_kernel(owners, gathered, rights, out, right, sem):
    fetch = pltpu.make_async_copy(rights.at[owners[block_id()]], right, sem)
    fetch.start()
    grad = gathered[:, :512]
    wide = grad.astype(F32)
    grad_sq = jnp.sum(wide * wide)
    fetch.wait()
    mixed = jnp.dot(right[...], grad, preferred_element_type=F32).astype(BF16)
    pieces = [mixed[:, 128 * b : 128 * (b + 1)] for b in range(4)]
    total = jnp.zeros((128, 128), F32)
    for a in range(4):
        left = gathered[128 * a : 128 * (a + 1), 640:768]
        acc = lax.dot_general(pieces[(a + 1) % 4], left, (((1,), (1,)), ((), ())), preferred_element_type=F32)
        for j in range(3):
            b = (a - j) % 4
            left = gathered[128 * b : 128 * (b + 1), 512 + 128 * j : 640 + 128 * j]
            acc += jnp.dot(pieces[b], left, preferred_element_type=F32)
        total += acc * acc

        @pl.when(axis("zh") == a)
        def _():
            out[:, :16, :] = acc.T.reshape(8, 16, 128)

    out[:, 16:20, :] = jnp.full((8, 4, 128), jnp.sum(total), F32)
    out[:, 20:24, :] = jnp.full((8, 4, 128), grad_sq, F32)


def place_kernel(got, out):
    for block in range(2):
        parts = [2 * l + (block ^ (l & 1)) for l in range(4)]
        pre_sq = sum(got[i, 16:17, :] for i in parts)
        scale = jnp.sqrt(got[parts[0], 20:21, :] / (pre_sq + 1e-06))
        for l, i in enumerate(parts):
            out[:, 512 * block + 128 * l : 512 * block + 128 * (l + 1)] = got[i, :16, :] * scale


def shards(activations, key_cotangent, block_owner, left_root, right_root):
    def product(half):
        columns = lax.dynamic_slice_in_dim(key_cotangent, half * 512, 512, 1)
        return lax.dot_general(columns, activations, ROWS_FIRST, preferred_element_type=F32)

    theirs = product(1 - column()).astype(BF16)
    swapped = lax.ppermute(theirs, "core", [(0, 1), (1, 0)])
    mine = product(column())

    left_sends, right_sends = call(
        send_kernel, (block_owner, left_root, right_root), (1,),
        [whole(4, 16, 512), pl.BlockSpec((4, 128, 512), lambda i, owners: (0, axis("zl"), 0))],
        [whole(32, 16, 512), whole(16, 128, 512)],
        [shape_of((32, 16, 512), BF16), shape_of((16, 128, 512), BF16)],
        [pltpu.SMEM((32,), jnp.int32)], prefetch=1,
    )

    piece = shape_of((128, 512), BF16)
    across, up, down, own = call(
        split_kernel, (mine, swapped), (1,), [whole(512, 512)] * 2,
        [whole(128, 512)] * 4, [piece] * 3 + [shape_of((128, 512), F32)],
    )
    own, left_sends = lax.optimization_barrier((own, left_sends))

    def shift(x, by):
        moves = [(i, (i + 2 * by) % 32 ^ (by & 1)) for i in range(32)]
        return lax.ppermute(x, ("zh", "zl", "core"), moves)

    a, b, c = shift(across, 2), shift(up, 1), shift(down, -1)
    lefts = lax.all_to_all(left_sends, ("core", "owner"), 0, 0, tiled=True).reshape(2, 16, 16, 512)
    band = shape_of((32, 512), BF16)
    across, up, down, own = call(
        near_kernel, (own, a, b, c), (1,), [whole(128, 512)] * 4, [whole(32, 512)] * 4,
        [band] * 3 + [shape_of((32, 512), F32)], [pltpu.VMEM((128, 512), F32)], cost=WAIT,
    )
    own, right_sends = lax.optimization_barrier((own, right_sends))
    a, b, c = shift(across, 8), shift(up, 4), shift(down, -4)
    rights = lax.all_to_all(right_sends, "owner", 0, 0, tiled=True)
    part = call(
        far_kernel, (block_owner, own, a, b, c, lefts), (1,),
        [whole(32, 512)] * 4 + [pl.BlockSpec((2, 1, 16, 512), lambda i, owners: (0, owners[block_id()], 0, 0))],
        whole(32, 896), shape_of((32, 896), BF16), prefetch=1, cost=WAIT,
    )
    groups = [[2 * z + (z & 1 ^ c) for z in range(16)] for c in range(2)]
    gathered = lax.all_gather(part, ("zh", "zl", "core"), axis=0, tiled=True, axis_index_groups=groups)

    results = call(
        middle_kernel, (block_owner, gathered, rights), (1,),
        [whole(512, 896), ANY], whole(8, 24, 128), shape_of((8, 24, 128), F32),
        [pltpu.VMEM((128, 512), BF16), pltpu.SemaphoreType.DMA], prefetch=1,
    )
    got = lax.all_to_all(results, ("zl", "core"), 0, 0, tiled=True)
    return call(place_kernel, (got,), (1,), [whole(8, 24, 128)], whole(16, 1024), shape_of((16, 1024), F32))


def solution(mesh):
    split = Mesh(mesh.devices.reshape(4, 4, 2, 16), ("zh", "zl", "core", "owner"))
    dp = ("zh", "zl", "core")
    in_specs = (
        P(dp, "owner"),
        P(dp, None),
        P(),
        P("owner", dp, None),
        P("owner", None, None),
    )
    out_specs = P(("owner",) + dp, None)
    return jax.shard_map(shards, mesh=split, in_specs=in_specs, out_specs=out_specs, check_vma=False)
```

time: 337 us -> 106 us (0.31)
  waiting for transfers between devices: 243 us -> 0.02 us
  starting transfers between devices: 0.09 us -> 52 us
  blocking collectives: 64.6 us -> 39.2 us
  between operations: 13.1 us -> 0.23 us
  matrix products: 11.6 us -> 4.08 us
  Pallas kernels: 0 us -> 6.4 us
    all_gather x2 -> x0, waiting for transfers between devices: 131 us -> none  [the longest x1 76.3 us: shards(): lax.all_gather(right_mixed, 'dp', axis=1, tiled=True)]
    reduce_scatter x1 -> x0, waiting for transfers between devices: 111 us -> none  [shards(): lax.psum_scatter(lax.dot_general(activations, key_cotangent, (((0,), (0,)...]
    psum x1 -> x0, blocking collectives: 45.4 us -> none  [shards(): grad_total = lax.psum(grad_sq, 'dp')]
    ppermute x0 -> x7, starting transfers between devices: none -> 37.7 us  [the longest x6 28.9 us: shift(): return lax.ppermute(x, ('zh', 'zl', 'core'), moves)]
    all_to_all x0 -> x2, starting transfers between devices: none -> 14.3 us  [the longest x1 7.6 us: shards(): lax.all_to_all(left_sends, ('core', 'owner'), 0, 0, tiled=True)]
    all_gather x1, blocking collectives: 19.2 us -> 31.5 us  [shards(): lax.all_gather(part, ('zh', 'zl', 'core'), axis=0, tiled=True, axis_index...]
    all_to_all x0 -> x1, blocking collectives: none -> 7.7 us  [shards(): got = lax.all_to_all(results, ('zl', 'core'), 0, 0, tiled=True)]
    dot_general x5 -> x2, matrix products: 11.6 us -> 4.08 us  [product(): lax.dot_general(columns, activations, ROWS_FIRST, preferred_element_type=...]
  transfers between devices with their start and end apart: 3 -> 9, of which waited for: 3 -> 0; matrix products, arithmetic and copies ran while one was open for 0% -> 2% of each run, Pallas kernels for 0% -> 2%
where the time goes in v2:
time: 106 us; the launch traced here: 105 us
  starting transfers between devices  52 us (49%)
  blocking collectives  39.2 us (37%)
  Pallas kernels  6.4 us (6%)
  matrix products  4.08 us (4%)
  local copies, waits for them, and re-layouts  2.95 us (3%)
    all_gather x1, blocking collectives, shards(): lax.all_gather(part, ('zh', 'zl', 'core'), axis=0, tiled=True, axis_index...  31.5 us
    ppermute x6, starting transfers between devices, shift(): return lax.ppermute(x, ('zh', 'zl', 'core'), moves)  28.9 us
    ppermute x1, starting transfers between devices, shards(): swapped = lax.ppermute(theirs, 'core', [(0, 1), (1, 0)])  8.78 us
    all_to_all x1, blocking collectives, shards(): got = lax.all_to_all(results, ('zl', 'core'), 0, 0, tiled=True)  7.7 us
    all_to_all x1, starting transfers between devices, shards(): lax.all_to_all(left_sends, ('core', 'owner'), 0, 0, tiled=True)  7.6 us
    all_to_all x1, starting transfers between devices, shards(): rights = lax.all_to_all(right_sends, 'owner', 0, 0, tiled=True)  6.75 us
    pallas_call x6, Pallas kernels, call(): pl.pallas_call(kernel, grid_spec=pltpu.PrefetchScalarGridSpec(num_scalar_...  6.4 us
    dot_general x2, matrix products, product(): lax.dot_general(columns, activations, ROWS_FIRST, preferred_element_type=...  4.08 us
  transfers between devices with their start and end apart: 9, of which 0 were waited for; matrix products, arithmetic and copies ran while one was open for 2% of the time, Pallas kernels for 2%

profile of v2, /device:TPU:1, one launch (start us, length us, event | category | flops | bytes accessed | tf_op | source)
XLA Modules:
  0.0 104.9 jit_solution(6357274622530290055)
XLA Ops:
  0.0 1.6 %copy-done = bf16[1024,1024]{1,0:T(8,128)(2,1)S(1)} copy-done((bf16[1024,1024]{1,0:T(8,128)(2,1)S(1)}, bf16[1024,1024]{1,0:T(8,128)(2,1)}, u32[]{:S(2)}) %copy-start) | copy-done | bytes 2097176
  1.6 2.0 %convolution_convert_fusion = bf16[512,512]{1,0:T(8,128)(2,1)S(1)} fusion(bf16[1024,512]{1,0:T(8,128)(2,1)} %param.5, bf16[1024,1024]{1,0:T(8,128)(2,1)S(1)} %copy-done, s32[]{:T(128)S(6)} %select_n.7), kind=kOutput, calls=%fused_computation | convolution fusion | flops 537133056 | bytes 2621444 | tf_op jit(solution)/shard_map/dot_general | solution.py:128
  3.6 8.8 %collective-permute-start = (bf16[512,512]{1,0:T(8,128)(2,1)S(1)}, bf16[512,512]{1,0:T(8,128)(2,1)S(1)}, u32[]{:S(2)}, u32[]{:S(2)}) collective-permute-start(bf16[512,512]{1,0:T(8,128)(2,1)S(1)} %convolution_convert_fusion), channel_id=1, source_target_pairs={{0,16},{16,0},{1,17},{17,1},{2,18},{18,2},{3,19},{19,3},{4,20},{20... | collective-permute-start | bytes 1572872 | tf_op jit(solution)/shard_map/ppermute | solution.py:131
  12.4 0.0 copy-start.1
  12.4 0.0 copy-start.3
  12.4 0.0 copy-start.4
  12.4 2.1 %fusion.1.mine = f32[512,512]{1,0:T(8,128)S(1)} fusion(bf16[1024,512]{1,0:T(8,128)(2,1)} %param.5, bf16[1024,1024]{1,0:T(8,128)(2,1)S(1)} %copy-done, s32[]{:T(128)S(6)} %select_n.6), kind=kOutput, calls=%fused_computation.2 | convolution fusion | flops 536870912 | bytes 3145732 | tf_op jit(solution)/shard_map/dot_general | solution.py:128
  14.5 0.0 collective-permute-done.swapped
  14.5 0.7 shard_map.55
  15.3 1.9 %collective-permute-start.1 = (bf16[128,512]{1,0:T(8,128)(2,1)}, bf16[128,512]{1,0:T(8,128)(2,1)S(1)}, u32[]{:S(2)}, u32[]{:S(2)}) collective-permute-start(bf16[128,512]{1,0:T(8,128)(2,1)} %get-tuple-element.22), channel_id=1, source_target_pairs={{0,64},{16,80},{32,96},{48,112},{64,128},{80,144},{96,160},{112,17... | collective-permute-start | bytes 393224 | tf_op jit(solution)/shard_map/ppermute | solution.py:151
  17.2 1.9 %collective-permute-start.2 = (bf16[128,512]{1,0:T(8,128)(2,1)S(1)}, bf16[128,512]{1,0:T(8,128)(2,1)S(1)}, u32[]{:S(2)}, u32[]{:S(2)}) collective-permute-start(bf16[128,512]{1,0:T(8,128)(2,1)S(1)} %get-tuple-element.23), channel_id=1, source_target_pairs={{0,48},{16,32},{32,80},{48,64},{64,112},{80,96},{96,144},{112,128}... | collective-permute-start | bytes 393224 | tf_op jit(solution)/shard_map/ppermute | solution.py:151
  19.1 5.6 %collective-permute-start.3 = (bf16[128,512]{1,0:T(8,128)(2,1)S(1)}, bf16[128,512]{1,0:T(8,128)(2,1)S(1)}, u32[]{:S(2)}, u32[]{:S(2)}) collective-permute-start(bf16[128,512]{1,0:T(8,128)(2,1)S(1)} %get-tuple-element.24), channel_id=1, source_target_pairs={{0,496},{16,480},{32,16},{48,0},{64,48},{80,32},{96,80},{112,64},{... | collective-permute-start | bytes 393224 | tf_op jit(solution)/shard_map/ppermute | solution.py:151
  24.8 1.6 %shard_map.56 = (bf16[32,16,512]{2,1,0:T(8,128)(2,1)}, bf16[16,128,512]{2,1,0:T(8,128)(2,1)S(1)}) custom-call(s32[32]{0:T(128)S(1)} %copy-done.4, bf16[4,16,512]{2,1,0:T(8,128)(2,1)S(1)} %copy-done.3, bf16[4,512,512]{2,1,0:T(8,128)(2,1)S(1)} %copy-done.1), custom_call_target="tpu_custom_call" | custom-call | tf_op jit(solution)/shard_map/pallas_call | solution.py:28
  26.4 1.3 %copy-done.2 = bf16[16,128,512]{2,1,0:T(8,128)(2,1)} copy-done((bf16[16,128,512]{2,1,0:T(8,128)(2,1)}, bf16[16,128,512]{2,1,0:T(8,128)(2,1)S(1)}, u32[]{:S(2)}) %copy-start.2) | copy-done | bytes 2097176
  27.7 7.6 %all-to-all-start = ((bf16[32,16,512]{2,1,0:T(8,128)(2,1)}), bf16[32,16,512]{2,1,0:T(8,128)(2,1)S(1)}, u32[]{:S(2)}, u32[]{:S(2)}) async-start(bf16[32,16,512]{2,1,0:T(8,128)(2,1)} %get-tuple-element.31), calls=%async_computation | async-start | bytes 1048576 | tf_op jit(solution)/shard_map/all_to_all | solution.py:154
  35.3 0.0 collective-permute-done.1.a
  35.3 0.0 collective-permute-done.2.b
  35.3 0.0 collective-permute-done.3.c
  35.4 0.1 shard_map.57
  35.4 10.2 %collective-permute-start.4 = (bf16[32,512]{1,0:T(8,128)(2,1)S(1)}, bf16[32,512]{1,0:T(8,128)(2,1)S(1)}, u32[]{:S(2)}, u32[]{:S(2)}) collective-permute-start(bf16[32,512]{1,0:T(8,128)(2,1)S(1)} %get-tuple-element.28), channel_id=1, source_target_pairs={{0,256},{16,272},{32,288},{48,304},{64,320},{80,336},{96,352},{112... | collective-permute-start | bytes 98312 | tf_op jit(solution)/shard_map/ppermute | solution.py:151
  45.7 4.0 %collective-permute-start.5 = (bf16[32,512]{1,0:T(8,128)(2,1)S(1)}, bf16[32,512]{1,0:T(8,128)(2,1)S(1)}, u32[]{:S(2)}, u32[]{:S(2)}) collective-permute-start(bf16[32,512]{1,0:T(8,128)(2,1)S(1)} %get-tuple-element.29), channel_id=1, source_target_pairs={{0,128},{16,144},{32,160},{48,176},{64,192},{80,208},{96,224},{112... | collective-permute-start | bytes 98312 | tf_op jit(solution)/shard_map/ppermute | solution.py:151
  49.7 5.2 %collective-permute-start.6 = (bf16[32,512]{1,0:T(8,128)(2,1)S(1)}, bf16[32,512]{1,0:T(8,128)(2,1)S(1)}, u32[]{:S(2)}, u32[]{:S(2)}) collective-permute-start(bf16[32,512]{1,0:T(8,128)(2,1)S(1)} %get-tuple-element.30), channel_id=1, source_target_pairs={{0,384},{16,400},{32,416},{48,432},{64,448},{80,464},{96,480},{112... | collective-permute-start | bytes 98312 | tf_op jit(solution)/shard_map/ppermute | solution.py:151
  54.9 0.0 all-to-all-done
  54.9 6.8 %all-to-all-start.1 = ((bf16[16,128,512]{2,1,0:T(8,128)(2,1)}), bf16[16,128,512]{2,1,0:T(8,128)(2,1)}, u32[]{:S(2)}, u32[]{:S(2)}) async-start(bf16[16,128,512]{2,1,0:T(8,128)(2,1)} %copy-done.2), calls=%async_computation.1 | async-start | bytes 4194304 | tf_op jit(solution)/shard_map/all_to_all | solution.py:162
  61.7 0.0 collective-permute-done.4.a
  61.7 0.0 collective-permute-done.5.b
  61.7 0.0 collective-permute-done.6.c
  61.7 0.6 shard_map.58
  62.3 31.5 %all_gather.3.gathered = bf16[512,896]{1,0:T(8,128)(2,1)S(1)} all-gather(bf16[32,896]{1,0:T(8,128)(2,1)S(1)} %shard_map.58), channel_id=1, replica_groups={{0,48,64,112,128,176,192,240,256,304,320,368,384,432,448,496},{16,32,80..., dimensions={0}, use_global_device_ids=true | all-gather | bytes 974848 | tf_op jit(solution)/shard_map/all_gather | solution.py:169
  93.8 2.8 %shard_map.59 = f32[8,24,128]{2,1,0:T(8,128)S(1)} custom-call(s32[32]{0:T(128)S(1)} %copy-done.4, bf16[512,896]{1,0:T(8,128)(2,1)S(1)} %all_gather.3.gathered, bf16[16,128,512]{2,1,0:T(8,128)(2,1)} %all-to-all-done.1.rights), custom_call_target="tpu_custom_call" | custom-call | tf_op jit(solution)/shard_map/pallas_call | solution.py:28
  96.6 7.7 %all_to_all.15.got = f32[8,24,128]{2,1,0:T(8,128)S(1)} all-to-all(f32[8,24,128]{2,1,0:T(8,128)S(1)} %shard_map.59), channel_id=1, replica_groups=mesh['zh'=4,'zl'=4,'core'=2,'owner'=16] {'zl','core'}, dimensions={0} | all-to-all | bytes 196608 | tf_op jit(solution)/shard_map/all_to_all | solution.py:176
  104.3 0.7 shard_map.60
  (6 shorter events, 0.0 us)
Async XLA Ops:
  0.0 1.6 %copy-start = (bf16[1024,1024]{1,0:T(8,128)(2,1)S(1)}, bf16[1024,1024]{1,0:T(8,128)(2,1)}, u32[]{:S(2)}) copy-start(bf16[1024,1024]{1,0:T(8,128)(2,1)} %param.6) | copy-start | bytes 6291460
  3.6 11.0 %collective-permute-start = (bf16[512,512]{1,0:T(8,128)(2,1)S(1)}, bf16[512,512]{1,0:T(8,128)(2,1)S(1)}, u32[]{:S(2)}, u32[]{:S(2)}) collective-permute-start(bf16[512,512]{1,0:T(8,128)(2,1)S(1)} %convolution_convert_fusion), channel_id=1, source_target_pairs={{0,16},{16,0},{1,17},{17,1},{2,18},{18,2},{3,19},{19,3},{4,20},{20... | collective-permute-start | bytes 1572872 | tf_op jit(solution)/shard_map/ppermute | solution.py:131
  12.4 12.4 %copy-start.1 = (bf16[4,512,512]{2,1,0:T(8,128)(2,1)S(1)}, bf16[4,512,512]{2,1,0:T(8,128)(2,1)}, u32[]{:S(2)}) copy-start(bf16[4,512,512]{2,1,0:T(8,128)(2,1)} %right.1) | copy-start | bytes 6291460
  12.4 12.4 %copy-start.3 = (bf16[4,16,512]{2,1,0:T(8,128)(2,1)S(1)}, bf16[4,16,512]{2,1,0:T(8,128)(2,1)}, u32[]{:S(2)}) copy-start(bf16[4,16,512]{2,1,0:T(8,128)(2,1)} %left.1) | copy-start | bytes 196612
  12.4 12.4 %copy-start.4 = (s32[32]{0:T(128)S(1)}, s32[32]{0:T(128)}, u32[]{:S(2)}) copy-start(s32[32]{0:T(128)} %owners.5) | copy-start | bytes 388
  15.3 20.1 %collective-permute-start.1 = (bf16[128,512]{1,0:T(8,128)(2,1)}, bf16[128,512]{1,0:T(8,128)(2,1)S(1)}, u32[]{:S(2)}, u32[]{:S(2)}) collective-permute-start(bf16[128,512]{1,0:T(8,128)(2,1)} %get-tuple-element.22), channel_id=1, source_target_pairs={{0,64},{16,80},{32,96},{48,112},{64,128},{80,144},{96,160},{112,17... | collective-permute-start | bytes 393224 | tf_op jit(solution)/shard_map/ppermute | solution.py:151
  17.2 18.2 %collective-permute-start.2 = (bf16[128,512]{1,0:T(8,128)(2,1)S(1)}, bf16[128,512]{1,0:T(8,128)(2,1)S(1)}, u32[]{:S(2)}, u32[]{:S(2)}) collective-permute-start(bf16[128,512]{1,0:T(8,128)(2,1)S(1)} %get-tuple-element.23), channel_id=1, source_target_pairs={{0,48},{16,32},{32,80},{48,64},{64,112},{80,96},{96,144},{112,128}... | collective-permute-start | bytes 393224 | tf_op jit(solution)/shard_map/ppermute | solution.py:151
  19.1 16.2 %collective-permute-start.3 = (bf16[128,512]{1,0:T(8,128)(2,1)S(1)}, bf16[128,512]{1,0:T(8,128)(2,1)S(1)}, u32[]{:S(2)}, u32[]{:S(2)}) collective-permute-start(bf16[128,512]{1,0:T(8,128)(2,1)S(1)} %get-tuple-element.24), channel_id=1, source_target_pairs={{0,496},{16,480},{32,16},{48,0},{64,48},{80,32},{96,80},{112,64},{... | collective-permute-start | bytes 393224 | tf_op jit(solution)/shard_map/ppermute | solution.py:151
  26.4 1.3 %copy-start.2 = (bf16[16,128,512]{2,1,0:T(8,128)(2,1)}, bf16[16,128,512]{2,1,0:T(8,128)(2,1)S(1)}, u32[]{:S(2)}) copy-start(bf16[16,128,512]{2,1,0:T(8,128)(2,1)S(1)} %get-tuple-element.32) | copy-start | bytes 6291460
  27.7 27.2 %all-to-all-start = ((bf16[32,16,512]{2,1,0:T(8,128)(2,1)}), bf16[32,16,512]{2,1,0:T(8,128)(2,1)S(1)}, u32[]{:S(2)}, u32[]{:S(2)}) async-start(bf16[32,16,512]{2,1,0:T(8,128)(2,1)} %get-tuple-element.31), calls=%async_computation | async-start | bytes 1048576 | tf_op jit(solution)/shard_map/all_to_all | solution.py:154
  35.4 26.2 %collective-permute-start.4 = (bf16[32,512]{1,0:T(8,128)(2,1)S(1)}, bf16[32,512]{1,0:T(8,128)(2,1)S(1)}, u32[]{:S(2)}, u32[]{:S(2)}) collective-permute-start(bf16[32,512]{1,0:T(8,128)(2,1)S(1)} %get-tuple-element.28), channel_id=1, source_target_pairs={{0,256},{16,272},{32,288},{48,304},{64,320},{80,336},{96,352},{112... | collective-permute-start | bytes 98312 | tf_op jit(solution)/shard_map/ppermute | solution.py:151
  45.7 16.0 %collective-permute-start.5 = (bf16[32,512]{1,0:T(8,128)(2,1)S(1)}, bf16[32,512]{1,0:T(8,128)(2,1)S(1)}, u32[]{:S(2)}, u32[]{:S(2)}) collective-permute-start(bf16[32,512]{1,0:T(8,128)(2,1)S(1)} %get-tuple-element.29), channel_id=1, source_target_pairs={{0,128},{16,144},{32,160},{48,176},{64,192},{80,208},{96,224},{112... | collective-permute-start | bytes 98312 | tf_op jit(solution)/shard_map/ppermute | solution.py:151
  49.7 12.0 %collective-permute-start.6 = (bf16[32,512]{1,0:T(8,128)(2,1)S(1)}, bf16[32,512]{1,0:T(8,128)(2,1)S(1)}, u32[]{:S(2)}, u32[]{:S(2)}) collective-permute-start(bf16[32,512]{1,0:T(8,128)(2,1)S(1)} %get-tuple-element.30), channel_id=1, source_target_pairs={{0,384},{16,400},{32,416},{48,432},{64,448},{80,464},{96,480},{112... | collective-permute-start | bytes 98312 | tf_op jit(solution)/shard_map/ppermute | solution.py:151
  54.9 38.9 %all-to-all-start.1 = ((bf16[16,128,512]{2,1,0:T(8,128)(2,1)}), bf16[16,128,512]{2,1,0:T(8,128)(2,1)}, u32[]{:S(2)}, u32[]{:S(2)}) async-start(bf16[16,128,512]{2,1,0:T(8,128)(2,1)} %copy-done.2), calls=%async_computation.1 | async-start | bytes 4194304 | tf_op jit(solution)/shard_map/all_to_all | solution.py:162

commit v3 on v2

--- a/solution.py
+++ b/solution.py
@@ -64,30 +64,63 @@
             left_out[16 * core + i] = left[slots[2 * i + (core ^ flip)]]
 
 
-def split_kernel(mine, swapped, across, up, down, own):
-    for ref, offset in ((across, 2), (up, 1), (down, 3), (own, 0)):
-        for h in range(4):
-            rows = pl.ds(pl.multiple_of(128 * h + 32 * lax.rem(axis("zl") + offset, 4), 32), 32)
+def theirs_kernel(acts, cots, out, some_acts, some_cots, sems):
+    lanes = pl.ds(pl.multiple_of((1 - column()) * 512, 512), 512)
+    copies = []
+    for i in range(4):
+        rows = pl.ds(256 * i, 256)
+        copies.append(pltpu.make_async_copy(cots.at[rows, lanes], some_cots.at[rows], sems.at[0, i]))
+        copies.append(pltpu.make_async_copy(acts.at[rows], some_acts.at[rows], sems.at[1, i]))
+    for copy in copies:
+        copy.start()
+    acc = jnp.zeros((512, 512), F32)
+    for i in range(4):
+        copies[2 * i].wait()
+        copies[2 * i + 1].wait()
+        rows = pl.ds(256 * i, 256)
+        acc += lax.dot_general(some_cots[rows, :], some_acts[rows, :], ROWS_FIRST, preferred_element_type=F32)
+    out[...] = acc.astype(BF16)
+
+
+def holder(owners):
+    lane = lax.broadcasted_iota(jnp.int32, (1, 32), 1)
+    return jnp.sum(jnp.where(lane == block_id(), owners[...], 0))
+
+
+def odd_even_kernel(mine, swapped, send, keep):
+    here = axis("zl") & 1
+    for h in range(8):
+        for ref, side in ((send, 1 - here), (keep, here)):
+            rows = pl.ds(pl.multiple_of(64 * h + 32 * side, 32), 32)
             ref[32 * h : 32 * (h + 1)] = (mine[rows, :] + swapped[rows, :].astype(F32)).astype(ref.dtype)
 
 
-def near_kernel(own, a, b, c, across, up, down, keep, acc):
-    acc[...] = own[...] + a[...].astype(F32) + b[...].astype(F32) + c[...].astype(F32)
+def quarter_kernel(kept, got, send, keep):
+    here = axis("zl") >> 1
+    for h in range(4):
+        for ref, side in ((send, 1 - here), (keep, here)):
+            rows = pl.ds(pl.multiple_of(64 * h + 32 * side, 32), 32)
+            ref[32 * h : 32 * (h + 1)] = (kept[rows, :] + got[rows, :].astype(F32)).astype(ref.dtype)
+
+
+def near_kernel(own, got, across, up, down, keep, acc):
+    acc[...] = own[...] + got[...].astype(F32)
     for ref, offset in ((across, 2), (up, 1), (down, 3), (keep, 0)):
         rows = pl.ds(pl.multiple_of(lax.rem(axis("zh") + offset, 4) * 32, 32), 32)
         ref[...] = acc[rows, :].astype(ref.dtype)
 
 
 def far_kernel(owners, own, a, b, c, left, out):
+    held = holder(owners)
     out[:, :512] = (own[...] + a[...].astype(F32) + b[...].astype(F32) + c[...].astype(F32)).astype(BF16)
     for j in range(3):
         lanes = pl.ds(pl.multiple_of(lax.rem(axis("zh") + j, 4) * 128, 128), 128)
         for half in range(2):
-            out[16 * half : 16 * (half + 1), 512 + 128 * j : 640 + 128 * j] = left[half, 0, :, lanes]
+            out[16 * half : 16 * (half + 1), 512 + 128 * j : 640 + 128 * j] = left[half, held, :, lanes]
 
 
 def middle_kernel(owners, gathered, rights, out, right, sem):
-    fetch = pltpu.make_async_copy(rights.at[owners[block_id()]], right, sem)
+    fetch = pltpu.make_async_copy(rights.at[holder(owners)], right, sem)
     fetch.start()
     grad = gathered[:, :512]
     wide = grad.astype(F32)
@@ -123,14 +156,33 @@
 
 
 def shards(activations, key_cotangent, block_owner, left_root, right_root):
-    def product(half):
-        columns = lax.dynamic_slice_in_dim(key_cotangent, half * 512, 512, 1)
-        return lax.dot_general(columns, activations, ROWS_FIRST, preferred_element_type=F32)
-
-    theirs = product(1 - column()).astype(BF16)
+    hbm = pl.BlockSpec(memory_space=pltpu.HBM)
+    theirs = pl.pallas_call(
+        theirs_kernel, in_specs=[hbm] * 2, out_specs=pl.BlockSpec(memory_space=pltpu.VMEM),
+        out_shape=shape_of((512, 512), BF16),
+        scratch_shapes=[pltpu.VMEM((1024, 512), BF16)] * 2 + [pltpu.SemaphoreType.DMA((2, 4))],
+        compiler_params=pltpu.CompilerParams(vmem_limit_bytes=60 * 1024 * 1024),
+    )(activations, key_cotangent)
     swapped = lax.ppermute(theirs, "core", [(0, 1), (1, 0)])
-    mine = product(column())
-
+    columns = lax.dynamic_slice_in_dim(key_cotangent, column() * 512, 512, 1)
+    mine = lax.dot_general(columns, activations, ROWS_FIRST, preferred_element_type=F32)
+
+    def shift(x, step, turned=False):
+        moves = []
+        for z in range(16):
+            for block in range(2):
+                to = (z + (-step if turned and block else step)) % 16
+                moves.append((2 * z + (block ^ (z & 1)), 2 * to + (block ^ (to & 1))))
+        return lax.ppermute(x, ("zh", "zl", "core"), moves)
+
+    send, own = call(
+        odd_even_kernel, (mine, swapped), (1,), [whole(512, 512)] * 2,
+        [whole(256, 512)] * 2, [shape_of((256, 512), BF16), shape_of((256, 512), F32)],
+    )
+    got = shift(send, 1, True)
+
+    owner_row = block_owner.reshape(1, 32)
+    own, block_owner = lax.optimization_barrier((own, block_owner))
     left_sends, right_sends = call(
         send_kernel, (block_owner, left_root, right_root), (1,),
         [whole(4, 16, 512), pl.BlockSpec((4, 128, 512), lambda i, owners: (0, axis("zl"), 0))],
@@ -139,39 +191,34 @@
         [pltpu.SMEM((32,), jnp.int32)], prefetch=1,
     )
 
-    piece = shape_of((128, 512), BF16)
-    across, up, down, own = call(
-        split_kernel, (mine, swapped), (1,), [whole(512, 512)] * 2,
-        [whole(128, 512)] * 4, [piece] * 3 + [shape_of((128, 512), F32)],
+    own, left_sends, right_sends = lax.optimization_barrier((own, left_sends, right_sends))
+    send, own = call(
+        quarter_kernel, (own, got), (1,), [whole(256, 512)] * 2,
+        [whole(128, 512)] * 2, [shape_of((128, 512), BF16), shape_of((128, 512), F32)],
     )
     own, left_sends = lax.optimization_barrier((own, left_sends))
-
-    def shift(x, by):
-        moves = [(i, (i + 2 * by) % 32 ^ (by & 1)) for i in range(32)]
-        return lax.ppermute(x, ("zh", "zl", "core"), moves)
-
-    a, b, c = shift(across, 2), shift(up, 1), shift(down, -1)
     lefts = lax.all_to_all(left_sends, ("core", "owner"), 0, 0, tiled=True).reshape(2, 16, 16, 512)
+    got = shift(send, 2, True)
     band = shape_of((32, 512), BF16)
     across, up, down, own = call(
-        near_kernel, (own, a, b, c), (1,), [whole(128, 512)] * 4, [whole(32, 512)] * 4,
+        near_kernel, (own, got), (1,), [whole(128, 512)] * 2, [whole(32, 512)] * 4,
         [band] * 3 + [shape_of((32, 512), F32)], [pltpu.VMEM((128, 512), F32)], cost=WAIT,
     )
     own, right_sends = lax.optimization_barrier((own, right_sends))
     a, b, c = shift(across, 8), shift(up, 4), shift(down, -4)
     rights = lax.all_to_all(right_sends, "owner", 0, 0, tiled=True)
     part = call(
-        far_kernel, (block_owner, own, a, b, c, lefts), (1,),
-        [whole(32, 512)] * 4 + [pl.BlockSpec((2, 1, 16, 512), lambda i, owners: (0, owners[block_id()], 0, 0))],
-        whole(32, 896), shape_of((32, 896), BF16), prefetch=1, cost=WAIT,
+        far_kernel, (owner_row, own, a, b, c, lefts), (1,),
+        [whole(1, 32)] + [whole(32, 512)] * 4 + [whole(2, 16, 16, 512)],
+        whole(32, 896), shape_of((32, 896), BF16), cost=WAIT,
     )
     groups = [[2 * z + (z & 1 ^ c) for z in range(16)] for c in range(2)]
     gathered = lax.all_gather(part, ("zh", "zl", "core"), axis=0, tiled=True, axis_index_groups=groups)
 
     results = call(
-        middle_kernel, (block_owner, gathered, rights), (1,),
-        [whole(512, 896), ANY], whole(8, 24, 128), shape_of((8, 24, 128), F32),
-        [pltpu.VMEM((128, 512), BF16), pltpu.SemaphoreType.DMA], prefetch=1,
+        middle_kernel, (owner_row, gathered, rights), (1,),
+        [whole(1, 32), whole(512, 896), ANY], whole(8, 24, 128), shape_of((8, 24, 128), F32),
+        [pltpu.VMEM((128, 512), BF16), pltpu.SemaphoreType.DMA],
     )
     got = lax.all_to_all(results, ("zl", "core"), 0, 0, tiled=True)
     return call(place_kernel, (got,), (1,), [whole(8, 24, 128)], whole(16, 1024), shape_of((16, 1024), F32))

time: 106 us -> 102 us (0.962)
  starting transfers between devices: 52 us -> 49.6 us
  matrix products: 4.08 us -> 2.11 us
  local copies, waits for them, and re-layouts: 2.95 us -> 1.36 us
  Pallas kernels: 6.4 us -> 7.66 us
    pallas_call x0 -> x1, Pallas kernels: none -> 3.1 us  [shards(): pl.pallas_call(theirs_kernel, in_specs=[hbm] * 2, out_specs=pl.BlockSpec(...]
    ppermute x6 -> x5, starting transfers between devices: 28.9 us -> 26.9 us  [shift(): return lax.ppermute(x, ('zh', 'zl', 'core'), moves)]
    dot_general x2 -> x1, matrix products: 4.08 us -> 2.11 us  [shards(): lax.dot_general(columns, activations, ROWS_FIRST, preferred_element_type=...]
    pallas_call x6 -> x7, Pallas kernels: 6.4 us -> 4.56 us  [call(): pl.pallas_call(kernel, grid_spec=pltpu.PrefetchScalarGridSpec(num_scalar_...]
    unnamed x10, local copies, waits for them, and re-layouts: 2.95 us -> 1.36 us
  transfers between devices with their start and end apart: 9 -> 8, of which waited for: 0 -> 1; matrix products, arithmetic and copies ran while one was open for 2% -> 2% of each run, Pallas kernels for 2% -> 2%
where the time goes in v3:
time: 102 us; the launch traced here: 101 us
  starting transfers between devices  49.6 us (49%)
  blocking collectives  40.1 us (39%)
  Pallas kernels  7.66 us (8%)
  matrix products  2.11 us (2%)
  local copies, waits for them, and re-layouts  1.36 us (1%)
    all_gather x1, blocking collectives, shards(): lax.all_gather(part, ('zh', 'zl', 'core'), axis=0, tiled=True, axis_index...  32.4 us
    ppermute x5, starting transfers between devices, shift(): return lax.ppermute(x, ('zh', 'zl', 'core'), moves)  26.9 us
    ppermute x1, starting transfers between devices, shards(): swapped = lax.ppermute(theirs, 'core', [(0, 1), (1, 0)])  8.79 us
    all_to_all x1, blocking collectives, shards(): got = lax.all_to_all(results, ('zl', 'core'), 0, 0, tiled=True)  7.72 us
    all_to_all x1, starting transfers between devices, shards(): lax.all_to_all(left_sends, ('core', 'owner'), 0, 0, tiled=True)  7.22 us
    all_to_all x1, starting transfers between devices, shards(): rights = lax.all_to_all(right_sends, 'owner', 0, 0, tiled=True)  6.7 us
    pallas_call x7, Pallas kernels, call(): pl.pallas_call(kernel, grid_spec=pltpu.PrefetchScalarGridSpec(num_scalar_...  4.56 us
    pallas_call x1, Pallas kernels, shards(): pl.pallas_call(theirs_kernel, in_specs=[hbm] * 2, out_specs=pl.BlockSpec(...  3.1 us
  transfers between devices with their start and end apart: 8, of which 1 were waited for; matrix products, arithmetic and copies ran while one was open for 2% of the time, Pallas kernels for 2%

profile of v3, /device:TPU:1, one launch (start us, length us, event | category | flops | bytes accessed | tf_op | source)
XLA Modules:
  0.0 101.5 jit_solution(12813370132279327877)
XLA Ops:
  0.0 3.1 %shard_map.55 = bf16[512,512]{1,0:T(8,128)(2,1)} custom-call(bf16[1024,512]{1,0:T(8,128)(2,1)} %acts.1, bf16[1024,1024]{1,0:T(8,128)(2,1)} %cots.1), custom_call_target="tpu_custom_call" | custom-call | tf_op jit(solution)/shard_map/pallas_call | solution.py:160
  3.1 8.8 %collective-permute-start = (bf16[512,512]{1,0:T(8,128)(2,1)}, bf16[512,512]{1,0:T(8,128)(2,1)S(1)}, u32[]{:S(2)}, u32[]{:S(2)}) collective-permute-start(bf16[512,512]{1,0:T(8,128)(2,1)} %shard_map.55), channel_id=1, source_target_pairs={{0,16},{16,0},{1,17},{17,1},{2,18},{18,2},{3,19},{19,3},{4,20},{20... | collective-permute-start | bytes 1572872 | tf_op jit(solution)/shard_map/ppermute | solution.py:166
  11.9 0.0 copy-done.4
  11.9 0.0 copy-start
  11.9 0.0 copy-start.2
  12.0 0.0 copy-start.3
  12.0 2.1 %fusion.mine = f32[512,512]{1,0:T(8,128)S(1)} fusion(bf16[1024,512]{1,0:T(8,128)(2,1)} %acts.1, bf16[1024,1024]{1,0:T(8,128)(2,1)S(1)} %copy-done.4, s32[]{:T(128)S(6)} %select_n.3), kind=kOutput, calls=%fused_computation | convolution fusion | flops 536870912 | bytes 3145732 | tf_op jit(solution)/shard_map/dot_general | solution.py:168
  14.1 0.0 collective-permute-done.swapped
  14.1 0.1 shard_map.56
  14.2 5.6 %collective-permute-start.1 = (bf16[256,512]{1,0:T(8,128)(2,1)S(1)}, bf16[256,512]{1,0:T(8,128)(2,1)S(1)}, u32[]{:S(2)}, u32[]{:S(2)}) collective-permute-start(bf16[256,512]{1,0:T(8,128)(2,1)S(1)} %get-tuple-element.30), channel_id=1, source_target_pairs={{0,48},{16,480},{48,64},{32,16},{64,112},{80,32},{112,128},{96,80}... | collective-permute-start | bytes 786440 | tf_op jit(solution)/shard_map/ppermute | solution.py:176
  19.8 0.0 copy-done
  19.9 0.0 copy-done.2
  19.9 1.6 %shard_map.57 = (bf16[32,16,512]{2,1,0:T(8,128)(2,1)}, bf16[16,128,512]{2,1,0:T(8,128)(2,1)S(1)}) custom-call(s32[32]{0:T(128)S(1)} %copy-done.3, bf16[4,16,512]{2,1,0:T(8,128)(2,1)S(1)} %copy-done.2, bf16[4,512,512]{2,1,0:T(8,128)(2,1)S(1)} %copy-done), custom_call_target="tpu_custom_call" | custom-call | tf_op jit(solution)/shard_map/pallas_call | solution.py:28
  21.5 1.3 %copy-done.1 = bf16[16,128,512]{2,1,0:T(8,128)(2,1)} copy-done((bf16[16,128,512]{2,1,0:T(8,128)(2,1)}, bf16[16,128,512]{2,1,0:T(8,128)(2,1)S(1)}, u32[]{:S(2)}) %copy-start.1) | copy-done | bytes 2097176
  22.8 0.3 collective-permute-done.1.got
  23.2 4.9 %collective-permute-start.2 = (bf16[128,512]{1,0:T(8,128)(2,1)S(1)}, bf16[128,512]{1,0:T(8,128)(2,1)S(1)}, u32[]{:S(2)}, u32[]{:S(2)}) collective-permute-start(bf16[128,512]{1,0:T(8,128)(2,1)S(1)} %get-tuple-element.34), channel_id=1, source_target_pairs={{0,64},{16,464},{48,112},{32,480},{64,128},{80,16},{112,176},{96,3... | collective-permute-start | bytes 393224 | tf_op jit(solution)/shard_map/ppermute | solution.py:176
  28.1 7.2 %all-to-all-start = ((bf16[32,16,512]{2,1,0:T(8,128)(2,1)}), bf16[32,16,512]{2,1,0:T(8,128)(2,1)S(1)}, u32[]{:S(2)}, u32[]{:S(2)}) async-start(bf16[32,16,512]{2,1,0:T(8,128)(2,1)} %get-tuple-element.41), calls=%async_computation | async-start | bytes 1048576 | tf_op jit(solution)/shard_map/all_to_all | solution.py:200
  35.4 0.0 collective-permute-done.2.got
  35.4 7.2 %collective-permute-start.3 = (bf16[32,512]{1,0:T(8,128)(2,1)S(1)}, bf16[32,512]{1,0:T(8,128)(2,1)S(1)}, u32[]{:S(2)}, u32[]{:S(2)}) collective-permute-start(bf16[32,512]{1,0:T(8,128)(2,1)S(1)} %get-tuple-element.38), channel_id=1, source_target_pairs={{0,256},{16,272},{48,304},{32,288},{64,320},{80,336},{112,368},{96... | collective-permute-start | bytes 98312 | tf_op jit(solution)/shard_map/ppermute | solution.py:176
  42.6 5.0 %collective-permute-start.4 = (bf16[32,512]{1,0:T(8,128)(2,1)S(1)}, bf16[32,512]{1,0:T(8,128)(2,1)S(1)}, u32[]{:S(2)}, u32[]{:S(2)}) collective-permute-start(bf16[32,512]{1,0:T(8,128)(2,1)S(1)} %get-tuple-element.39), channel_id=1, source_target_pairs={{0,128},{16,144},{48,176},{32,160},{64,192},{80,208},{112,240},{96... | collective-permute-start | bytes 98312 | tf_op jit(solution)/shard_map/ppermute | solution.py:176
  47.6 4.2 %collective-permute-start.5 = (bf16[32,512]{1,0:T(8,128)(2,1)S(1)}, bf16[32,512]{1,0:T(8,128)(2,1)S(1)}, u32[]{:S(2)}, u32[]{:S(2)}) collective-permute-start(bf16[32,512]{1,0:T(8,128)(2,1)S(1)} %get-tuple-element.40), channel_id=1, source_target_pairs={{0,384},{16,400},{48,432},{32,416},{64,448},{80,464},{112,496},{96... | collective-permute-start | bytes 98312 | tf_op jit(solution)/shard_map/ppermute | solution.py:176
  51.8 0.0 all-to-all-done
  51.8 6.7 %all-to-all-start.1 = ((bf16[16,128,512]{2,1,0:T(8,128)(2,1)}), bf16[16,128,512]{2,1,0:T(8,128)(2,1)S(1)}, u32[]{:S(2)}, u32[]{:S(2)}) async-start(bf16[16,128,512]{2,1,0:T(8,128)(2,1)} %copy-done.1), calls=%async_computation.1 | async-start | bytes 4194304 | tf_op jit(solution)/shard_map/all_to_all | solution.py:209
  58.5 0.0 collective-permute-done.3.a
  58.5 0.0 collective-permute-done.4.b
  58.5 0.0 collective-permute-done.5.c
  58.5 0.1 shard_map.60
  58.7 32.4 %all_gather.3.gathered = bf16[512,896]{1,0:T(8,128)(2,1)S(1)} all-gather(bf16[32,896]{1,0:T(8,128)(2,1)S(1)} %shard_map.60), channel_id=1, replica_groups={{0,48,64,112,128,176,192,240,256,304,320,368,384,432,448,496},{16,32,80..., dimensions={0}, use_global_device_ids=true | all-gather | bytes 974848 | tf_op jit(solution)/shard_map/all_gather | solution.py:216
  91.1 0.0 all-to-all-done.1.rights
  91.1 2.0 %shard_map.61 = f32[8,24,128]{2,1,0:T(8,128)S(1)} custom-call(s32[1,32]{1,0:T(1,128)S(1)} %bitcast.5, bf16[512,896]{1,0:T(8,128)(2,1)S(1)} %all_gather.3.gathered, bf16[16,128,512]{2,1,0:T(8,128)(2,1)S(1)} %all-to-all-done.1.rights), custom_call_target="tpu_custom_call" | custom-call | tf_op jit(solution)/shard_map/pallas_call | solution.py:28
  93.1 7.7 %all_to_all.15.got = f32[8,24,128]{2,1,0:T(8,128)S(1)} all-to-all(f32[8,24,128]{2,1,0:T(8,128)S(1)} %shard_map.61), channel_id=1, replica_groups=mesh['zh'=4,'zl'=4,'core'=2,'owner'=16] {'zl','core'}, dimensions={0} | all-to-all | bytes 196608 | tf_op jit(solution)/shard_map/all_to_all | solution.py:223
  100.8 0.7 shard_map.62
  (5 shorter events, 0.1 us)
Async XLA Ops:
  0.0 11.9 %copy-start.4 = (bf16[1024,1024]{1,0:T(8,128)(2,1)S(1)}, bf16[1024,1024]{1,0:T(8,128)(2,1)}, u32[]{:S(2)}) copy-start(bf16[1024,1024]{1,0:T(8,128)(2,1)} %cots.1) | copy-start | bytes 6291460
  3.1 11.0 %collective-permute-start = (bf16[512,512]{1,0:T(8,128)(2,1)}, bf16[512,512]{1,0:T(8,128)(2,1)S(1)}, u32[]{:S(2)}, u32[]{:S(2)}) collective-permute-start(bf16[512,512]{1,0:T(8,128)(2,1)} %shard_map.55), channel_id=1, source_target_pairs={{0,16},{16,0},{1,17},{17,1},{2,18},{18,2},{3,19},{19,3},{4,20},{20... | collective-permute-start | bytes 1572872 | tf_op jit(solution)/shard_map/ppermute | solution.py:166
  11.9 7.9 %copy-start = (bf16[4,512,512]{2,1,0:T(8,128)(2,1)S(1)}, bf16[4,512,512]{2,1,0:T(8,128)(2,1)}, u32[]{:S(2)}) copy-start(bf16[4,512,512]{2,1,0:T(8,128)(2,1)} %right.1) | copy-start | bytes 6291460
  11.9 7.9 %copy-start.2 = (bf16[4,16,512]{2,1,0:T(8,128)(2,1)S(1)}, bf16[4,16,512]{2,1,0:T(8,128)(2,1)}, u32[]{:S(2)}) copy-start(bf16[4,16,512]{2,1,0:T(8,128)(2,1)} %left.1) | copy-start | bytes 196612
  12.0 7.9 %copy-start.3 = (s32[32]{0:T(128)S(1)}, s32[32]{0:T(128)}, u32[]{:S(2)}) copy-start(s32[32]{0:T(128)} %owners) | copy-start | bytes 388
  14.2 8.9 %collective-permute-start.1 = (bf16[256,512]{1,0:T(8,128)(2,1)S(1)}, bf16[256,512]{1,0:T(8,128)(2,1)S(1)}, u32[]{:S(2)}, u32[]{:S(2)}) collective-permute-start(bf16[256,512]{1,0:T(8,128)(2,1)S(1)} %get-tuple-element.30), channel_id=1, source_target_pairs={{0,48},{16,480},{48,64},{32,16},{64,112},{80,32},{112,128},{96,80}... | collective-permute-start | bytes 786440 | tf_op jit(solution)/shard_map/ppermute | solution.py:176
  21.5 1.3 %copy-start.1 = (bf16[16,128,512]{2,1,0:T(8,128)(2,1)}, bf16[16,128,512]{2,1,0:T(8,128)(2,1)S(1)}, u32[]{:S(2)}) copy-start(bf16[16,128,512]{2,1,0:T(8,128)(2,1)S(1)} %get-tuple-element.42) | copy-start | bytes 6291460
  23.2 12.2 %collective-permute-start.2 = (bf16[128,512]{1,0:T(8,128)(2,1)S(1)}, bf16[128,512]{1,0:T(8,128)(2,1)S(1)}, u32[]{:S(2)}, u32[]{:S(2)}) collective-permute-start(bf16[128,512]{1,0:T(8,128)(2,1)S(1)} %get-tuple-element.34), channel_id=1, source_target_pairs={{0,64},{16,464},{48,112},{32,480},{64,128},{80,16},{112,176},{96,3... | collective-permute-start | bytes 393224 | tf_op jit(solution)/shard_map/ppermute | solution.py:176
  28.1 23.7 %all-to-all-start = ((bf16[32,16,512]{2,1,0:T(8,128)(2,1)}), bf16[32,16,512]{2,1,0:T(8,128)(2,1)S(1)}, u32[]{:S(2)}, u32[]{:S(2)}) async-start(bf16[32,16,512]{2,1,0:T(8,128)(2,1)} %get-tuple-element.41), calls=%async_computation | async-start | bytes 1048576 | tf_op jit(solution)/shard_map/all_to_all | solution.py:200
  35.4 23.1 %collective-permute-start.3 = (bf16[32,512]{1,0:T(8,128)(2,1)S(1)}, bf16[32,512]{1,0:T(8,128)(2,1)S(1)}, u32[]{:S(2)}, u32[]{:S(2)}) collective-permute-start(bf16[32,512]{1,0:T(8,128)(2,1)S(1)} %get-tuple-element.38), channel_id=1, source_target_pairs={{0,256},{16,272},{48,304},{32,288},{64,320},{80,336},{112,368},{96... | collective-permute-start | bytes 98312 | tf_op jit(solution)/shard_map/ppermute | solution.py:176
  42.6 15.9 %collective-permute-start.4 = (bf16[32,512]{1,0:T(8,128)(2,1)S(1)}, bf16[32,512]{1,0:T(8,128)(2,1)S(1)}, u32[]{:S(2)}, u32[]{:S(2)}) collective-permute-start(bf16[32,512]{1,0:T(8,128)(2,1)S(1)} %get-tuple-element.39), channel_id=1, source_target_pairs={{0,128},{16,144},{48,176},{32,160},{64,192},{80,208},{112,240},{96... | collective-permute-start | bytes 98312 | tf_op jit(solution)/shard_map/ppermute | solution.py:176
  47.6 10.9 %collective-permute-start.5 = (bf16[32,512]{1,0:T(8,128)(2,1)S(1)}, bf16[32,512]{1,0:T(8,128)(2,1)S(1)}, u32[]{:S(2)}, u32[]{:S(2)}) collective-permute-start(bf16[32,512]{1,0:T(8,128)(2,1)S(1)} %get-tuple-element.40), channel_id=1, source_target_pairs={{0,384},{16,400},{48,432},{32,416},{64,448},{80,464},{112,496},{96... | collective-permute-start | bytes 98312 | tf_op jit(solution)/shard_map/ppermute | solution.py:176
  51.8 39.3 %all-to-all-start.1 = ((bf16[16,128,512]{2,1,0:T(8,128)(2,1)}), bf16[16,128,512]{2,1,0:T(8,128)(2,1)S(1)}, u32[]{:S(2)}, u32[]{:S(2)}) async-start(bf16[16,128,512]{2,1,0:T(8,128)(2,1)} %copy-done.1), calls=%async_computation.1 | async-start | bytes 4194304 | tf_op jit(solution)/shard_map/all_to_all | solution.py:209

commit v4 on v3

--- a/solution.py
+++ b/solution.py
@@ -55,13 +55,17 @@
         held += hit.astype(jnp.int32)
 
 
-def send_kernel(owners, left, right, left_out, right_out, slots):
+def send_left_kernel(owners, left, out, slots):
     slots_to_send(owners, slots)
     flip = axis("zl") & 1
+    for i in range(32):
+        out[i] = left[slots[2 * (i % 16) + (i // 16 ^ flip)]]
+
+
+def send_right_kernel(owners, right, out, slots):
+    slots_to_send(owners, slots)
     for i in range(16):
-        right_out[i] = right[slots[2 * i + column()]]
-        for core in range(2):
-            left_out[16 * core + i] = left[slots[2 * i + (core ^ flip)]]
+        out[i] = right[slots[2 * i + column()]]
 
 
 def theirs_kernel(acts, cots, out, some_acts, some_cots, sems):
@@ -87,20 +91,19 @@
     return jnp.sum(jnp.where(lane == block_id(), owners[...], 0))
 
 
-def odd_even_kernel(mine, swapped, send, keep):
-    here = axis("zl") & 1
-    for h in range(8):
-        for ref, side in ((send, 1 - here), (keep, here)):
-            rows = pl.ds(pl.multiple_of(64 * h + 32 * side, 32), 32)
-            ref[32 * h : 32 * (h + 1)] = (mine[rows, :] + swapped[rows, :].astype(F32)).astype(ref.dtype)
+def half_kernel(mine, swapped, send, keep):
+    for j in range(4):
+        ref = send if j > 1 else keep
+        first = 32 * lax.rem(axis("zl") + j * (1 + 2 * column()), 4)
+        for h in range(4):
+            rows = pl.ds(pl.multiple_of(128 * h + first, 32), 32)
+            here = slice(128 * (j % 2) + 32 * h, 128 * (j % 2) + 32 * (h + 1))
+            ref[here] = (mine[rows, :] + swapped[rows, :].astype(F32)).astype(ref.dtype)
 
 
 def quarter_kernel(kept, got, send, keep):
-    here = axis("zl") >> 1
-    for h in range(4):
-        for ref, side in ((send, 1 - here), (keep, here)):
-            rows = pl.ds(pl.multiple_of(64 * h + 32 * side, 32), 32)
-            ref[32 * h : 32 * (h + 1)] = (kept[rows, :] + got[rows, :].astype(F32)).astype(ref.dtype)
+    keep[...] = kept[:128] + got[:128].astype(F32)
+    send[...] = (kept[128:] + got[128:].astype(F32)).astype(BF16)
 
 
 def near_kernel(own, got, across, up, down, keep, acc):
@@ -124,35 +127,45 @@
     fetch.start()
     grad = gathered[:, :512]
     wide = grad.astype(F32)
-    grad_sq = jnp.sum(wide * wide)
+    grad_sq = jnp.sum(jnp.sum(wide * wide, axis=0, keepdims=True), axis=1, keepdims=True)
     fetch.wait()
     mixed = jnp.dot(right[...], grad, preferred_element_type=F32).astype(BF16)
-    pieces = [mixed[:, 128 * b : 128 * (b + 1)] for b in range(4)]
+    mixed = mixed.T
+    pieces = [mixed[128 * b : 128 * (b + 1)] for b in range(4)]
     total = jnp.zeros((128, 128), F32)
     for a in range(4):
-        left = gathered[128 * a : 128 * (a + 1), 640:768]
-        acc = lax.dot_general(pieces[(a + 1) % 4], left, (((1,), (1,)), ((), ())), preferred_element_type=F32)
-        for j in range(3):
-            b = (a - j) % 4
-            left = gathered[128 * b : 128 * (b + 1), 512 + 128 * j : 640 + 128 * j]
-            acc += jnp.dot(pieces[b], left, preferred_element_type=F32)
+        left = gathered[128 * a : 128 * (a + 1), 512:896]
+        turn = gathered[128 * ((a + 3) % 4) : 128 * ((a + 3) % 4 + 1), 640:768]
+        three = jnp.concatenate([pieces[(a + j) % 4] for j in range(3)], axis=0)
+        acc = jnp.dot(left, three, preferred_element_type=F32)
+        acc += lax.dot_general(turn, pieces[(a + 3) % 4], ROWS_FIRST, preferred_element_type=F32)
         total += acc * acc
 
         @pl.when(axis("zh") == a)
         def _():
-            out[:, :16, :] = acc.T.reshape(8, 16, 128)
-
-    out[:, 16:20, :] = jnp.full((8, 4, 128), jnp.sum(total), F32)
-    out[:, 20:24, :] = jnp.full((8, 4, 128), grad_sq, F32)
+            out[:, :16, :] = acc.astype(BF16).reshape(8, 16, 128)
+
+    pre_sq = jnp.sum(jnp.sum(total, axis=0, keepdims=True), axis=1, keepdims=True)
+    row = lax.broadcasted_iota(jnp.int32, (16, 128), 0)
+    rest = jnp.where(row < 8, pre_sq, grad_sq)
+    terms = jnp.zeros((16, 128), F32)
+    for i in range(3):
+        term = rest.astype(BF16).astype(F32)
+        terms = jnp.where(row % 8 == i, term, terms)
+        rest -= term
+    out[:, 16:, :] = jnp.broadcast_to(terms.astype(BF16)[None], (8, 16, 128))
 
 
 def place_kernel(got, out):
+    def total(part, first):
+        return sum(got[part, first + i : first + i + 1, :].astype(F32) for i in (2, 1, 0))
+
     for block in range(2):
         parts = [2 * l + (block ^ (l & 1)) for l in range(4)]
-        pre_sq = sum(got[i, 16:17, :] for i in parts)
-        scale = jnp.sqrt(got[parts[0], 20:21, :] / (pre_sq + 1e-06))
+        pre_sq = sum(total(i, 16) for i in parts)
+        scale = jnp.sqrt(total(parts[0], 24) / (pre_sq + 1e-06))
         for l, i in enumerate(parts):
-            out[:, 512 * block + 128 * l : 512 * block + 128 * (l + 1)] = got[i, :16, :] * scale
+            out[:, 512 * block + 128 * l : 512 * block + 128 * (l + 1)] = got[i, :16, :].astype(F32) * scale
 
 
 def shards(activations, key_cotangent, block_owner, left_root, right_root):
@@ -176,33 +189,35 @@
         return lax.ppermute(x, ("zh", "zl", "core"), moves)
 
     send, own = call(
-        odd_even_kernel, (mine, swapped), (1,), [whole(512, 512)] * 2,
+        half_kernel, (mine, swapped), (1,), [whole(512, 512)] * 2,
         [whole(256, 512)] * 2, [shape_of((256, 512), BF16), shape_of((256, 512), F32)],
     )
-    got = shift(send, 1, True)
+    got = shift(send, 2, True)
 
     owner_row = block_owner.reshape(1, 32)
     own, block_owner = lax.optimization_barrier((own, block_owner))
-    left_sends, right_sends = call(
-        send_kernel, (block_owner, left_root, right_root), (1,),
-        [whole(4, 16, 512), pl.BlockSpec((4, 128, 512), lambda i, owners: (0, axis("zl"), 0))],
-        [whole(32, 16, 512), whole(16, 128, 512)],
-        [shape_of((32, 16, 512), BF16), shape_of((16, 128, 512), BF16)],
-        [pltpu.SMEM((32,), jnp.int32)], prefetch=1,
-    )
-
-    own, left_sends, right_sends = lax.optimization_barrier((own, left_sends, right_sends))
+    left_sends = call(
+        send_left_kernel, (block_owner, left_root), (1,), [whole(4, 16, 512)], whole(32, 16, 512),
+        shape_of((32, 16, 512), BF16), [pltpu.SMEM((32,), jnp.int32)], prefetch=1,
+    )
+    lefts = lax.all_to_all(left_sends, ("core", "owner"), 0, 0, tiled=True).reshape(2, 16, 16, 512)
+    own, left_sends = lax.optimization_barrier((own, left_sends))
     send, own = call(
         quarter_kernel, (own, got), (1,), [whole(256, 512)] * 2,
-        [whole(128, 512)] * 2, [shape_of((128, 512), BF16), shape_of((128, 512), F32)],
-    )
-    own, left_sends = lax.optimization_barrier((own, left_sends))
-    lefts = lax.all_to_all(left_sends, ("core", "owner"), 0, 0, tiled=True).reshape(2, 16, 16, 512)
-    got = shift(send, 2, True)
+        [whole(128, 512)] * 2, [shape_of((128, 512), BF16), shape_of((128, 512), F32)], cost=WAIT,
+    )
+    got = shift(send, 1, True)
+    own, block_owner = lax.optimization_barrier((own, block_owner))
+    right_sends = call(
+        send_right_kernel, (block_owner, right_root), (1,),
+        [pl.BlockSpec((4, 128, 512), lambda i, owners: (0, axis("zl"), 0))],
+        whole(16, 128, 512), shape_of((16, 128, 512), BF16), [pltpu.SMEM((32,), jnp.int32)], prefetch=1,
+    )
+    own, right_sends = lax.optimization_barrier((own, right_sends))
     band = shape_of((32, 512), BF16)
     across, up, down, own = call(
         near_kernel, (own, got), (1,), [whole(128, 512)] * 2, [whole(32, 512)] * 4,
-        [band] * 3 + [shape_of((32, 512), F32)], [pltpu.VMEM((128, 512), F32)], cost=WAIT,
+        [band] * 3 + [shape_of((32, 512), F32)], [pltpu.VMEM((128, 512), F32)],
     )
     own, right_sends = lax.optimization_barrier((own, right_sends))
     a, b, c = shift(across, 8), shift(up, 4), shift(down, -4)
@@ -217,11 +232,11 @@
 
     results = call(
         middle_kernel, (owner_row, gathered, rights), (1,),
-        [whole(1, 32), whole(512, 896), ANY], whole(8, 24, 128), shape_of((8, 24, 128), F32),
+        [whole(1, 32), whole(512, 896), ANY], whole(8, 32, 128), shape_of((8, 32, 128), BF16),
         [pltpu.VMEM((128, 512), BF16), pltpu.SemaphoreType.DMA],
     )
     got = lax.all_to_all(results, ("zl", "core"), 0, 0, tiled=True)
-    return call(place_kernel, (got,), (1,), [whole(8, 24, 128)], whole(16, 1024), shape_of((16, 1024), F32))
+    return call(place_kernel, (got,), (1,), [whole(8, 32, 128)], whole(16, 1024), shape_of((16, 1024), F32))
 
 
 def solution(mesh):

time: 102 us -> 101 us (level)
  Pallas kernels: 7.66 us -> 9.26 us
  local copies, waits for them, and re-layouts: 1.36 us -> 0.02 us
  starting transfers between devices: 49.6 us -> 48.3 us
  waiting for transfers between devices: 0.35 us -> 1.56 us
    pallas_call x7 -> x8, Pallas kernels: 4.56 us -> 6.17 us  [call(): pl.pallas_call(kernel, grid_spec=pltpu.PrefetchScalarGridSpec(num_scalar_...]
    unnamed x10 -> x8, local copies, waits for them, and re-layouts: 1.36 us -> 0.02 us
    ppermute x5, starting transfers between devices: 26.9 us -> 25.6 us  [shift(): return lax.ppermute(x, ('zh', 'zl', 'core'), moves)]
    ppermute x5, waiting for transfers between devices: 0.34 us -> 1.55 us  [shift(): return lax.ppermute(x, ('zh', 'zl', 'core'), moves)]
  transfers between devices with their start and end apart: 8 -> 8, of which waited for: 1 -> 1; matrix products, arithmetic and copies ran while one was open for 2% -> 2% of each run, Pallas kernels for 2% -> 4%
where the time goes in v4:
time: 101 us
  starting transfers between devices  48.3 us (48%)
  blocking collectives  39.2 us (39%)
  Pallas kernels  9.26 us (9%)
  matrix products  2 us (2%)
  waiting for transfers between devices  1.56 us (2%)
    all_gather x1, blocking collectives, shards(): lax.all_gather(part, ('zh', 'zl', 'core'), axis=0, tiled=True, axis_index...  32.2 us
    ppermute x5, starting transfers between devices, shift(): return lax.ppermute(x, ('zh', 'zl', 'core'), moves)  25.6 us
    ppermute x1, starting transfers between devices, shards(): swapped = lax.ppermute(theirs, 'core', [(0, 1), (1, 0)])  8.79 us
    all_to_all x1, starting transfers between devices, shards(): lax.all_to_all(left_sends, ('core', 'owner'), 0, 0, tiled=True)  7.2 us
    all_to_all x1, blocking collectives, shards(): got = lax.all_to_all(results, ('zl', 'core'), 0, 0, tiled=True)  6.96 us
    all_to_all x1, starting transfers between devices, shards(): rights = lax.all_to_all(right_sends, 'owner', 0, 0, tiled=True)  6.7 us
    pallas_call x8, Pallas kernels, call(): pl.pallas_call(kernel, grid_spec=pltpu.PrefetchScalarGridSpec(num_scalar_...  6.17 us
    pallas_call x1, Pallas kernels, shards(): pl.pallas_call(theirs_kernel, in_specs=[hbm] * 2, out_specs=pl.BlockSpec(...  3.09 us
  transfers between devices with their start and end apart: 8, of which 1 were waited for; matrix products, arithmetic and copies ran while one was open for 2% of the time, Pallas kernels for 4%

profile of v4, /device:TPU:1, one launch (start us, length us, event | category | flops | bytes accessed | tf_op | source)
XLA Modules:
  0.0 100.6 jit_solution(17158968290090017972)
XLA Ops:
  0.0 3.1 %shard_map.55 = bf16[512,512]{1,0:T(8,128)(2,1)} custom-call(bf16[1024,512]{1,0:T(8,128)(2,1)} %acts.1, bf16[1024,1024]{1,0:T(8,128)(2,1)} %cots.1), custom_call_target="tpu_custom_call" | custom-call | tf_op jit(solution)/shard_map/pallas_call | solution.py:173
  3.1 8.8 %collective-permute-start = (bf16[512,512]{1,0:T(8,128)(2,1)}, bf16[512,512]{1,0:T(8,128)(2,1)S(1)}, u32[]{:S(2)}, u32[]{:S(2)}) collective-permute-start(bf16[512,512]{1,0:T(8,128)(2,1)} %shard_map.55), channel_id=1, source_target_pairs={{0,16},{16,0},{1,17},{17,1},{2,18},{18,2},{3,19},{19,3},{4,20},{20... | collective-permute-start | bytes 1572872 | tf_op jit(solution)/shard_map/ppermute | solution.py:179
  11.9 0.0 copy-done.3
  11.9 0.0 copy-start.1
  11.9 0.0 copy-start.2
  11.9 2.0 %fusion.mine = f32[512,512]{1,0:T(8,128)S(1)} fusion(bf16[1024,512]{1,0:T(8,128)(2,1)} %acts.1, bf16[1024,1024]{1,0:T(8,128)(2,1)S(1)} %copy-done.3, s32[]{:T(128)S(6)} %select_n.3), kind=kOutput, calls=%fused_computation | convolution fusion | flops 536870912 | bytes 3145732 | tf_op jit(solution)/shard_map/dot_general | solution.py:181
  13.9 0.0 collective-permute-done.swapped
  14.0 0.1 shard_map.56
  14.1 6.2 %collective-permute-start.1 = (bf16[256,512]{1,0:T(8,128)(2,1)S(1)}, bf16[256,512]{1,0:T(8,128)(2,1)S(1)}, u32[]{:S(2)}, u32[]{:S(2)}) collective-permute-start(bf16[256,512]{1,0:T(8,128)(2,1)S(1)} %get-tuple-element.26), channel_id=1, source_target_pairs={{0,64},{16,464},{48,112},{32,480},{64,128},{80,16},{112,176},{96,3... | collective-permute-start | bytes 786440 | tf_op jit(solution)/shard_map/ppermute | solution.py:189
  20.3 0.0 copy-done.1
  20.3 1.5 %shard_map.57 = bf16[32,16,512]{2,1,0:T(8,128)(2,1)} custom-call(s32[32]{0:T(128)S(1)} %copy-done.2, bf16[4,16,512]{2,1,0:T(8,128)(2,1)S(1)} %copy-done.1), custom_call_target="tpu_custom_call" | custom-call | tf_op jit(solution)/shard_map/pallas_call | solution.py:28
  21.8 7.2 %all-to-all-start = ((bf16[32,16,512]{2,1,0:T(8,128)(2,1)}), bf16[32,16,512]{2,1,0:T(8,128)(2,1)S(1)}, u32[]{:S(2)}, u32[]{:S(2)}) async-start(bf16[32,16,512]{2,1,0:T(8,128)(2,1)} %shard_map.57), calls=%async_computation | async-start | bytes 1048576 | tf_op jit(solution)/shard_map/all_to_all | solution.py:203
  29.0 0.0 copy-start
  29.0 0.0 collective-permute-done.1.got
  29.0 3.1 %collective-permute-start.2 = (bf16[128,512]{1,0:T(8,128)(2,1)S(1)}, bf16[128,512]{1,0:T(8,128)(2,1)S(1)}, u32[]{:S(2)}, u32[]{:S(2)}) collective-permute-start(bf16[128,512]{1,0:T(8,128)(2,1)S(1)} %get-tuple-element.31), channel_id=1, source_target_pairs={{0,48},{16,480},{48,64},{32,16},{64,112},{80,32},{112,128},{96,80}... | collective-permute-start | bytes 393224 | tf_op jit(solution)/shard_map/ppermute | solution.py:189
  32.1 0.0 copy-done
  32.1 2.1 %shard_map.59 = bf16[16,128,512]{2,1,0:T(8,128)(2,1)} custom-call(s32[32]{0:T(128)S(1)} %copy-done.2, bf16[4,512,512]{2,1,0:T(8,128)(2,1)S(1)} %copy-done), custom_call_target="tpu_custom_call" | custom-call | tf_op jit(solution)/shard_map/pallas_call | solution.py:28
  34.2 1.5 %collective-permute-done.2.got = bf16[128,512]{1,0:T(8,128)(2,1)S(1)} collective-permute-done((bf16[128,512]{1,0:T(8,128)(2,1)S(1)}, bf16[128,512]{1,0:T(8,128)(2,1)S(1)}, u32[]{:S(2)}, u32[]{:S(2)}) %collective-permute-start.2) | collective-permute-done | bytes 131104 | tf_op jit(solution)/shard_map/ppermute | solution.py:189
  35.8 7.2 %collective-permute-start.3 = (bf16[32,512]{1,0:T(8,128)(2,1)S(1)}, bf16[32,512]{1,0:T(8,128)(2,1)S(1)}, u32[]{:S(2)}, u32[]{:S(2)}) collective-permute-start(bf16[32,512]{1,0:T(8,128)(2,1)S(1)} %get-tuple-element.35), channel_id=1, source_target_pairs={{0,256},{16,272},{48,304},{32,288},{64,320},{80,336},{112,368},{96... | collective-permute-start | bytes 98312 | tf_op jit(solution)/shard_map/ppermute | solution.py:189
  43.0 5.0 %collective-permute-start.4 = (bf16[32,512]{1,0:T(8,128)(2,1)S(1)}, bf16[32,512]{1,0:T(8,128)(2,1)S(1)}, u32[]{:S(2)}, u32[]{:S(2)}) collective-permute-start(bf16[32,512]{1,0:T(8,128)(2,1)S(1)} %get-tuple-element.36), channel_id=1, source_target_pairs={{0,128},{16,144},{48,176},{32,160},{64,192},{80,208},{112,240},{96... | collective-permute-start | bytes 98312 | tf_op jit(solution)/shard_map/ppermute | solution.py:189
  48.0 4.2 %collective-permute-start.5 = (bf16[32,512]{1,0:T(8,128)(2,1)S(1)}, bf16[32,512]{1,0:T(8,128)(2,1)S(1)}, u32[]{:S(2)}, u32[]{:S(2)}) collective-permute-start(bf16[32,512]{1,0:T(8,128)(2,1)S(1)} %get-tuple-element.37), channel_id=1, source_target_pairs={{0,384},{16,400},{48,432},{32,416},{64,448},{80,464},{112,496},{96... | collective-permute-start | bytes 98312 | tf_op jit(solution)/shard_map/ppermute | solution.py:189
  52.2 0.0 all-to-all-done
  52.2 6.7 %all-to-all-start.1 = ((bf16[16,128,512]{2,1,0:T(8,128)(2,1)}), bf16[16,128,512]{2,1,0:T(8,128)(2,1)S(1)}, u32[]{:S(2)}, u32[]{:S(2)}) async-start(bf16[16,128,512]{2,1,0:T(8,128)(2,1)} %shard_map.59), calls=%async_computation.1 | async-start | bytes 4194304 | tf_op jit(solution)/shard_map/all_to_all | solution.py:224
  58.9 0.0 collective-permute-done.3.a
  58.9 0.0 collective-permute-done.4.b
  58.9 0.0 collective-permute-done.5.c
  58.9 0.1 shard_map.61
  59.1 32.2 %all_gather.3.gathered = bf16[512,896]{1,0:T(8,128)(2,1)S(1)} all-gather(bf16[32,896]{1,0:T(8,128)(2,1)S(1)} %shard_map.61), channel_id=1, replica_groups={{0,48,64,112,128,176,192,240,256,304,320,368,384,432,448,496},{16,32,80..., dimensions={0}, use_global_device_ids=true | all-gather | bytes 974848 | tf_op jit(solution)/shard_map/all_gather | solution.py:231
  91.3 0.0 all-to-all-done.1.rights
  91.3 1.6 %shard_map.62 = bf16[8,32,128]{2,1,0:T(8,128)(2,1)S(1)} custom-call(s32[1,32]{1,0:T(1,128)S(1)} %bitcast.5, bf16[512,896]{1,0:T(8,128)(2,1)S(1)} %all_gather.3.gathered, bf16[16,128,512]{2,1,0:T(8,128)(2,1)S(1)} %all-to-all-done.1.rights), custom_call_target="tpu_custom_call" | custom-call | tf_op jit(solution)/shard_map/pallas_call | solution.py:28
  92.9 7.0 %all_to_all.15.got = bf16[8,32,128]{2,1,0:T(8,128)(2,1)S(1)} all-to-all(bf16[8,32,128]{2,1,0:T(8,128)(2,1)S(1)} %shard_map.62), channel_id=1, replica_groups=mesh['zh'=4,'zl'=4,'core'=2,'owner'=16] {'zl','core'}, dimensions={0} | all-to-all | bytes 131072 | tf_op jit(solution)/shard_map/all_to_all | solution.py:238
  99.9 0.7 shard_map.63
  (4 shorter events, 0.1 us)
Async XLA Ops:
  0.0 11.9 %copy-start.3 = (bf16[1024,1024]{1,0:T(8,128)(2,1)S(1)}, bf16[1024,1024]{1,0:T(8,128)(2,1)}, u32[]{:S(2)}) copy-start(bf16[1024,1024]{1,0:T(8,128)(2,1)} %cots.1) | copy-start | bytes 6291460
  3.1 10.8 %collective-permute-start = (bf16[512,512]{1,0:T(8,128)(2,1)}, bf16[512,512]{1,0:T(8,128)(2,1)S(1)}, u32[]{:S(2)}, u32[]{:S(2)}) collective-permute-start(bf16[512,512]{1,0:T(8,128)(2,1)} %shard_map.55), channel_id=1, source_target_pairs={{0,16},{16,0},{1,17},{17,1},{2,18},{18,2},{3,19},{19,3},{4,20},{20... | collective-permute-start | bytes 1572872 | tf_op jit(solution)/shard_map/ppermute | solution.py:179
  11.9 8.3 %copy-start.1 = (bf16[4,16,512]{2,1,0:T(8,128)(2,1)S(1)}, bf16[4,16,512]{2,1,0:T(8,128)(2,1)}, u32[]{:S(2)}) copy-start(bf16[4,16,512]{2,1,0:T(8,128)(2,1)} %left.1) | copy-start | bytes 196612
  11.9 8.3 %copy-start.2 = (s32[32]{0:T(128)S(1)}, s32[32]{0:T(128)}, u32[]{:S(2)}) copy-start(s32[32]{0:T(128)} %owners.1) | copy-start | bytes 388
  14.1 14.9 %collective-permute-start.1 = (bf16[256,512]{1,0:T(8,128)(2,1)S(1)}, bf16[256,512]{1,0:T(8,128)(2,1)S(1)}, u32[]{:S(2)}, u32[]{:S(2)}) collective-permute-start(bf16[256,512]{1,0:T(8,128)(2,1)S(1)} %get-tuple-element.26), channel_id=1, source_target_pairs={{0,64},{16,464},{48,112},{32,480},{64,128},{80,16},{112,176},{96,3... | collective-permute-start | bytes 786440 | tf_op jit(solution)/shard_map/ppermute | solution.py:189
  21.8 30.4 %all-to-all-start = ((bf16[32,16,512]{2,1,0:T(8,128)(2,1)}), bf16[32,16,512]{2,1,0:T(8,128)(2,1)S(1)}, u32[]{:S(2)}, u32[]{:S(2)}) async-start(bf16[32,16,512]{2,1,0:T(8,128)(2,1)} %shard_map.57), calls=%async_computation | async-start | bytes 1048576 | tf_op jit(solution)/shard_map/all_to_all | solution.py:203
  29.0 3.2 %copy-start = (bf16[4,512,512]{2,1,0:T(8,128)(2,1)S(1)}, bf16[4,512,512]{2,1,0:T(8,128)(2,1)}, u32[]{:S(2)}) copy-start(bf16[4,512,512]{2,1,0:T(8,128)(2,1)} %right.1) | copy-start | bytes 6291460
  29.0 6.7 %collective-permute-start.2 = (bf16[128,512]{1,0:T(8,128)(2,1)S(1)}, bf16[128,512]{1,0:T(8,128)(2,1)S(1)}, u32[]{:S(2)}, u32[]{:S(2)}) collective-permute-start(bf16[128,512]{1,0:T(8,128)(2,1)S(1)} %get-tuple-element.31), channel_id=1, source_target_pairs={{0,48},{16,480},{48,64},{32,16},{64,112},{80,32},{112,128},{96,80}... | collective-permute-start | bytes 393224 | tf_op jit(solution)/shard_map/ppermute | solution.py:189
  35.8 23.1 %collective-permute-start.3 = (bf16[32,512]{1,0:T(8,128)(2,1)S(1)}, bf16[32,512]{1,0:T(8,128)(2,1)S(1)}, u32[]{:S(2)}, u32[]{:S(2)}) collective-permute-start(bf16[32,512]{1,0:T(8,128)(2,1)S(1)} %get-tuple-element.35), channel_id=1, source_target_pairs={{0,256},{16,272},{48,304},{32,288},{64,320},{80,336},{112,368},{96... | collective-permute-start | bytes 98312 | tf_op jit(solution)/shard_map/ppermute | solution.py:189
  43.0 15.9 %collective-permute-start.4 = (bf16[32,512]{1,0:T(8,128)(2,1)S(1)}, bf16[32,512]{1,0:T(8,128)(2,1)S(1)}, u32[]{:S(2)}, u32[]{:S(2)}) collective-permute-start(bf16[32,512]{1,0:T(8,128)(2,1)S(1)} %get-tuple-element.36), channel_id=1, source_target_pairs={{0,128},{16,144},{48,176},{32,160},{64,192},{80,208},{112,240},{96... | collective-permute-start | bytes 98312 | tf_op jit(solution)/shard_map/ppermute | solution.py:189
  48.0 10.9 %collective-permute-start.5 = (bf16[32,512]{1,0:T(8,128)(2,1)S(1)}, bf16[32,512]{1,0:T(8,128)(2,1)S(1)}, u32[]{:S(2)}, u32[]{:S(2)}) collective-permute-start(bf16[32,512]{1,0:T(8,128)(2,1)S(1)} %get-tuple-element.37), channel_id=1, source_target_pairs={{0,384},{16,400},{48,432},{32,416},{64,448},{80,464},{112,496},{96... | collective-permute-start | bytes 98312 | tf_op jit(solution)/shard_map/ppermute | solution.py:189
  52.2 39.1 %all-to-all-start.1 = ((bf16[16,128,512]{2,1,0:T(8,128)(2,1)}), bf16[16,128,512]{2,1,0:T(8,128)(2,1)S(1)}, u32[]{:S(2)}, u32[]{:S(2)}) async-start(bf16[16,128,512]{2,1,0:T(8,128)(2,1)} %shard_map.59), calls=%async_computation.1 | async-start | bytes 4194304 | tf_op jit(solution)/shard_map/all_to_all | solution.py:224

commit v5 on v4

--- a/solution.py
+++ b/solution.py
@@ -55,17 +55,15 @@
         held += hit.astype(jnp.int32)
 
 
-def send_left_kernel(owners, left, out, slots):
+def send_kernel(owners, left, right, left_out, right_out, slots):
     slots_to_send(owners, slots)
     flip = axis("zl") & 1
-    for i in range(32):
-        out[i] = left[slots[2 * (i % 16) + (i // 16 ^ flip)]]
-
-
-def send_right_kernel(owners, right, out, slots):
-    slots_to_send(owners, slots)
     for i in range(16):
-        out[i] = right[slots[2 * i + column()]]
+        right_out[i] = right[slots[2 * i + column()]]
+        for core in range(2):
+            for j in range(3):
+                lanes = pl.ds(pl.multiple_of(lax.rem(axis("zh") + j, 4) * 128, 128), 128)
+                left_out[16 * core + i, :, 128 * j : 128 * (j + 1)] = left[slots[2 * i + (core ^ flip)], :, lanes]
 
 
 def theirs_kernel(acts, cots, out, some_acts, some_cots, sems):
@@ -91,35 +89,33 @@
     return jnp.sum(jnp.where(lane == block_id(), owners[...], 0))
 
 
-def half_kernel(mine, swapped, send, keep):
-    for j in range(4):
-        ref = send if j > 1 else keep
-        first = 32 * lax.rem(axis("zl") + j * (1 + 2 * column()), 4)
+def split_kernel(mine, swapped, across, up, down, own):
+    for ref, offset in ((across, 2), (up, 1 + 2 * column()), (down, 3 - 2 * column()), (own, 0)):
+        first = 32 * lax.rem(axis("zl") + offset, 4)
         for h in range(4):
             rows = pl.ds(pl.multiple_of(128 * h + first, 32), 32)
-            here = slice(128 * (j % 2) + 32 * h, 128 * (j % 2) + 32 * (h + 1))
-            ref[here] = (mine[rows, :] + swapped[rows, :].astype(F32)).astype(ref.dtype)
-
-
-def quarter_kernel(kept, got, send, keep):
-    keep[...] = kept[:128] + got[:128].astype(F32)
-    send[...] = (kept[128:] + got[128:].astype(F32)).astype(BF16)
-
-
-def near_kernel(own, got, across, up, down, keep, acc):
-    acc[...] = own[...] + got[...].astype(F32)
-    for ref, offset in ((across, 2), (up, 1), (down, 3), (keep, 0)):
-        rows = pl.ds(pl.multiple_of(lax.rem(axis("zh") + offset, 4) * 32, 32), 32)
-        ref[...] = acc[rows, :].astype(ref.dtype)
-
-
-def far_kernel(owners, own, a, b, c, left, out):
+            ref[32 * h : 32 * (h + 1)] = (mine[rows, :] + swapped[rows, :].astype(F32)).astype(ref.dtype)
+
+
+def near_kernel(own, a, b, c, send, keep, acc):
+    acc[...] = own[...] + a[...].astype(F32) + b[...].astype(F32) + c[...].astype(F32)
+    other = axis("zh") + 1 + 2 * column()
+    for ref, first in ((send, other), (keep, axis("zh"))):
+        for j in range(2):
+            rows = pl.ds(pl.multiple_of(lax.rem(first + 2 * j, 4) * 32, 32), 32)
+            ref[32 * j : 32 * (j + 1)] = acc[rows, :].astype(ref.dtype)
+
+
+def pair_kernel(kept, got, send, keep):
+    keep[...] = kept[:32] + got[:32].astype(F32)
+    send[...] = (kept[32:] + got[32:].astype(F32)).astype(BF16)
+
+
+def far_kernel(owners, own, got, left, out):
     held = holder(owners)
-    out[:, :512] = (own[...] + a[...].astype(F32) + b[...].astype(F32) + c[...].astype(F32)).astype(BF16)
-    for j in range(3):
-        lanes = pl.ds(pl.multiple_of(lax.rem(axis("zh") + j, 4) * 128, 128), 128)
-        for half in range(2):
-            out[16 * half : 16 * (half + 1), 512 + 128 * j : 640 + 128 * j] = left[half, held, :, lanes]
+    out[:, :512] = (own[...] + got[...].astype(F32)).astype(BF16)
+    for half in range(2):
+        out[16 * half : 16 * (half + 1), 512:] = left[half, held]
 
 
 def middle_kernel(owners, gathered, rights, out, right, sem):
@@ -180,51 +176,48 @@
     columns = lax.dynamic_slice_in_dim(key_cotangent, column() * 512, 512, 1)
     mine = lax.dot_general(columns, activations, ROWS_FIRST, preferred_element_type=F32)
 
-    def shift(x, step, turned=False):
+    def shift(x, step):
         moves = []
         for z in range(16):
             for block in range(2):
-                to = (z + (-step if turned and block else step)) % 16
+                to = (z + (-step if block else step)) % 16
                 moves.append((2 * z + (block ^ (z & 1)), 2 * to + (block ^ (to & 1))))
         return lax.ppermute(x, ("zh", "zl", "core"), moves)
 
-    send, own = call(
-        half_kernel, (mine, swapped), (1,), [whole(512, 512)] * 2,
-        [whole(256, 512)] * 2, [shape_of((256, 512), BF16), shape_of((256, 512), F32)],
-    )
-    got = shift(send, 2, True)
+    quarter = shape_of((128, 512), BF16)
+    across, up, down, own = call(
+        split_kernel, (mine, swapped), (1,), [whole(512, 512)] * 2,
+        [whole(128, 512)] * 4, [quarter] * 3 + [shape_of((128, 512), F32)],
+    )
+    a, b, c = shift(across, 2), shift(up, 1), shift(down, -1)
 
     owner_row = block_owner.reshape(1, 32)
     own, block_owner = lax.optimization_barrier((own, block_owner))
-    left_sends = call(
-        send_left_kernel, (block_owner, left_root), (1,), [whole(4, 16, 512)], whole(32, 16, 512),
-        shape_of((32, 16, 512), BF16), [pltpu.SMEM((32,), jnp.int32)], prefetch=1,
-    )
-    lefts = lax.all_to_all(left_sends, ("core", "owner"), 0, 0, tiled=True).reshape(2, 16, 16, 512)
+    left_sends, right_sends = call(
+        send_kernel, (block_owner, left_root, right_root), (1,),
+        [whole(4, 16, 512), pl.BlockSpec((4, 128, 512), lambda i, owners: (0, axis("zl"), 0))],
+        [whole(32, 16, 384), whole(16, 128, 512)],
+        [shape_of((32, 16, 384), BF16), shape_of((16, 128, 512), BF16)],
+        [pltpu.SMEM((32,), jnp.int32)], prefetch=1,
+    )
+    own, left_sends, right_sends = lax.optimization_barrier((own, left_sends, right_sends))
+    send, own = call(
+        near_kernel, (own, a, b, c), (1,), [whole(128, 512)] * 4, [whole(64, 512)] * 2,
+        [shape_of((64, 512), BF16), shape_of((64, 512), F32)], [pltpu.VMEM((128, 512), F32)], cost=WAIT,
+    )
     own, left_sends = lax.optimization_barrier((own, left_sends))
+    lefts = lax.all_to_all(left_sends, ("core", "owner"), 0, 0, tiled=True).reshape(2, 16, 16, 384)
+    got = shift(send, 4)
     send, own = call(
-        quarter_kernel, (own, got), (1,), [whole(256, 512)] * 2,
-        [whole(128, 512)] * 2, [shape_of((128, 512), BF16), shape_of((128, 512), F32)], cost=WAIT,
-    )
-    got = shift(send, 1, True)
-    own, block_owner = lax.optimization_barrier((own, block_owner))
-    right_sends = call(
-        send_right_kernel, (block_owner, right_root), (1,),
-        [pl.BlockSpec((4, 128, 512), lambda i, owners: (0, axis("zl"), 0))],
-        whole(16, 128, 512), shape_of((16, 128, 512), BF16), [pltpu.SMEM((32,), jnp.int32)], prefetch=1,
+        pair_kernel, (own, got), (1,), [whole(64, 512)] * 2, [whole(32, 512)] * 2,
+        [shape_of((32, 512), BF16), shape_of((32, 512), F32)], cost=WAIT,
     )
     own, right_sends = lax.optimization_barrier((own, right_sends))
-    band = shape_of((32, 512), BF16)
-    across, up, down, own = call(
-        near_kernel, (own, got), (1,), [whole(128, 512)] * 2, [whole(32, 512)] * 4,
-        [band] * 3 + [shape_of((32, 512), F32)], [pltpu.VMEM((128, 512), F32)],
-    )
-    own, right_sends = lax.optimization_barrier((own, right_sends))
-    a, b, c = shift(across, 8), shift(up, 4), shift(down, -4)
+    got = shift(send, 8)
     rights = lax.all_to_all(right_sends, "owner", 0, 0, tiled=True)
     part = call(
-        far_kernel, (owner_row, own, a, b, c, lefts), (1,),
-        [whole(1, 32)] + [whole(32, 512)] * 4 + [whole(2, 16, 16, 512)],
+        far_kernel, (owner_row, own, got, lefts), (1,),
+        [whole(1, 32)] + [whole(32, 512)] * 2 + [whole(2, 16, 16, 384)],
         whole(32, 896), shape_of((32, 896), BF16), cost=WAIT,
     )
     groups = [[2 * z + (z & 1 ^ c) for z in range(16)] for c in range(2)]

time: 101 us -> 99.6 us (0.986)
  starting transfers between devices: 48.3 us -> 42.2 us
  waiting for transfers between devices: 1.56 us -> 7.46 us
  Pallas kernels: 9.26 us -> 7.31 us
    all_to_all x1, waiting for transfers between devices: 0.01 us -> 4.34 us  [shards(): lax.all_to_all(left_sends, ('core', 'owner'), 0, 0, tiled=True)]
    ppermute x5, starting transfers between devices: 25.6 us -> 22.5 us  [shift(): return lax.ppermute(x, ('zh', 'zl', 'core'), moves)]
    all_to_all x1, starting transfers between devices: 6.7 us -> 3.72 us  [shards(): rights = lax.all_to_all(right_sends, 'owner', 0, 0, tiled=True)]
    pallas_call x8 -> x7, Pallas kernels: 6.17 us -> 4.21 us  [call(): pl.pallas_call(kernel, grid_spec=pltpu.PrefetchScalarGridSpec(num_scalar_...]
    ppermute x5, waiting for transfers between devices: 1.55 us -> 3.12 us  [shift(): return lax.ppermute(x, ('zh', 'zl', 'core'), moves)]
    all_to_all x1, blocking collectives: 6.96 us -> 8.35 us  [shards(): got = lax.all_to_all(results, ('zl', 'core'), 0, 0, tiled=True)]
  transfers between devices with their start and end apart: 8 -> 8, of which waited for: 1 -> 2; matrix products, arithmetic and copies ran while one was open for 2% -> 2% of each run, Pallas kernels for 4% -> 2%
where the time goes in v5:
time: 99.6 us; the launch traced here: 99.1 us
  starting transfers between devices  42.2 us (42%)
  blocking collectives  39.8 us (40%)
  waiting for transfers between devices  7.46 us (7%)
  Pallas kernels  7.31 us (7%)
  matrix products  2.11 us (2%)
    all_gather x1, blocking collectives, shards(): lax.all_gather(part, ('zh', 'zl', 'core'), axis=0, tiled=True, axis_index...  31.4 us
    ppermute x5, starting transfers between devices, shift(): return lax.ppermute(x, ('zh', 'zl', 'core'), moves)  22.5 us
    ppermute x1, starting transfers between devices, shards(): swapped = lax.ppermute(theirs, 'core', [(0, 1), (1, 0)])  8.79 us
    all_to_all x1, blocking collectives, shards(): got = lax.all_to_all(results, ('zl', 'core'), 0, 0, tiled=True)  8.35 us
    all_to_all x1, starting transfers between devices, shards(): lax.all_to_all(left_sends, ('core', 'owner'), 0, 0, tiled=True)  7.22 us
    all_to_all x1, waiting for transfers between devices, shards(): lax.all_to_all(left_sends, ('core', 'owner'), 0, 0, tiled=True)  4.34 us
    pallas_call x7, Pallas kernels, call(): pl.pallas_call(kernel, grid_spec=pltpu.PrefetchScalarGridSpec(num_scalar_...  4.21 us
    all_to_all x1, starting transfers between devices, shards(): rights = lax.all_to_all(right_sends, 'owner', 0, 0, tiled=True)  3.72 us
  transfers between devices with their start and end apart: 8, of which 2 were waited for; matrix products, arithmetic and copies ran while one was open for 2% of the time, Pallas kernels for 2%

profile of v5, /device:TPU:1, one launch (start us, length us, event | category | flops | bytes accessed | tf_op | source)
XLA Modules:
  0.0 99.1 jit_solution(10283369486803392337)
XLA Ops:
  0.0 3.1 %shard_map.55 = bf16[512,512]{1,0:T(8,128)(2,1)} custom-call(bf16[1024,512]{1,0:T(8,128)(2,1)} %acts.1, bf16[1024,1024]{1,0:T(8,128)(2,1)} %cots.1), custom_call_target="tpu_custom_call" | custom-call | tf_op jit(solution)/shard_map/pallas_call | solution.py:169
  3.1 8.8 %collective-permute-start = (bf16[512,512]{1,0:T(8,128)(2,1)}, bf16[512,512]{1,0:T(8,128)(2,1)S(1)}, u32[]{:S(2)}, u32[]{:S(2)}) collective-permute-start(bf16[512,512]{1,0:T(8,128)(2,1)} %shard_map.55), channel_id=1, source_target_pairs={{0,16},{16,0},{1,17},{17,1},{2,18},{18,2},{3,19},{19,3},{4,20},{20... | collective-permute-start | bytes 1572872 | tf_op jit(solution)/shard_map/ppermute | solution.py:175
  11.9 0.0 copy-done.4
  11.9 0.0 copy-start
  11.9 0.0 copy-start.2
  12.0 0.0 copy-start.3
  12.0 2.1 %fusion.mine = f32[512,512]{1,0:T(8,128)S(1)} fusion(bf16[1024,512]{1,0:T(8,128)(2,1)} %acts.1, bf16[1024,1024]{1,0:T(8,128)(2,1)S(1)} %copy-done.4, s32[]{:T(128)S(6)} %select_n.3), kind=kOutput, calls=%fused_computation | convolution fusion | flops 536870912 | bytes 3145732 | tf_op jit(solution)/shard_map/dot_general | solution.py:177
  14.1 0.0 collective-permute-done.swapped
  14.1 0.1 shard_map.56
  14.2 6.2 %collective-permute-start.1 = (bf16[128,512]{1,0:T(8,128)(2,1)S(1)}, bf16[128,512]{1,0:T(8,128)(2,1)S(1)}, u32[]{:S(2)}, u32[]{:S(2)}) collective-permute-start(bf16[128,512]{1,0:T(8,128)(2,1)S(1)} %get-tuple-element.30), channel_id=1, source_target_pairs={{0,64},{16,464},{48,112},{32,480},{64,128},{80,16},{112,176},{96,3... | collective-permute-start | bytes 393224 | tf_op jit(solution)/shard_map/ppermute | solution.py:185
  20.4 2.8 %collective-permute-start.2 = (bf16[128,512]{1,0:T(8,128)(2,1)S(1)}, bf16[128,512]{1,0:T(8,128)(2,1)S(1)}, u32[]{:S(2)}, u32[]{:S(2)}) collective-permute-start(bf16[128,512]{1,0:T(8,128)(2,1)S(1)} %get-tuple-element.31), channel_id=1, source_target_pairs={{0,48},{16,480},{48,64},{32,16},{64,112},{80,32},{112,128},{96,80}... | collective-permute-start | bytes 393224 | tf_op jit(solution)/shard_map/ppermute | solution.py:185
  23.2 2.7 %collective-permute-start.3 = (bf16[128,512]{1,0:T(8,128)(2,1)S(1)}, bf16[128,512]{1,0:T(8,128)(2,1)S(1)}, u32[]{:S(2)}, u32[]{:S(2)}) collective-permute-start(bf16[128,512]{1,0:T(8,128)(2,1)S(1)} %get-tuple-element.32), channel_id=1, source_target_pairs={{0,496},{16,32},{48,0},{32,80},{64,48},{80,96},{112,64},{96,144},{... | collective-permute-start | bytes 393224 | tf_op jit(solution)/shard_map/ppermute | solution.py:185
  26.0 0.0 copy-done
  26.0 0.0 copy-done.2
  26.0 1.6 %shard_map.57 = (bf16[32,16,384]{2,1,0:T(8,128)(2,1)}, bf16[16,128,512]{2,1,0:T(8,128)(2,1)S(1)}) custom-call(s32[32]{0:T(128)S(1)} %copy-done.3, bf16[4,16,512]{2,1,0:T(8,128)(2,1)S(1)} %copy-done.2, bf16[4,512,512]{2,1,0:T(8,128)(2,1)S(1)} %copy-done), custom_call_target="tpu_custom_call" | custom-call | tf_op jit(solution)/shard_map/pallas_call | solution.py:28
  27.6 0.0 collective-permute-done.1.a
  27.6 0.0 collective-permute-done.2.b
  27.6 3.1 %collective-permute-done.3.c = bf16[128,512]{1,0:T(8,128)(2,1)S(1)} collective-permute-done((bf16[128,512]{1,0:T(8,128)(2,1)S(1)}, bf16[128,512]{1,0:T(8,128)(2,1)S(1)}, u32[]{:S(2)}, u32[]{:S(2)}) %collective-permute-start.3) | collective-permute-done | bytes 131104 | tf_op jit(solution)/shard_map/ppermute | solution.py:185
  30.7 0.1 shard_map.58
  30.8 5.2 %collective-permute-start.4 = (bf16[64,512]{1,0:T(8,128)(2,1)S(1)}, bf16[64,512]{1,0:T(8,128)(2,1)S(1)}, u32[]{:S(2)}, u32[]{:S(2)}) collective-permute-start(bf16[64,512]{1,0:T(8,128)(2,1)S(1)} %get-tuple-element.36), channel_id=1, source_target_pairs={{0,128},{16,400},{48,176},{32,416},{64,192},{80,464},{112,240},{96... | collective-permute-start | bytes 196616 | tf_op jit(solution)/shard_map/ppermute | solution.py:185
  36.0 7.2 %all-to-all-start = ((bf16[32,16,384]{2,1,0:T(8,128)(2,1)}), bf16[32,16,384]{2,1,0:T(8,128)(2,1)S(1)}, u32[]{:S(2)}, u32[]{:S(2)}) async-start(bf16[32,16,384]{2,1,0:T(8,128)(2,1)} %get-tuple-element.41), calls=%async_computation | async-start | bytes 786432 | tf_op jit(solution)/shard_map/all_to_all | solution.py:209
  43.2 0.0 collective-permute-done.4.got
  43.3 5.6 %collective-permute-start.5 = (bf16[32,512]{1,0:T(8,128)(2,1)S(1)}, bf16[32,512]{1,0:T(8,128)(2,1)S(1)}, u32[]{:S(2)}, u32[]{:S(2)}) collective-permute-start(bf16[32,512]{1,0:T(8,128)(2,1)S(1)} %get-tuple-element.40), channel_id=1, source_target_pairs={{0,256},{16,272},{48,304},{32,288},{64,320},{80,336},{112,368},{96... | collective-permute-start | bytes 98312 | tf_op jit(solution)/shard_map/ppermute | solution.py:185
  48.9 4.3 %all-to-all-done = bf16[32,16,384]{2,1,0:T(8,128)(2,1)S(1)} async-done(((bf16[32,16,384]{2,1,0:T(8,128)(2,1)}), bf16[32,16,384]{2,1,0:T(8,128)(2,1)S(1)}, u32[]{:S(2)}, u32[]{:S(2)}) %all-to-all-start) | async-done | bytes 393248 | tf_op jit(solution)/shard_map/all_to_all | solution.py:209
  53.2 3.7 %all-to-all-start.1 = ((bf16[16,128,512]{2,1,0:T(8,128)(2,1)}), bf16[16,128,512]{2,1,0:T(8,128)(2,1)S(1)}, u32[]{:S(2)}, u32[]{:S(2)}) async-start(bf16[16,128,512]{2,1,0:T(8,128)(2,1)} %copy-done.1), calls=%async_computation.1 | async-start | bytes 4194304 | tf_op jit(solution)/shard_map/all_to_all | solution.py:217
  56.9 0.0 collective-permute-done.5.got
  56.9 0.1 shard_map.60
  57.1 31.4 %all_gather.3.gathered = bf16[512,896]{1,0:T(8,128)(2,1)S(1)} all-gather(bf16[32,896]{1,0:T(8,128)(2,1)S(1)} %shard_map.60), channel_id=1, replica_groups={{0,48,64,112,128,176,192,240,256,304,320,368,384,432,448,496},{16,32,80..., dimensions={0}, use_global_device_ids=true | all-gather | bytes 974848 | tf_op jit(solution)/shard_map/all_gather | solution.py:224
  88.5 0.0 all-to-all-done.1.rights
  88.5 1.6 %shard_map.61 = bf16[8,32,128]{2,1,0:T(8,128)(2,1)S(1)} custom-call(s32[1,32]{1,0:T(1,128)S(1)} %bitcast.5, bf16[512,896]{1,0:T(8,128)(2,1)S(1)} %all_gather.3.gathered, bf16[16,128,512]{2,1,0:T(8,128)(2,1)S(1)} %all-to-all-done.1.rights), custom_call_target="tpu_custom_call" | custom-call | tf_op jit(solution)/shard_map/pallas_call | solution.py:28
  90.1 8.3 %all_to_all.15.got = bf16[8,32,128]{2,1,0:T(8,128)(2,1)S(1)} all-to-all(bf16[8,32,128]{2,1,0:T(8,128)(2,1)S(1)} %shard_map.61), channel_id=1, replica_groups=mesh['zh'=4,'zl'=4,'core'=2,'owner'=16] {'zl','core'}, dimensions={0} | all-to-all | bytes 131072 | tf_op jit(solution)/shard_map/all_to_all | solution.py:231
  98.5 0.7 shard_map.62
  (5 shorter events, 0.0 us)
Async XLA Ops:
  0.0 11.9 %copy-start.4 = (bf16[1024,1024]{1,0:T(8,128)(2,1)S(1)}, bf16[1024,1024]{1,0:T(8,128)(2,1)}, u32[]{:S(2)}) copy-start(bf16[1024,1024]{1,0:T(8,128)(2,1)} %cots.1) | copy-start | bytes 6291460
  3.1 11.0 %collective-permute-start = (bf16[512,512]{1,0:T(8,128)(2,1)}, bf16[512,512]{1,0:T(8,128)(2,1)S(1)}, u32[]{:S(2)}, u32[]{:S(2)}) collective-permute-start(bf16[512,512]{1,0:T(8,128)(2,1)} %shard_map.55), channel_id=1, source_target_pairs={{0,16},{16,0},{1,17},{17,1},{2,18},{18,2},{3,19},{19,3},{4,20},{20... | collective-permute-start | bytes 1572872 | tf_op jit(solution)/shard_map/ppermute | solution.py:175
  11.9 14.0 %copy-start = (bf16[4,512,512]{2,1,0:T(8,128)(2,1)S(1)}, bf16[4,512,512]{2,1,0:T(8,128)(2,1)}, u32[]{:S(2)}) copy-start(bf16[4,512,512]{2,1,0:T(8,128)(2,1)} %right.1) | copy-start | bytes 6291460
  11.9 14.0 %copy-start.2 = (bf16[4,16,512]{2,1,0:T(8,128)(2,1)S(1)}, bf16[4,16,512]{2,1,0:T(8,128)(2,1)}, u32[]{:S(2)}) copy-start(bf16[4,16,512]{2,1,0:T(8,128)(2,1)} %left.1) | copy-start | bytes 196612
  12.0 14.0 %copy-start.3 = (s32[32]{0:T(128)S(1)}, s32[32]{0:T(128)}, u32[]{:S(2)}) copy-start(s32[32]{0:T(128)} %owners) | copy-start | bytes 388
  14.2 13.4 %collective-permute-start.1 = (bf16[128,512]{1,0:T(8,128)(2,1)S(1)}, bf16[128,512]{1,0:T(8,128)(2,1)S(1)}, u32[]{:S(2)}, u32[]{:S(2)}) collective-permute-start(bf16[128,512]{1,0:T(8,128)(2,1)S(1)} %get-tuple-element.30), channel_id=1, source_target_pairs={{0,64},{16,464},{48,112},{32,480},{64,128},{80,16},{112,176},{96,3... | collective-permute-start | bytes 393224 | tf_op jit(solution)/shard_map/ppermute | solution.py:185
  20.4 7.2 %collective-permute-start.2 = (bf16[128,512]{1,0:T(8,128)(2,1)S(1)}, bf16[128,512]{1,0:T(8,128)(2,1)S(1)}, u32[]{:S(2)}, u32[]{:S(2)}) collective-permute-start(bf16[128,512]{1,0:T(8,128)(2,1)S(1)} %get-tuple-element.31), channel_id=1, source_target_pairs={{0,48},{16,480},{48,64},{32,16},{64,112},{80,32},{112,128},{96,80}... | collective-permute-start | bytes 393224 | tf_op jit(solution)/shard_map/ppermute | solution.py:185
  23.2 7.5 %collective-permute-start.3 = (bf16[128,512]{1,0:T(8,128)(2,1)S(1)}, bf16[128,512]{1,0:T(8,128)(2,1)S(1)}, u32[]{:S(2)}, u32[]{:S(2)}) collective-permute-start(bf16[128,512]{1,0:T(8,128)(2,1)S(1)} %get-tuple-element.32), channel_id=1, source_target_pairs={{0,496},{16,32},{48,0},{32,80},{64,48},{80,96},{112,64},{96,144},{... | collective-permute-start | bytes 393224 | tf_op jit(solution)/shard_map/ppermute | solution.py:185
  27.6 3.2 %copy-start.1 = (bf16[16,128,512]{2,1,0:T(8,128)(2,1)}, bf16[16,128,512]{2,1,0:T(8,128)(2,1)S(1)}, u32[]{:S(2)}) copy-start(bf16[16,128,512]{2,1,0:T(8,128)(2,1)S(1)} %get-tuple-element.42) | copy-start | bytes 6291460
  30.8 12.4 %collective-permute-start.4 = (bf16[64,512]{1,0:T(8,128)(2,1)S(1)}, bf16[64,512]{1,0:T(8,128)(2,1)S(1)}, u32[]{:S(2)}, u32[]{:S(2)}) collective-permute-start(bf16[64,512]{1,0:T(8,128)(2,1)S(1)} %get-tuple-element.36), channel_id=1, source_target_pairs={{0,128},{16,400},{48,176},{32,416},{64,192},{80,464},{112,240},{96... | collective-permute-start | bytes 196616 | tf_op jit(solution)/shard_map/ppermute | solution.py:185
  36.0 17.2 %all-to-all-start = ((bf16[32,16,384]{2,1,0:T(8,128)(2,1)}), bf16[32,16,384]{2,1,0:T(8,128)(2,1)S(1)}, u32[]{:S(2)}, u32[]{:S(2)}) async-start(bf16[32,16,384]{2,1,0:T(8,128)(2,1)} %get-tuple-element.41), calls=%async_computation | async-start | bytes 786432 | tf_op jit(solution)/shard_map/all_to_all | solution.py:209
  43.3 13.7 %collective-permute-start.5 = (bf16[32,512]{1,0:T(8,128)(2,1)S(1)}, bf16[32,512]{1,0:T(8,128)(2,1)S(1)}, u32[]{:S(2)}, u32[]{:S(2)}) collective-permute-start(bf16[32,512]{1,0:T(8,128)(2,1)S(1)} %get-tuple-element.40), channel_id=1, source_target_pairs={{0,256},{16,272},{48,304},{32,288},{64,320},{80,336},{112,368},{96... | collective-permute-start | bytes 98312 | tf_op jit(solution)/shard_map/ppermute | solution.py:185
  53.2 35.3 %all-to-all-start.1 = ((bf16[16,128,512]{2,1,0:T(8,128)(2,1)}), bf16[16,128,512]{2,1,0:T(8,128)(2,1)S(1)}, u32[]{:S(2)}, u32[]{:S(2)}) async-start(bf16[16,128,512]{2,1,0:T(8,128)(2,1)} %copy-done.1), calls=%async_computation.1 | async-start | bytes 4194304 | tf_op jit(solution)/shard_map/all_to_all | solution.py:217

commit v6 on v5

--- a/solution.py
+++ b/solution.py
@@ -89,8 +89,8 @@
     return jnp.sum(jnp.where(lane == block_id(), owners[...], 0))
 
 
-def split_kernel(mine, swapped, across, up, down, own):
-    for ref, offset in ((across, 2), (up, 1 + 2 * column()), (down, 3 - 2 * column()), (own, 0)):
+def split_kernel(mine, swapped, up, across, down, own):
+    for ref, offset in ((up, 1 + 2 * column()), (across, 2), (down, 3 - 2 * column()), (own, 0)):
         first = 32 * lax.rem(axis("zl") + offset, 4)
         for h in range(4):
             rows = pl.ds(pl.multiple_of(128 * h + first, 32), 32)
@@ -185,11 +185,11 @@
         return lax.ppermute(x, ("zh", "zl", "core"), moves)
 
     quarter = shape_of((128, 512), BF16)
-    across, up, down, own = call(
+    up, across, down, own = call(
         split_kernel, (mine, swapped), (1,), [whole(512, 512)] * 2,
         [whole(128, 512)] * 4, [quarter] * 3 + [shape_of((128, 512), F32)],
     )
-    a, b, c = shift(across, 2), shift(up, 1), shift(down, -1)
+    a, b, c = shift(up, 1), shift(across, 2), shift(down, -1)
 
     owner_row = block_owner.reshape(1, 32)
     own, block_owner = lax.optimization_barrier((own, block_owner))

time: 99.6 us -> 98.8 us (level)
  starting transfers between devices: 42.2 us -> 43.8 us
  waiting for transfers between devices: 7.46 us -> 6.05 us
  blocking collectives: 39.8 us -> 38.8 us
    ppermute x5, starting transfers between devices: 22.5 us -> 24.1 us  [shift(): return lax.ppermute(x, ('zh', 'zl', 'core'), moves)]
    all_to_all x1, waiting for transfers between devices: 4.34 us -> 3.04 us  [shards(): lax.all_to_all(left_sends, ('core', 'owner'), 0, 0, tiled=True)]
  transfers between devices with their start and end apart: 8 -> 8, of which waited for: 2 -> 3; matrix products, arithmetic and copies ran while one was open for 2% -> 2% of each run, Pallas kernels for 2% -> 2%
where the time goes in v6:
time: 98.8 us; the launch traced here: 98.3 us
  starting transfers between devices  43.8 us (44%)
  blocking collectives  38.8 us (39%)
  Pallas kernels  7.31 us (7%)
  waiting for transfers between devices  6.05 us (6%)
  matrix products  2.11 us (2%)
    all_gather x1, blocking collectives, shards(): lax.all_gather(part, ('zh', 'zl', 'core'), axis=0, tiled=True, axis_index...  31.4 us
    ppermute x5, starting transfers between devices, shift(): return lax.ppermute(x, ('zh', 'zl', 'core'), moves)  24.1 us
    ppermute x1, starting transfers between devices, shards(): swapped = lax.ppermute(theirs, 'core', [(0, 1), (1, 0)])  8.79 us
    all_to_all x1, blocking collectives, shards(): got = lax.all_to_all(results, ('zl', 'core'), 0, 0, tiled=True)  7.39 us
    all_to_all x1, starting transfers between devices, shards(): lax.all_to_all(left_sends, ('core', 'owner'), 0, 0, tiled=True)  7.22 us
    pallas_call x7, Pallas kernels, call(): pl.pallas_call(kernel, grid_spec=pltpu.PrefetchScalarGridSpec(num_scalar_...  4.2 us
    all_to_all x1, starting transfers between devices, shards(): rights = lax.all_to_all(right_sends, 'owner', 0, 0, tiled=True)  3.72 us
    pallas_call x1, Pallas kernels, shards(): pl.pallas_call(theirs_kernel, in_specs=[hbm] * 2, out_specs=pl.BlockSpec(...  3.1 us
  transfers between devices with their start and end apart: 8, of which 3 were waited for; matrix products, arithmetic and copies ran while one was open for 2% of the time, Pallas kernels for 2%

profile of v6, /device:TPU:1, one launch (start us, length us, event | category | flops | bytes accessed | tf_op | source)
XLA Modules:
  0.0 98.3 jit_solution(17641931215680869819)
XLA Ops:
  0.0 3.1 %shard_map.55 = bf16[512,512]{1,0:T(8,128)(2,1)} custom-call(bf16[1024,512]{1,0:T(8,128)(2,1)} %acts.1, bf16[1024,1024]{1,0:T(8,128)(2,1)} %cots.1), custom_call_target="tpu_custom_call" | custom-call | tf_op jit(solution)/shard_map/pallas_call | solution.py:169
  3.1 8.8 %collective-permute-start = (bf16[512,512]{1,0:T(8,128)(2,1)}, bf16[512,512]{1,0:T(8,128)(2,1)S(1)}, u32[]{:S(2)}, u32[]{:S(2)}) collective-permute-start(bf16[512,512]{1,0:T(8,128)(2,1)} %shard_map.55), channel_id=1, source_target_pairs={{0,16},{16,0},{1,17},{17,1},{2,18},{18,2},{3,19},{19,3},{4,20},{20... | collective-permute-start | bytes 1572872 | tf_op jit(solution)/shard_map/ppermute | solution.py:175
  11.9 0.0 copy-done.4
  11.9 0.0 copy-start
  11.9 0.0 copy-start.2
  12.0 0.0 copy-start.3
  12.0 2.1 %fusion.mine = f32[512,512]{1,0:T(8,128)S(1)} fusion(bf16[1024,512]{1,0:T(8,128)(2,1)} %acts.1, bf16[1024,1024]{1,0:T(8,128)(2,1)S(1)} %copy-done.4, s32[]{:T(128)S(6)} %select_n.3), kind=kOutput, calls=%fused_computation | convolution fusion | flops 536870912 | bytes 3145732 | tf_op jit(solution)/shard_map/dot_general | solution.py:177
  14.1 0.0 collective-permute-done.swapped
  14.1 0.1 shard_map.56
  14.2 5.6 %collective-permute-start.1 = (bf16[128,512]{1,0:T(8,128)(2,1)S(1)}, bf16[128,512]{1,0:T(8,128)(2,1)S(1)}, u32[]{:S(2)}, u32[]{:S(2)}) collective-permute-start(bf16[128,512]{1,0:T(8,128)(2,1)S(1)} %get-tuple-element.30), channel_id=1, source_target_pairs={{0,48},{16,480},{48,64},{32,16},{64,112},{80,32},{112,128},{96,80}... | collective-permute-start | bytes 393224 | tf_op jit(solution)/shard_map/ppermute | solution.py:185
  19.9 3.1 %collective-permute-start.2 = (bf16[128,512]{1,0:T(8,128)(2,1)S(1)}, bf16[128,512]{1,0:T(8,128)(2,1)S(1)}, u32[]{:S(2)}, u32[]{:S(2)}) collective-permute-start(bf16[128,512]{1,0:T(8,128)(2,1)S(1)} %get-tuple-element.31), channel_id=1, source_target_pairs={{0,64},{16,464},{48,112},{32,480},{64,128},{80,16},{112,176},{96,3... | collective-permute-start | bytes 393224 | tf_op jit(solution)/shard_map/ppermute | solution.py:185
  22.9 3.3 %collective-permute-start.3 = (bf16[128,512]{1,0:T(8,128)(2,1)S(1)}, bf16[128,512]{1,0:T(8,128)(2,1)S(1)}, u32[]{:S(2)}, u32[]{:S(2)}) collective-permute-start(bf16[128,512]{1,0:T(8,128)(2,1)S(1)} %get-tuple-element.32), channel_id=1, source_target_pairs={{0,496},{16,32},{48,0},{32,80},{64,48},{80,96},{112,64},{96,144},{... | collective-permute-start | bytes 393224 | tf_op jit(solution)/shard_map/ppermute | solution.py:185
  26.3 0.0 copy-done
  26.3 0.0 copy-done.2
  26.3 1.6 %shard_map.57 = (bf16[32,16,384]{2,1,0:T(8,128)(2,1)}, bf16[16,128,512]{2,1,0:T(8,128)(2,1)S(1)}) custom-call(s32[32]{0:T(128)S(1)} %copy-done.3, bf16[4,16,512]{2,1,0:T(8,128)(2,1)S(1)} %copy-done.2, bf16[4,512,512]{2,1,0:T(8,128)(2,1)S(1)} %copy-done), custom_call_target="tpu_custom_call" | custom-call | tf_op jit(solution)/shard_map/pallas_call | solution.py:28
  27.9 0.0 collective-permute-done.1.a
  27.9 0.0 collective-permute-done.2.b
  27.9 2.5 %collective-permute-done.3.c = bf16[128,512]{1,0:T(8,128)(2,1)S(1)} collective-permute-done((bf16[128,512]{1,0:T(8,128)(2,1)S(1)}, bf16[128,512]{1,0:T(8,128)(2,1)S(1)}, u32[]{:S(2)}, u32[]{:S(2)}) %collective-permute-start.3) | collective-permute-done | bytes 131104 | tf_op jit(solution)/shard_map/ppermute | solution.py:185
  30.4 0.1 shard_map.58
  30.5 5.2 %collective-permute-start.4 = (bf16[64,512]{1,0:T(8,128)(2,1)S(1)}, bf16[64,512]{1,0:T(8,128)(2,1)S(1)}, u32[]{:S(2)}, u32[]{:S(2)}) collective-permute-start(bf16[64,512]{1,0:T(8,128)(2,1)S(1)} %get-tuple-element.36), channel_id=1, source_target_pairs={{0,128},{16,400},{48,176},{32,416},{64,192},{80,464},{112,240},{96... | collective-permute-start | bytes 196616 | tf_op jit(solution)/shard_map/ppermute | solution.py:185
  35.7 7.2 %all-to-all-start = ((bf16[32,16,384]{2,1,0:T(8,128)(2,1)}), bf16[32,16,384]{2,1,0:T(8,128)(2,1)S(1)}, u32[]{:S(2)}, u32[]{:S(2)}) async-start(bf16[32,16,384]{2,1,0:T(8,128)(2,1)} %get-tuple-element.41), calls=%async_computation | async-start | bytes 786432 | tf_op jit(solution)/shard_map/all_to_all | solution.py:209
  43.0 0.0 collective-permute-done.4.got
  43.0 6.9 %collective-permute-start.5 = (bf16[32,512]{1,0:T(8,128)(2,1)S(1)}, bf16[32,512]{1,0:T(8,128)(2,1)S(1)}, u32[]{:S(2)}, u32[]{:S(2)}) collective-permute-start(bf16[32,512]{1,0:T(8,128)(2,1)S(1)} %get-tuple-element.40), channel_id=1, source_target_pairs={{0,256},{16,272},{48,304},{32,288},{64,320},{80,336},{112,368},{96... | collective-permute-start | bytes 98312 | tf_op jit(solution)/shard_map/ppermute | solution.py:185
  49.9 3.0 %all-to-all-done = bf16[32,16,384]{2,1,0:T(8,128)(2,1)S(1)} async-done(((bf16[32,16,384]{2,1,0:T(8,128)(2,1)}), bf16[32,16,384]{2,1,0:T(8,128)(2,1)S(1)}, u32[]{:S(2)}, u32[]{:S(2)}) %all-to-all-start) | async-done | bytes 393248 | tf_op jit(solution)/shard_map/all_to_all | solution.py:209
  52.9 3.7 %all-to-all-start.1 = ((bf16[16,128,512]{2,1,0:T(8,128)(2,1)}), bf16[16,128,512]{2,1,0:T(8,128)(2,1)S(1)}, u32[]{:S(2)}, u32[]{:S(2)}) async-start(bf16[16,128,512]{2,1,0:T(8,128)(2,1)} %copy-done.1), calls=%async_computation.1 | async-start | bytes 4194304 | tf_op jit(solution)/shard_map/all_to_all | solution.py:217
  56.6 0.5 collective-permute-done.5.got
  57.1 0.1 shard_map.60
  57.2 31.4 %all_gather.3.gathered = bf16[512,896]{1,0:T(8,128)(2,1)S(1)} all-gather(bf16[32,896]{1,0:T(8,128)(2,1)S(1)} %shard_map.60), channel_id=1, replica_groups={{0,48,64,112,128,176,192,240,256,304,320,368,384,432,448,496},{16,32,80..., dimensions={0}, use_global_device_ids=true | all-gather | bytes 974848 | tf_op jit(solution)/shard_map/all_gather | solution.py:224
  88.7 0.0 all-to-all-done.1.rights
  88.7 1.6 %shard_map.61 = bf16[8,32,128]{2,1,0:T(8,128)(2,1)S(1)} custom-call(s32[1,32]{1,0:T(1,128)S(1)} %bitcast.5, bf16[512,896]{1,0:T(8,128)(2,1)S(1)} %all_gather.3.gathered, bf16[16,128,512]{2,1,0:T(8,128)(2,1)S(1)} %all-to-all-done.1.rights), custom_call_target="tpu_custom_call" | custom-call | tf_op jit(solution)/shard_map/pallas_call | solution.py:28
  90.3 7.4 %all_to_all.15.got = bf16[8,32,128]{2,1,0:T(8,128)(2,1)S(1)} all-to-all(bf16[8,32,128]{2,1,0:T(8,128)(2,1)S(1)} %shard_map.61), channel_id=1, replica_groups=mesh['zh'=4,'zl'=4,'core'=2,'owner'=16] {'zl','core'}, dimensions={0} | all-to-all | bytes 131072 | tf_op jit(solution)/shard_map/all_to_all | solution.py:231
  97.7 0.7 shard_map.62
  (5 shorter events, 0.0 us)
Async XLA Ops:
  0.0 11.9 %copy-start.4 = (bf16[1024,1024]{1,0:T(8,128)(2,1)S(1)}, bf16[1024,1024]{1,0:T(8,128)(2,1)}, u32[]{:S(2)}) copy-start(bf16[1024,1024]{1,0:T(8,128)(2,1)} %cots.1) | copy-start | bytes 6291460
  3.1 11.0 %collective-permute-start = (bf16[512,512]{1,0:T(8,128)(2,1)}, bf16[512,512]{1,0:T(8,128)(2,1)S(1)}, u32[]{:S(2)}, u32[]{:S(2)}) collective-permute-start(bf16[512,512]{1,0:T(8,128)(2,1)} %shard_map.55), channel_id=1, source_target_pairs={{0,16},{16,0},{1,17},{17,1},{2,18},{18,2},{3,19},{19,3},{4,20},{20... | collective-permute-start | bytes 1572872 | tf_op jit(solution)/shard_map/ppermute | solution.py:175
  11.9 14.3 %copy-start = (bf16[4,512,512]{2,1,0:T(8,128)(2,1)S(1)}, bf16[4,512,512]{2,1,0:T(8,128)(2,1)}, u32[]{:S(2)}) copy-start(bf16[4,512,512]{2,1,0:T(8,128)(2,1)} %right.1) | copy-start | bytes 6291460
  11.9 14.3 %copy-start.2 = (bf16[4,16,512]{2,1,0:T(8,128)(2,1)S(1)}, bf16[4,16,512]{2,1,0:T(8,128)(2,1)}, u32[]{:S(2)}) copy-start(bf16[4,16,512]{2,1,0:T(8,128)(2,1)} %left.1) | copy-start | bytes 196612
  12.0 14.3 %copy-start.3 = (s32[32]{0:T(128)S(1)}, s32[32]{0:T(128)}, u32[]{:S(2)}) copy-start(s32[32]{0:T(128)} %owners) | copy-start | bytes 388
  14.2 13.7 %collective-permute-start.1 = (bf16[128,512]{1,0:T(8,128)(2,1)S(1)}, bf16[128,512]{1,0:T(8,128)(2,1)S(1)}, u32[]{:S(2)}, u32[]{:S(2)}) collective-permute-start(bf16[128,512]{1,0:T(8,128)(2,1)S(1)} %get-tuple-element.30), channel_id=1, source_target_pairs={{0,48},{16,480},{48,64},{32,16},{64,112},{80,32},{112,128},{96,80}... | collective-permute-start | bytes 393224 | tf_op jit(solution)/shard_map/ppermute | solution.py:185
  19.9 8.0 %collective-permute-start.2 = (bf16[128,512]{1,0:T(8,128)(2,1)S(1)}, bf16[128,512]{1,0:T(8,128)(2,1)S(1)}, u32[]{:S(2)}, u32[]{:S(2)}) collective-permute-start(bf16[128,512]{1,0:T(8,128)(2,1)S(1)} %get-tuple-element.31), channel_id=1, source_target_pairs={{0,64},{16,464},{48,112},{32,480},{64,128},{80,16},{112,176},{96,3... | collective-permute-start | bytes 393224 | tf_op jit(solution)/shard_map/ppermute | solution.py:185
  22.9 7.5 %collective-permute-start.3 = (bf16[128,512]{1,0:T(8,128)(2,1)S(1)}, bf16[128,512]{1,0:T(8,128)(2,1)S(1)}, u32[]{:S(2)}, u32[]{:S(2)}) collective-permute-start(bf16[128,512]{1,0:T(8,128)(2,1)S(1)} %get-tuple-element.32), channel_id=1, source_target_pairs={{0,496},{16,32},{48,0},{32,80},{64,48},{80,96},{112,64},{96,144},{... | collective-permute-start | bytes 393224 | tf_op jit(solution)/shard_map/ppermute | solution.py:185
  27.9 2.7 %copy-start.1 = (bf16[16,128,512]{2,1,0:T(8,128)(2,1)}, bf16[16,128,512]{2,1,0:T(8,128)(2,1)S(1)}, u32[]{:S(2)}) copy-start(bf16[16,128,512]{2,1,0:T(8,128)(2,1)S(1)} %get-tuple-element.42) | copy-start | bytes 6291460
  30.5 12.4 %collective-permute-start.4 = (bf16[64,512]{1,0:T(8,128)(2,1)S(1)}, bf16[64,512]{1,0:T(8,128)(2,1)S(1)}, u32[]{:S(2)}, u32[]{:S(2)}) collective-permute-start(bf16[64,512]{1,0:T(8,128)(2,1)S(1)} %get-tuple-element.36), channel_id=1, source_target_pairs={{0,128},{16,400},{48,176},{32,416},{64,192},{80,464},{112,240},{96... | collective-permute-start | bytes 196616 | tf_op jit(solution)/shard_map/ppermute | solution.py:185
  35.7 17.2 %all-to-all-start = ((bf16[32,16,384]{2,1,0:T(8,128)(2,1)}), bf16[32,16,384]{2,1,0:T(8,128)(2,1)S(1)}, u32[]{:S(2)}, u32[]{:S(2)}) async-start(bf16[32,16,384]{2,1,0:T(8,128)(2,1)} %get-tuple-element.41), calls=%async_computation | async-start | bytes 786432 | tf_op jit(solution)/shard_map/all_to_all | solution.py:209
  43.0 14.1 %collective-permute-start.5 = (bf16[32,512]{1,0:T(8,128)(2,1)S(1)}, bf16[32,512]{1,0:T(8,128)(2,1)S(1)}, u32[]{:S(2)}, u32[]{:S(2)}) collective-permute-start(bf16[32,512]{1,0:T(8,128)(2,1)S(1)} %get-tuple-element.40), channel_id=1, source_target_pairs={{0,256},{16,272},{48,304},{32,288},{64,320},{80,336},{112,368},{96... | collective-permute-start | bytes 98312 | tf_op jit(solution)/shard_map/ppermute | solution.py:185
  52.9 35.7 %all-to-all-start.1 = ((bf16[16,128,512]{2,1,0:T(8,128)(2,1)}), bf16[16,128,512]{2,1,0:T(8,128)(2,1)S(1)}, u32[]{:S(2)}, u32[]{:S(2)}) async-start(bf16[16,128,512]{2,1,0:T(8,128)(2,1)} %copy-done.1), calls=%async_computation.1 | async-start | bytes 4194304 | tf_op jit(solution)/shard_map/all_to_all | solution.py:217

commit v7 on v6

--- a/solution.py
+++ b/solution.py
@@ -118,14 +118,12 @@
         out[16 * half : 16 * (half + 1), 512:] = left[half, held]
 
 
-def middle_kernel(owners, gathered, rights, out, right, sem):
-    fetch = pltpu.make_async_copy(rights.at[holder(owners)], right, sem)
-    fetch.start()
+def middle_kernel(owners, gathered, rights, out):
+    right = rights[holder(owners)]
     grad = gathered[:, :512]
     wide = grad.astype(F32)
     grad_sq = jnp.sum(jnp.sum(wide * wide, axis=0, keepdims=True), axis=1, keepdims=True)
-    fetch.wait()
-    mixed = jnp.dot(right[...], grad, preferred_element_type=F32).astype(BF16)
+    mixed = jnp.dot(right, grad, preferred_element_type=F32).astype(BF16)
     mixed = mixed.T
     pieces = [mixed[128 * b : 128 * (b + 1)] for b in range(4)]
     total = jnp.zeros((128, 128), F32)
@@ -225,8 +223,7 @@
 
     results = call(
         middle_kernel, (owner_row, gathered, rights), (1,),
-        [whole(1, 32), whole(512, 896), ANY], whole(8, 32, 128), shape_of((8, 32, 128), BF16),
-        [pltpu.VMEM((128, 512), BF16), pltpu.SemaphoreType.DMA],
+        [whole(1, 32), whole(512, 896), whole(16, 128, 512)], whole(8, 32, 128), shape_of((8, 32, 128), BF16),
     )
     got = lax.all_to_all(results, ("zl", "core"), 0, 0, tiled=True)
     return call(place_kernel, (got,), (1,), [whole(8, 32, 128)], whole(16, 1024), shape_of((16, 1024), F32))

time: 98.8 us -> 98.4 us (level)
  no operation moved by 1% of the time
where the time goes in v7:
time: 98.4 us; the launch traced here: 98 us
  starting transfers between devices  43.8 us (45%)
  blocking collectives  38.8 us (39%)
  Pallas kernels  6.98 us (7%)
  waiting for transfers between devices  6.05 us (6%)
  matrix products  2.11 us (2%)
    all_gather x1, blocking collectives, shards(): lax.all_gather(part, ('zh', 'zl', 'core'), axis=0, tiled=True, axis_index...  31.4 us
    ppermute x5, starting transfers between devices, shift(): return lax.ppermute(x, ('zh', 'zl', 'core'), moves)  24.1 us
    ppermute x1, starting transfers between devices, shards(): swapped = lax.ppermute(theirs, 'core', [(0, 1), (1, 0)])  8.79 us
    all_to_all x1, blocking collectives, shards(): got = lax.all_to_all(results, ('zl', 'core'), 0, 0, tiled=True)  7.38 us
    all_to_all x1, starting transfers between devices, shards(): lax.all_to_all(left_sends, ('core', 'owner'), 0, 0, tiled=True)  7.22 us
    pallas_call x7, Pallas kernels, call(): pl.pallas_call(kernel, grid_spec=pltpu.PrefetchScalarGridSpec(num_scalar_...  3.88 us
    all_to_all x1, starting transfers between devices, shards(): rights = lax.all_to_all(right_sends, 'owner', 0, 0, tiled=True)  3.72 us
    pallas_call x1, Pallas kernels, shards(): pl.pallas_call(theirs_kernel, in_specs=[hbm] * 2, out_specs=pl.BlockSpec(...  3.1 us
  transfers between devices with their start and end apart: 8, of which 3 were waited for; matrix products, arithmetic and copies ran while one was open for 2% of the time, Pallas kernels for 2%

profile of v7, /device:TPU:1, one launch (start us, length us, event | category | flops | bytes accessed | tf_op | source)
XLA Modules:
  0.0 98.0 jit_solution(16025679285671850344)
XLA Ops:
  0.0 3.1 %shard_map.55 = bf16[512,512]{1,0:T(8,128)(2,1)} custom-call(bf16[1024,512]{1,0:T(8,128)(2,1)} %acts.1, bf16[1024,1024]{1,0:T(8,128)(2,1)} %cots.1), custom_call_target="tpu_custom_call" | custom-call | tf_op jit(solution)/shard_map/pallas_call | solution.py:167
  3.1 8.8 %collective-permute-start = (bf16[512,512]{1,0:T(8,128)(2,1)}, bf16[512,512]{1,0:T(8,128)(2,1)S(1)}, u32[]{:S(2)}, u32[]{:S(2)}) collective-permute-start(bf16[512,512]{1,0:T(8,128)(2,1)} %shard_map.55), channel_id=1, source_target_pairs={{0,16},{16,0},{1,17},{17,1},{2,18},{18,2},{3,19},{19,3},{4,20},{20... | collective-permute-start | bytes 1572872 | tf_op jit(solution)/shard_map/ppermute | solution.py:173
  11.9 0.0 copy-done.4
  11.9 0.0 copy-start
  11.9 0.0 copy-start.2
  12.0 0.0 copy-start.3
  12.0 2.1 %fusion.mine = f32[512,512]{1,0:T(8,128)S(1)} fusion(bf16[1024,512]{1,0:T(8,128)(2,1)} %acts.1, bf16[1024,1024]{1,0:T(8,128)(2,1)S(1)} %copy-done.4, s32[]{:T(128)S(6)} %select_n.3), kind=kOutput, calls=%fused_computation | convolution fusion | flops 536870912 | bytes 3145732 | tf_op jit(solution)/shard_map/dot_general | solution.py:175
  14.1 0.0 collective-permute-done.swapped
  14.1 0.1 shard_map.56
  14.2 5.6 %collective-permute-start.1 = (bf16[128,512]{1,0:T(8,128)(2,1)S(1)}, bf16[128,512]{1,0:T(8,128)(2,1)S(1)}, u32[]{:S(2)}, u32[]{:S(2)}) collective-permute-start(bf16[128,512]{1,0:T(8,128)(2,1)S(1)} %get-tuple-element.30), channel_id=1, source_target_pairs={{0,48},{16,480},{48,64},{32,16},{64,112},{80,32},{112,128},{96,80}... | collective-permute-start | bytes 393224 | tf_op jit(solution)/shard_map/ppermute | solution.py:183
  19.9 3.1 %collective-permute-start.2 = (bf16[128,512]{1,0:T(8,128)(2,1)S(1)}, bf16[128,512]{1,0:T(8,128)(2,1)S(1)}, u32[]{:S(2)}, u32[]{:S(2)}) collective-permute-start(bf16[128,512]{1,0:T(8,128)(2,1)S(1)} %get-tuple-element.31), channel_id=1, source_target_pairs={{0,64},{16,464},{48,112},{32,480},{64,128},{80,16},{112,176},{96,3... | collective-permute-start | bytes 393224 | tf_op jit(solution)/shard_map/ppermute | solution.py:183
  22.9 3.3 %collective-permute-start.3 = (bf16[128,512]{1,0:T(8,128)(2,1)S(1)}, bf16[128,512]{1,0:T(8,128)(2,1)S(1)}, u32[]{:S(2)}, u32[]{:S(2)}) collective-permute-start(bf16[128,512]{1,0:T(8,128)(2,1)S(1)} %get-tuple-element.32), channel_id=1, source_target_pairs={{0,496},{16,32},{48,0},{32,80},{64,48},{80,96},{112,64},{96,144},{... | collective-permute-start | bytes 393224 | tf_op jit(solution)/shard_map/ppermute | solution.py:183
  26.3 0.0 copy-done
  26.3 0.0 copy-done.2
  26.3 1.6 %shard_map.57 = (bf16[32,16,384]{2,1,0:T(8,128)(2,1)}, bf16[16,128,512]{2,1,0:T(8,128)(2,1)S(1)}) custom-call(s32[32]{0:T(128)S(1)} %copy-done.3, bf16[4,16,512]{2,1,0:T(8,128)(2,1)S(1)} %copy-done.2, bf16[4,512,512]{2,1,0:T(8,128)(2,1)S(1)} %copy-done), custom_call_target="tpu_custom_call" | custom-call | tf_op jit(solution)/shard_map/pallas_call | solution.py:28
  27.9 0.0 collective-permute-done.1.a
  27.9 0.0 collective-permute-done.2.b
  27.9 2.5 %collective-permute-done.3.c = bf16[128,512]{1,0:T(8,128)(2,1)S(1)} collective-permute-done((bf16[128,512]{1,0:T(8,128)(2,1)S(1)}, bf16[128,512]{1,0:T(8,128)(2,1)S(1)}, u32[]{:S(2)}, u32[]{:S(2)}) %collective-permute-start.3) | collective-permute-done | bytes 131104 | tf_op jit(solution)/shard_map/ppermute | solution.py:183
  30.4 0.1 shard_map.58
  30.5 5.2 %collective-permute-start.4 = (bf16[64,512]{1,0:T(8,128)(2,1)S(1)}, bf16[64,512]{1,0:T(8,128)(2,1)S(1)}, u32[]{:S(2)}, u32[]{:S(2)}) collective-permute-start(bf16[64,512]{1,0:T(8,128)(2,1)S(1)} %get-tuple-element.36), channel_id=1, source_target_pairs={{0,128},{16,400},{48,176},{32,416},{64,192},{80,464},{112,240},{96... | collective-permute-start | bytes 196616 | tf_op jit(solution)/shard_map/ppermute | solution.py:183
  35.7 7.2 %all-to-all-start = ((bf16[32,16,384]{2,1,0:T(8,128)(2,1)}), bf16[32,16,384]{2,1,0:T(8,128)(2,1)S(1)}, u32[]{:S(2)}, u32[]{:S(2)}) async-start(bf16[32,16,384]{2,1,0:T(8,128)(2,1)} %get-tuple-element.41), calls=%async_computation | async-start | bytes 786432 | tf_op jit(solution)/shard_map/all_to_all | solution.py:207
  43.0 0.0 collective-permute-done.4.got
  43.0 6.9 %collective-permute-start.5 = (bf16[32,512]{1,0:T(8,128)(2,1)S(1)}, bf16[32,512]{1,0:T(8,128)(2,1)S(1)}, u32[]{:S(2)}, u32[]{:S(2)}) collective-permute-start(bf16[32,512]{1,0:T(8,128)(2,1)S(1)} %get-tuple-element.40), channel_id=1, source_target_pairs={{0,256},{16,272},{48,304},{32,288},{64,320},{80,336},{112,368},{96... | collective-permute-start | bytes 98312 | tf_op jit(solution)/shard_map/ppermute | solution.py:183
  49.9 3.0 %all-to-all-done = bf16[32,16,384]{2,1,0:T(8,128)(2,1)S(1)} async-done(((bf16[32,16,384]{2,1,0:T(8,128)(2,1)}), bf16[32,16,384]{2,1,0:T(8,128)(2,1)S(1)}, u32[]{:S(2)}, u32[]{:S(2)}) %all-to-all-start) | async-done | bytes 393248 | tf_op jit(solution)/shard_map/all_to_all | solution.py:207
  52.9 3.7 %all-to-all-start.1 = ((bf16[16,128,512]{2,1,0:T(8,128)(2,1)}), bf16[16,128,512]{2,1,0:T(8,128)(2,1)S(1)}, u32[]{:S(2)}, u32[]{:S(2)}) async-start(bf16[16,128,512]{2,1,0:T(8,128)(2,1)} %copy-done.1), calls=%async_computation.1 | async-start | bytes 4194304 | tf_op jit(solution)/shard_map/all_to_all | solution.py:215
  56.6 0.5 collective-permute-done.5.got
  57.1 0.1 shard_map.60
  57.2 31.4 %all_gather.3.gathered = bf16[512,896]{1,0:T(8,128)(2,1)S(1)} all-gather(bf16[32,896]{1,0:T(8,128)(2,1)S(1)} %shard_map.60), channel_id=1, replica_groups={{0,48,64,112,128,176,192,240,256,304,320,368,384,432,448,496},{16,32,80..., dimensions={0}, use_global_device_ids=true | all-gather | bytes 974848 | tf_op jit(solution)/shard_map/all_gather | solution.py:222
  88.7 0.0 all-to-all-done.1.rights
  88.7 1.3 %shard_map.61 = bf16[8,32,128]{2,1,0:T(8,128)(2,1)S(1)} custom-call(s32[1,32]{1,0:T(1,128)S(1)} %bitcast.5, bf16[512,896]{1,0:T(8,128)(2,1)S(1)} %all_gather.3.gathered, bf16[16,128,512]{2,1,0:T(8,128)(2,1)S(1)} %all-to-all-done.1.rights), custom_call_target="tpu_custom_call" | custom-call | tf_op jit(solution)/shard_map/pallas_call | solution.py:28
  89.9 7.4 %all_to_all.15.got = bf16[8,32,128]{2,1,0:T(8,128)(2,1)S(1)} all-to-all(bf16[8,32,128]{2,1,0:T(8,128)(2,1)S(1)} %shard_map.61), channel_id=1, replica_groups=mesh['zh'=4,'zl'=4,'core'=2,'owner'=16] {'zl','core'}, dimensions={0} | all-to-all | bytes 131072 | tf_op jit(solution)/shard_map/all_to_all | solution.py:228
  97.3 0.7 shard_map.62
  (5 shorter events, 0.0 us)
Async XLA Ops:
  0.0 11.9 %copy-start.4 = (bf16[1024,1024]{1,0:T(8,128)(2,1)S(1)}, bf16[1024,1024]{1,0:T(8,128)(2,1)}, u32[]{:S(2)}) copy-start(bf16[1024,1024]{1,0:T(8,128)(2,1)} %cots.1) | copy-start | bytes 6291460
  3.1 11.0 %collective-permute-start = (bf16[512,512]{1,0:T(8,128)(2,1)}, bf16[512,512]{1,0:T(8,128)(2,1)S(1)}, u32[]{:S(2)}, u32[]{:S(2)}) collective-permute-start(bf16[512,512]{1,0:T(8,128)(2,1)} %shard_map.55), channel_id=1, source_target_pairs={{0,16},{16,0},{1,17},{17,1},{2,18},{18,2},{3,19},{19,3},{4,20},{20... | collective-permute-start | bytes 1572872 | tf_op jit(solution)/shard_map/ppermute | solution.py:173
  11.9 14.3 %copy-start = (bf16[4,512,512]{2,1,0:T(8,128)(2,1)S(1)}, bf16[4,512,512]{2,1,0:T(8,128)(2,1)}, u32[]{:S(2)}) copy-start(bf16[4,512,512]{2,1,0:T(8,128)(2,1)} %right.1) | copy-start | bytes 6291460
  11.9 14.3 %copy-start.2 = (bf16[4,16,512]{2,1,0:T(8,128)(2,1)S(1)}, bf16[4,16,512]{2,1,0:T(8,128)(2,1)}, u32[]{:S(2)}) copy-start(bf16[4,16,512]{2,1,0:T(8,128)(2,1)} %left.1) | copy-start | bytes 196612
  12.0 14.3 %copy-start.3 = (s32[32]{0:T(128)S(1)}, s32[32]{0:T(128)}, u32[]{:S(2)}) copy-start(s32[32]{0:T(128)} %owners) | copy-start | bytes 388
  14.2 13.7 %collective-permute-start.1 = (bf16[128,512]{1,0:T(8,128)(2,1)S(1)}, bf16[128,512]{1,0:T(8,128)(2,1)S(1)}, u32[]{:S(2)}, u32[]{:S(2)}) collective-permute-start(bf16[128,512]{1,0:T(8,128)(2,1)S(1)} %get-tuple-element.30), channel_id=1, source_target_pairs={{0,48},{16,480},{48,64},{32,16},{64,112},{80,32},{112,128},{96,80}... | collective-permute-start | bytes 393224 | tf_op jit(solution)/shard_map/ppermute | solution.py:183
  19.9 8.0 %collective-permute-start.2 = (bf16[128,512]{1,0:T(8,128)(2,1)S(1)}, bf16[128,512]{1,0:T(8,128)(2,1)S(1)}, u32[]{:S(2)}, u32[]{:S(2)}) collective-permute-start(bf16[128,512]{1,0:T(8,128)(2,1)S(1)} %get-tuple-element.31), channel_id=1, source_target_pairs={{0,64},{16,464},{48,112},{32,480},{64,128},{80,16},{112,176},{96,3... | collective-permute-start | bytes 393224 | tf_op jit(solution)/shard_map/ppermute | solution.py:183
  22.9 7.5 %collective-permute-start.3 = (bf16[128,512]{1,0:T(8,128)(2,1)S(1)}, bf16[128,512]{1,0:T(8,128)(2,1)S(1)}, u32[]{:S(2)}, u32[]{:S(2)}) collective-permute-start(bf16[128,512]{1,0:T(8,128)(2,1)S(1)} %get-tuple-element.32), channel_id=1, source_target_pairs={{0,496},{16,32},{48,0},{32,80},{64,48},{80,96},{112,64},{96,144},{... | collective-permute-start | bytes 393224 | tf_op jit(solution)/shard_map/ppermute | solution.py:183
  27.9 2.7 %copy-start.1 = (bf16[16,128,512]{2,1,0:T(8,128)(2,1)}, bf16[16,128,512]{2,1,0:T(8,128)(2,1)S(1)}, u32[]{:S(2)}) copy-start(bf16[16,128,512]{2,1,0:T(8,128)(2,1)S(1)} %get-tuple-element.42) | copy-start | bytes 6291460
  30.5 12.4 %collective-permute-start.4 = (bf16[64,512]{1,0:T(8,128)(2,1)S(1)}, bf16[64,512]{1,0:T(8,128)(2,1)S(1)}, u32[]{:S(2)}, u32[]{:S(2)}) collective-permute-start(bf16[64,512]{1,0:T(8,128)(2,1)S(1)} %get-tuple-element.36), channel_id=1, source_target_pairs={{0,128},{16,400},{48,176},{32,416},{64,192},{80,464},{112,240},{96... | collective-permute-start | bytes 196616 | tf_op jit(solution)/shard_map/ppermute | solution.py:183
  35.7 17.2 %all-to-all-start = ((bf16[32,16,384]{2,1,0:T(8,128)(2,1)}), bf16[32,16,384]{2,1,0:T(8,128)(2,1)S(1)}, u32[]{:S(2)}, u32[]{:S(2)}) async-start(bf16[32,16,384]{2,1,0:T(8,128)(2,1)} %get-tuple-element.41), calls=%async_computation | async-start | bytes 786432 | tf_op jit(solution)/shard_map/all_to_all | solution.py:207
  43.0 14.1 %collective-permute-start.5 = (bf16[32,512]{1,0:T(8,128)(2,1)S(1)}, bf16[32,512]{1,0:T(8,128)(2,1)S(1)}, u32[]{:S(2)}, u32[]{:S(2)}) collective-permute-start(bf16[32,512]{1,0:T(8,128)(2,1)S(1)} %get-tuple-element.40), channel_id=1, source_target_pairs={{0,256},{16,272},{48,304},{32,288},{64,320},{80,336},{112,368},{96... | collective-permute-start | bytes 98312 | tf_op jit(solution)/shard_map/ppermute | solution.py:183
  52.9 35.7 %all-to-all-start.1 = ((bf16[16,128,512]{2,1,0:T(8,128)(2,1)}), bf16[16,128,512]{2,1,0:T(8,128)(2,1)S(1)}, u32[]{:S(2)}, u32[]{:S(2)}) async-start(bf16[16,128,512]{2,1,0:T(8,128)(2,1)} %copy-done.1), calls=%async_computation.1 | async-start | bytes 4194304 | tf_op jit(solution)/shard_map/all_to_all | solution.py:215

commit v8 on v7

--- a/solution.py
+++ b/solution.py
@@ -66,7 +66,7 @@
                 left_out[16 * core + i, :, 128 * j : 128 * (j + 1)] = left[slots[2 * i + (core ^ flip)], :, lanes]
 
 
-def theirs_kernel(acts, cots, out, some_acts, some_cots, sems):
+def theirs_kernel(acts, cots, out, some_acts, some_cots, staged, sems, out_sems):
     lanes = pl.ds(pl.multiple_of((1 - column()) * 512, 512), 512)
     copies = []
     for i in range(4):
@@ -76,12 +76,23 @@
     for copy in copies:
         copy.start()
     acc = jnp.zeros((512, 512), F32)
-    for i in range(4):
+    for i in range(3):
         copies[2 * i].wait()
         copies[2 * i + 1].wait()
         rows = pl.ds(256 * i, 256)
         acc += lax.dot_general(some_cots[rows, :], some_acts[rows, :], ROWS_FIRST, preferred_element_type=F32)
-    out[...] = acc.astype(BF16)
+    copies[6].wait()
+    copies[7].wait()
+    writes = []
+    for half in range(2):
+        here = slice(256 * half, 256 * (half + 1))
+        last = lax.dot_general(some_cots[768:, here], some_acts[768:, :], ROWS_FIRST, preferred_element_type=F32)
+        staged[here] = (acc[here] + last).astype(BF16)
+        rows = pl.ds(256 * half, 256)
+        writes.append(pltpu.make_async_copy(staged.at[rows], out.at[rows], out_sems.at[half]))
+        writes[half].start()
+    for write in writes:
+        write.wait()
 
 
 def holder(owners):
@@ -165,9 +176,10 @@
 def shards(activations, key_cotangent, block_owner, left_root, right_root):
     hbm = pl.BlockSpec(memory_space=pltpu.HBM)
     theirs = pl.pallas_call(
-        theirs_kernel, in_specs=[hbm] * 2, out_specs=pl.BlockSpec(memory_space=pltpu.VMEM),
+        theirs_kernel, in_specs=[hbm] * 2, out_specs=hbm,
         out_shape=shape_of((512, 512), BF16),
-        scratch_shapes=[pltpu.VMEM((1024, 512), BF16)] * 2 + [pltpu.SemaphoreType.DMA((2, 4))],
+        scratch_shapes=[pltpu.VMEM((1024, 512), BF16)] * 2
+        + [pltpu.VMEM((512, 512), BF16), pltpu.SemaphoreType.DMA((2, 4)), pltpu.SemaphoreType.DMA((2,))],
         compiler_params=pltpu.CompilerParams(vmem_limit_bytes=60 * 1024 * 1024),
     )(activations, key_cotangent)
     swapped = lax.ppermute(theirs, "core", [(0, 1), (1, 0)])

time: 98.4 us -> 98.4 us (level)
  no operation moved by 1% of the time
where the time goes in v8:
time: 98.4 us; the launch traced here: 97.9 us
  starting transfers between devices  43.8 us (45%)
  blocking collectives  38.8 us (39%)
  Pallas kernels  6.92 us (7%)
  waiting for transfers between devices  6.03 us (6%)
  matrix products  2.12 us (2%)
    all_gather x1, blocking collectives, shards(): lax.all_gather(part, ('zh', 'zl', 'core'), axis=0, tiled=True, axis_index...  31.4 us
    ppermute x5, starting transfers between devices, shift(): return lax.ppermute(x, ('zh', 'zl', 'core'), moves)  24.1 us
    ppermute x1, starting transfers between devices, shards(): swapped = lax.ppermute(theirs, 'core', [(0, 1), (1, 0)])  8.79 us
    all_to_all x1, blocking collectives, shards(): got = lax.all_to_all(results, ('zl', 'core'), 0, 0, tiled=True)  7.37 us
    all_to_all x1, starting transfers between devices, shards(): lax.all_to_all(left_sends, ('core', 'owner'), 0, 0, tiled=True)  7.22 us
    pallas_call x7, Pallas kernels, call(): pl.pallas_call(kernel, grid_spec=pltpu.PrefetchScalarGridSpec(num_scalar_...  3.88 us
    all_to_all x1, starting transfers between devices, shards(): rights = lax.all_to_all(right_sends, 'owner', 0, 0, tiled=True)  3.72 us
    pallas_call x1, Pallas kernels, shards(): pl.pallas_call(theirs_kernel, in_specs=[hbm] * 2, out_specs=hbm, out_shap...  3.04 us
  transfers between devices with their start and end apart: 8, of which 3 were waited for; matrix products, arithmetic and copies ran while one was open for 2% of the time, Pallas kernels for 2%

profile of v8, /device:TPU:1, one launch (start us, length us, event | category | flops | bytes accessed | tf_op | source)
XLA Modules:
  0.0 97.9 jit_solution(1900584420412109710)
XLA Ops:
  0.0 3.0 %shard_map.55 = bf16[512,512]{1,0:T(8,128)(2,1)} custom-call(bf16[1024,512]{1,0:T(8,128)(2,1)} %acts.1, bf16[1024,1024]{1,0:T(8,128)(2,1)} %cots.1), custom_call_target="tpu_custom_call" | custom-call | tf_op jit(solution)/shard_map/pallas_call | solution.py:178
  3.1 8.8 %collective-permute-start = (bf16[512,512]{1,0:T(8,128)(2,1)}, bf16[512,512]{1,0:T(8,128)(2,1)S(1)}, u32[]{:S(2)}, u32[]{:S(2)}) collective-permute-start(bf16[512,512]{1,0:T(8,128)(2,1)} %shard_map.55), channel_id=1, source_target_pairs={{0,16},{16,0},{1,17},{17,1},{2,18},{18,2},{3,19},{19,3},{4,20},{20... | collective-permute-start | bytes 1572872 | tf_op jit(solution)/shard_map/ppermute | solution.py:185
  11.9 0.0 copy-done.4
  11.9 0.0 copy-start
  11.9 0.0 copy-start.2
  11.9 0.0 copy-start.3
  11.9 2.1 %fusion.mine = f32[512,512]{1,0:T(8,128)S(1)} fusion(bf16[1024,512]{1,0:T(8,128)(2,1)} %acts.1, bf16[1024,1024]{1,0:T(8,128)(2,1)S(1)} %copy-done.4, s32[]{:T(128)S(6)} %select_n.3), kind=kOutput, calls=%fused_computation | convolution fusion | flops 536870912 | bytes 3145732 | tf_op jit(solution)/shard_map/dot_general | solution.py:187
  14.0 0.0 collective-permute-done.swapped
  14.0 0.1 shard_map.56
  14.2 5.6 %collective-permute-start.1 = (bf16[128,512]{1,0:T(8,128)(2,1)S(1)}, bf16[128,512]{1,0:T(8,128)(2,1)S(1)}, u32[]{:S(2)}, u32[]{:S(2)}) collective-permute-start(bf16[128,512]{1,0:T(8,128)(2,1)S(1)} %get-tuple-element.30), channel_id=1, source_target_pairs={{0,48},{16,480},{48,64},{32,16},{64,112},{80,32},{112,128},{96,80}... | collective-permute-start | bytes 393224 | tf_op jit(solution)/shard_map/ppermute | solution.py:195
  19.8 3.1 %collective-permute-start.2 = (bf16[128,512]{1,0:T(8,128)(2,1)S(1)}, bf16[128,512]{1,0:T(8,128)(2,1)S(1)}, u32[]{:S(2)}, u32[]{:S(2)}) collective-permute-start(bf16[128,512]{1,0:T(8,128)(2,1)S(1)} %get-tuple-element.31), channel_id=1, source_target_pairs={{0,64},{16,464},{48,112},{32,480},{64,128},{80,16},{112,176},{96,3... | collective-permute-start | bytes 393224 | tf_op jit(solution)/shard_map/ppermute | solution.py:195
  22.9 3.3 %collective-permute-start.3 = (bf16[128,512]{1,0:T(8,128)(2,1)S(1)}, bf16[128,512]{1,0:T(8,128)(2,1)S(1)}, u32[]{:S(2)}, u32[]{:S(2)}) collective-permute-start(bf16[128,512]{1,0:T(8,128)(2,1)S(1)} %get-tuple-element.32), channel_id=1, source_target_pairs={{0,496},{16,32},{48,0},{32,80},{64,48},{80,96},{112,64},{96,144},{... | collective-permute-start | bytes 393224 | tf_op jit(solution)/shard_map/ppermute | solution.py:195
  26.2 0.0 copy-done
  26.2 0.0 copy-done.2
  26.2 1.6 %shard_map.57 = (bf16[32,16,384]{2,1,0:T(8,128)(2,1)}, bf16[16,128,512]{2,1,0:T(8,128)(2,1)S(1)}) custom-call(s32[32]{0:T(128)S(1)} %copy-done.3, bf16[4,16,512]{2,1,0:T(8,128)(2,1)S(1)} %copy-done.2, bf16[4,512,512]{2,1,0:T(8,128)(2,1)S(1)} %copy-done), custom_call_target="tpu_custom_call" | custom-call | tf_op jit(solution)/shard_map/pallas_call | solution.py:28
  27.8 0.0 collective-permute-done.1.a
  27.8 0.0 collective-permute-done.2.b
  27.8 2.5 %collective-permute-done.3.c = bf16[128,512]{1,0:T(8,128)(2,1)S(1)} collective-permute-done((bf16[128,512]{1,0:T(8,128)(2,1)S(1)}, bf16[128,512]{1,0:T(8,128)(2,1)S(1)}, u32[]{:S(2)}, u32[]{:S(2)}) %collective-permute-start.3) | collective-permute-done | bytes 131104 | tf_op jit(solution)/shard_map/ppermute | solution.py:195
  30.4 0.1 shard_map.58
  30.5 5.2 %collective-permute-start.4 = (bf16[64,512]{1,0:T(8,128)(2,1)S(1)}, bf16[64,512]{1,0:T(8,128)(2,1)S(1)}, u32[]{:S(2)}, u32[]{:S(2)}) collective-permute-start(bf16[64,512]{1,0:T(8,128)(2,1)S(1)} %get-tuple-element.36), channel_id=1, source_target_pairs={{0,128},{16,400},{48,176},{32,416},{64,192},{80,464},{112,240},{96... | collective-permute-start | bytes 196616 | tf_op jit(solution)/shard_map/ppermute | solution.py:195
  35.7 7.2 %all-to-all-start = ((bf16[32,16,384]{2,1,0:T(8,128)(2,1)}), bf16[32,16,384]{2,1,0:T(8,128)(2,1)S(1)}, u32[]{:S(2)}, u32[]{:S(2)}) async-start(bf16[32,16,384]{2,1,0:T(8,128)(2,1)} %get-tuple-element.41), calls=%async_computation | async-start | bytes 786432 | tf_op jit(solution)/shard_map/all_to_all | solution.py:219
  42.9 0.0 collective-permute-done.4.got
  42.9 6.9 %collective-permute-start.5 = (bf16[32,512]{1,0:T(8,128)(2,1)S(1)}, bf16[32,512]{1,0:T(8,128)(2,1)S(1)}, u32[]{:S(2)}, u32[]{:S(2)}) collective-permute-start(bf16[32,512]{1,0:T(8,128)(2,1)S(1)} %get-tuple-element.40), channel_id=1, source_target_pairs={{0,256},{16,272},{48,304},{32,288},{64,320},{80,336},{112,368},{96... | collective-permute-start | bytes 98312 | tf_op jit(solution)/shard_map/ppermute | solution.py:195
  49.8 3.0 %all-to-all-done = bf16[32,16,384]{2,1,0:T(8,128)(2,1)S(1)} async-done(((bf16[32,16,384]{2,1,0:T(8,128)(2,1)}), bf16[32,16,384]{2,1,0:T(8,128)(2,1)S(1)}, u32[]{:S(2)}, u32[]{:S(2)}) %all-to-all-start) | async-done | bytes 393248 | tf_op jit(solution)/shard_map/all_to_all | solution.py:219
  52.9 3.7 %all-to-all-start.1 = ((bf16[16,128,512]{2,1,0:T(8,128)(2,1)}), bf16[16,128,512]{2,1,0:T(8,128)(2,1)S(1)}, u32[]{:S(2)}, u32[]{:S(2)}) async-start(bf16[16,128,512]{2,1,0:T(8,128)(2,1)} %copy-done.1), calls=%async_computation.1 | async-start | bytes 4194304 | tf_op jit(solution)/shard_map/all_to_all | solution.py:227
  56.6 0.4 collective-permute-done.5.got
  57.0 0.1 shard_map.60
  57.2 31.4 %all_gather.3.gathered = bf16[512,896]{1,0:T(8,128)(2,1)S(1)} all-gather(bf16[32,896]{1,0:T(8,128)(2,1)S(1)} %shard_map.60), channel_id=1, replica_groups={{0,48,64,112,128,176,192,240,256,304,320,368,384,432,448,496},{16,32,80..., dimensions={0}, use_global_device_ids=true | all-gather | bytes 974848 | tf_op jit(solution)/shard_map/all_gather | solution.py:234
  88.6 0.0 all-to-all-done.1.rights
  88.6 1.3 %shard_map.61 = bf16[8,32,128]{2,1,0:T(8,128)(2,1)S(1)} custom-call(s32[1,32]{1,0:T(1,128)S(1)} %bitcast.5, bf16[512,896]{1,0:T(8,128)(2,1)S(1)} %all_gather.3.gathered, bf16[16,128,512]{2,1,0:T(8,128)(2,1)S(1)} %all-to-all-done.1.rights), custom_call_target="tpu_custom_call" | custom-call | tf_op jit(solution)/shard_map/pallas_call | solution.py:28
  89.9 7.4 %all_to_all.15.got = bf16[8,32,128]{2,1,0:T(8,128)(2,1)S(1)} all-to-all(bf16[8,32,128]{2,1,0:T(8,128)(2,1)S(1)} %shard_map.61), channel_id=1, replica_groups=mesh['zh'=4,'zl'=4,'core'=2,'owner'=16] {'zl','core'}, dimensions={0} | all-to-all | bytes 131072 | tf_op jit(solution)/shard_map/all_to_all | solution.py:240
  97.3 0.7 shard_map.62
  (5 shorter events, 0.0 us)
Async XLA Ops:
  0.0 11.9 %copy-start.4 = (bf16[1024,1024]{1,0:T(8,128)(2,1)S(1)}, bf16[1024,1024]{1,0:T(8,128)(2,1)}, u32[]{:S(2)}) copy-start(bf16[1024,1024]{1,0:T(8,128)(2,1)} %cots.1) | copy-start | bytes 6291460
  3.1 11.0 %collective-permute-start = (bf16[512,512]{1,0:T(8,128)(2,1)}, bf16[512,512]{1,0:T(8,128)(2,1)S(1)}, u32[]{:S(2)}, u32[]{:S(2)}) collective-permute-start(bf16[512,512]{1,0:T(8,128)(2,1)} %shard_map.55), channel_id=1, source_target_pairs={{0,16},{16,0},{1,17},{17,1},{2,18},{18,2},{3,19},{19,3},{4,20},{20... | collective-permute-start | bytes 1572872 | tf_op jit(solution)/shard_map/ppermute | solution.py:185
  11.9 14.3 %copy-start = (bf16[4,512,512]{2,1,0:T(8,128)(2,1)S(1)}, bf16[4,512,512]{2,1,0:T(8,128)(2,1)}, u32[]{:S(2)}) copy-start(bf16[4,512,512]{2,1,0:T(8,128)(2,1)} %right.1) | copy-start | bytes 6291460
  11.9 14.3 %copy-start.2 = (bf16[4,16,512]{2,1,0:T(8,128)(2,1)S(1)}, bf16[4,16,512]{2,1,0:T(8,128)(2,1)}, u32[]{:S(2)}) copy-start(bf16[4,16,512]{2,1,0:T(8,128)(2,1)} %left.1) | copy-start | bytes 196612
  11.9 14.3 %copy-start.3 = (s32[32]{0:T(128)S(1)}, s32[32]{0:T(128)}, u32[]{:S(2)}) copy-start(s32[32]{0:T(128)} %owners) | copy-start | bytes 388
  14.2 13.7 %collective-permute-start.1 = (bf16[128,512]{1,0:T(8,128)(2,1)S(1)}, bf16[128,512]{1,0:T(8,128)(2,1)S(1)}, u32[]{:S(2)}, u32[]{:S(2)}) collective-permute-start(bf16[128,512]{1,0:T(8,128)(2,1)S(1)} %get-tuple-element.30), channel_id=1, source_target_pairs={{0,48},{16,480},{48,64},{32,16},{64,112},{80,32},{112,128},{96,80}... | collective-permute-start | bytes 393224 | tf_op jit(solution)/shard_map/ppermute | solution.py:195
  19.8 8.0 %collective-permute-start.2 = (bf16[128,512]{1,0:T(8,128)(2,1)S(1)}, bf16[128,512]{1,0:T(8,128)(2,1)S(1)}, u32[]{:S(2)}, u32[]{:S(2)}) collective-permute-start(bf16[128,512]{1,0:T(8,128)(2,1)S(1)} %get-tuple-element.31), channel_id=1, source_target_pairs={{0,64},{16,464},{48,112},{32,480},{64,128},{80,16},{112,176},{96,3... | collective-permute-start | bytes 393224 | tf_op jit(solution)/shard_map/ppermute | solution.py:195
  22.9 7.5 %collective-permute-start.3 = (bf16[128,512]{1,0:T(8,128)(2,1)S(1)}, bf16[128,512]{1,0:T(8,128)(2,1)S(1)}, u32[]{:S(2)}, u32[]{:S(2)}) collective-permute-start(bf16[128,512]{1,0:T(8,128)(2,1)S(1)} %get-tuple-element.32), channel_id=1, source_target_pairs={{0,496},{16,32},{48,0},{32,80},{64,48},{80,96},{112,64},{96,144},{... | collective-permute-start | bytes 393224 | tf_op jit(solution)/shard_map/ppermute | solution.py:195
  27.8 2.6 %copy-start.1 = (bf16[16,128,512]{2,1,0:T(8,128)(2,1)}, bf16[16,128,512]{2,1,0:T(8,128)(2,1)S(1)}, u32[]{:S(2)}) copy-start(bf16[16,128,512]{2,1,0:T(8,128)(2,1)S(1)} %get-tuple-element.42) | copy-start | bytes 6291460
  30.5 12.4 %collective-permute-start.4 = (bf16[64,512]{1,0:T(8,128)(2,1)S(1)}, bf16[64,512]{1,0:T(8,128)(2,1)S(1)}, u32[]{:S(2)}, u32[]{:S(2)}) collective-permute-start(bf16[64,512]{1,0:T(8,128)(2,1)S(1)} %get-tuple-element.36), channel_id=1, source_target_pairs={{0,128},{16,400},{48,176},{32,416},{64,192},{80,464},{112,240},{96... | collective-permute-start | bytes 196616 | tf_op jit(solution)/shard_map/ppermute | solution.py:195
  35.7 17.2 %all-to-all-start = ((bf16[32,16,384]{2,1,0:T(8,128)(2,1)}), bf16[32,16,384]{2,1,0:T(8,128)(2,1)S(1)}, u32[]{:S(2)}, u32[]{:S(2)}) async-start(bf16[32,16,384]{2,1,0:T(8,128)(2,1)} %get-tuple-element.41), calls=%async_computation | async-start | bytes 786432 | tf_op jit(solution)/shard_map/all_to_all | solution.py:219
  42.9 14.1 %collective-permute-start.5 = (bf16[32,512]{1,0:T(8,128)(2,1)S(1)}, bf16[32,512]{1,0:T(8,128)(2,1)S(1)}, u32[]{:S(2)}, u32[]{:S(2)}) collective-permute-start(bf16[32,512]{1,0:T(8,128)(2,1)S(1)} %get-tuple-element.40), channel_id=1, source_target_pairs={{0,256},{16,272},{48,304},{32,288},{64,320},{80,336},{112,368},{96... | collective-permute-start | bytes 98312 | tf_op jit(solution)/shard_map/ppermute | solution.py:195
  52.9 35.7 %all-to-all-start.1 = ((bf16[16,128,512]{2,1,0:T(8,128)(2,1)}), bf16[16,128,512]{2,1,0:T(8,128)(2,1)S(1)}, u32[]{:S(2)}, u32[]{:S(2)}) async-start(bf16[16,128,512]{2,1,0:T(8,128)(2,1)} %copy-done.1), calls=%async_computation.1 | async-start | bytes 4194304 | tf_op jit(solution)/shard_map/all_to_all | solution.py:227

commit v9 on v8

--- a/solution.py
+++ b/solution.py
@@ -101,7 +101,7 @@
 
 
 def split_kernel(mine, swapped, up, across, down, own):
-    for ref, offset in ((up, 1 + 2 * column()), (across, 2), (down, 3 - 2 * column()), (own, 0)):
+    for ref, offset in ((up, 1 + column()), (across, 2 + column()), (down, 3 - 2 * column()), (own, 0)):
         first = 32 * lax.rem(axis("zl") + offset, 4)
         for h in range(4):
             rows = pl.ds(pl.multiple_of(128 * h + first, 32), 32)
@@ -186,11 +186,11 @@
     columns = lax.dynamic_slice_in_dim(key_cotangent, column() * 512, 512, 1)
     mine = lax.dot_general(columns, activations, ROWS_FIRST, preferred_element_type=F32)
 
-    def shift(x, step):
+    def shift(x, step, other=None):
         moves = []
         for z in range(16):
             for block in range(2):
-                to = (z + (-step if block else step)) % 16
+                to = (z + (-(step if other is None else other) if block else step)) % 16
                 moves.append((2 * z + (block ^ (z & 1)), 2 * to + (block ^ (to & 1))))
         return lax.ppermute(x, ("zh", "zl", "core"), moves)
 
@@ -199,7 +199,7 @@
         split_kernel, (mine, swapped), (1,), [whole(512, 512)] * 2,
         [whole(128, 512)] * 4, [quarter] * 3 + [shape_of((128, 512), F32)],
     )
-    a, b, c = shift(up, 1), shift(across, 2), shift(down, -1)
+    a, b, c = shift(up, 1, 2), shift(across, 2, 1), shift(down, -1)
 
     owner_row = block_owner.reshape(1, 32)
     own, block_owner = lax.optimization_barrier((own, block_owner))

time: 98.4 us -> 98.9 us (level)
  waiting for transfers between devices: 6.03 us -> 7.75 us
  starting transfers between devices: 43.8 us -> 42.3 us
    ppermute x5, starting transfers between devices: 24.1 us -> 22.6 us  [shift(): return lax.ppermute(x, ('zh', 'zl', 'core'), moves)]
    all_to_all x1, waiting for transfers between devices: 3.04 us -> 4.26 us  [shards(): lax.all_to_all(left_sends, ('core', 'owner'), 0, 0, tiled=True)]
where the time goes in v9:
time: 98.9 us; the launch traced here: 98.4 us
  starting transfers between devices  42.3 us (43%)
  blocking collectives  39.1 us (40%)
  waiting for transfers between devices  7.75 us (8%)
  Pallas kernels  6.92 us (7%)
  matrix products  2.12 us (2%)
    all_gather x1, blocking collectives, shards(): lax.all_gather(part, ('zh', 'zl', 'core'), axis=0, tiled=True, axis_index...  31 us
    ppermute x5, starting transfers between devices, shift(): return lax.ppermute(x, ('zh', 'zl', 'core'), moves)  22.6 us
    ppermute x1, starting transfers between devices, shards(): swapped = lax.ppermute(theirs, 'core', [(0, 1), (1, 0)])  8.79 us
    all_to_all x1, blocking collectives, shards(): got = lax.all_to_all(results, ('zl', 'core'), 0, 0, tiled=True)  8.05 us
    all_to_all x1, starting transfers between devices, shards(): lax.all_to_all(left_sends, ('core', 'owner'), 0, 0, tiled=True)  7.22 us
    all_to_all x1, waiting for transfers between devices, shards(): lax.all_to_all(left_sends, ('core', 'owner'), 0, 0, tiled=True)  4.26 us
    pallas_call x7, Pallas kernels, call(): pl.pallas_call(kernel, grid_spec=pltpu.PrefetchScalarGridSpec(num_scalar_...  3.88 us
    all_to_all x1, starting transfers between devices, shards(): rights = lax.all_to_all(right_sends, 'owner', 0, 0, tiled=True)  3.72 us
  transfers between devices with their start and end apart: 8, of which 3 were waited for; matrix products, arithmetic and copies ran while one was open for 2% of the time, Pallas kernels for 2%

profile of v9, /device:TPU:1, one launch (start us, length us, event | category | flops | bytes accessed | tf_op | source)
XLA Modules:
  0.0 98.4 jit_solution(6817430518322928528)
XLA Ops:
  0.0 3.0 %shard_map.55 = bf16[512,512]{1,0:T(8,128)(2,1)} custom-call(bf16[1024,512]{1,0:T(8,128)(2,1)} %acts.1, bf16[1024,1024]{1,0:T(8,128)(2,1)} %cots.1), custom_call_target="tpu_custom_call" | custom-call | tf_op jit(solution)/shard_map/pallas_call | solution.py:178
  3.1 8.8 %collective-permute-start = (bf16[512,512]{1,0:T(8,128)(2,1)}, bf16[512,512]{1,0:T(8,128)(2,1)S(1)}, u32[]{:S(2)}, u32[]{:S(2)}) collective-permute-start(bf16[512,512]{1,0:T(8,128)(2,1)} %shard_map.55), channel_id=1, source_target_pairs={{0,16},{16,0},{1,17},{17,1},{2,18},{18,2},{3,19},{19,3},{4,20},{20... | collective-permute-start | bytes 1572872 | tf_op jit(solution)/shard_map/ppermute | solution.py:185
  11.9 0.0 copy-done.4
  11.9 0.0 copy-start
  11.9 0.0 copy-start.2
  11.9 0.0 copy-start.3
  11.9 2.1 %fusion.mine = f32[512,512]{1,0:T(8,128)S(1)} fusion(bf16[1024,512]{1,0:T(8,128)(2,1)} %acts.1, bf16[1024,1024]{1,0:T(8,128)(2,1)S(1)} %copy-done.4, s32[]{:T(128)S(6)} %select_n.3), kind=kOutput, calls=%fused_computation | convolution fusion | flops 536870912 | bytes 3145732 | tf_op jit(solution)/shard_map/dot_general | solution.py:187
  14.0 0.0 collective-permute-done.swapped
  14.0 0.1 shard_map.56
  14.2 6.2 %collective-permute-start.1 = (bf16[128,512]{1,0:T(8,128)(2,1)S(1)}, bf16[128,512]{1,0:T(8,128)(2,1)S(1)}, u32[]{:S(2)}, u32[]{:S(2)}) collective-permute-start(bf16[128,512]{1,0:T(8,128)(2,1)S(1)} %get-tuple-element.30), channel_id=1, source_target_pairs={{0,48},{16,464},{48,64},{32,480},{64,112},{80,16},{112,128},{96,32... | collective-permute-start | bytes 393224 | tf_op jit(solution)/shard_map/ppermute | solution.py:195
  20.4 2.8 %collective-permute-start.2 = (bf16[128,512]{1,0:T(8,128)(2,1)S(1)}, bf16[128,512]{1,0:T(8,128)(2,1)S(1)}, u32[]{:S(2)}, u32[]{:S(2)}) collective-permute-start(bf16[128,512]{1,0:T(8,128)(2,1)S(1)} %get-tuple-element.31), channel_id=1, source_target_pairs={{0,64},{16,480},{48,112},{32,16},{64,128},{80,32},{112,176},{96,80... | collective-permute-start | bytes 393224 | tf_op jit(solution)/shard_map/ppermute | solution.py:195
  23.2 2.8 %collective-permute-start.3 = (bf16[128,512]{1,0:T(8,128)(2,1)S(1)}, bf16[128,512]{1,0:T(8,128)(2,1)S(1)}, u32[]{:S(2)}, u32[]{:S(2)}) collective-permute-start(bf16[128,512]{1,0:T(8,128)(2,1)S(1)} %get-tuple-element.32), channel_id=1, source_target_pairs={{0,496},{16,32},{48,0},{32,80},{64,48},{80,96},{112,64},{96,144},{... | collective-permute-start | bytes 393224 | tf_op jit(solution)/shard_map/ppermute | solution.py:195
  25.9 0.0 copy-done
  25.9 0.0 copy-done.2
  26.0 1.6 %shard_map.57 = (bf16[32,16,384]{2,1,0:T(8,128)(2,1)}, bf16[16,128,512]{2,1,0:T(8,128)(2,1)S(1)}) custom-call(s32[32]{0:T(128)S(1)} %copy-done.3, bf16[4,16,512]{2,1,0:T(8,128)(2,1)S(1)} %copy-done.2, bf16[4,512,512]{2,1,0:T(8,128)(2,1)S(1)} %copy-done), custom_call_target="tpu_custom_call" | custom-call | tf_op jit(solution)/shard_map/pallas_call | solution.py:28
  27.6 0.0 collective-permute-done.1.a
  27.6 0.0 collective-permute-done.2.b
  27.6 3.1 %collective-permute-done.3.c = bf16[128,512]{1,0:T(8,128)(2,1)S(1)} collective-permute-done((bf16[128,512]{1,0:T(8,128)(2,1)S(1)}, bf16[128,512]{1,0:T(8,128)(2,1)S(1)}, u32[]{:S(2)}, u32[]{:S(2)}) %collective-permute-start.3) | collective-permute-done | bytes 131104 | tf_op jit(solution)/shard_map/ppermute | solution.py:195
  30.7 0.1 shard_map.58
  30.8 5.2 %collective-permute-start.4 = (bf16[64,512]{1,0:T(8,128)(2,1)S(1)}, bf16[64,512]{1,0:T(8,128)(2,1)S(1)}, u32[]{:S(2)}, u32[]{:S(2)}) collective-permute-start(bf16[64,512]{1,0:T(8,128)(2,1)S(1)} %get-tuple-element.36), channel_id=1, source_target_pairs={{0,128},{16,400},{48,176},{32,416},{64,192},{80,464},{112,240},{96... | collective-permute-start | bytes 196616 | tf_op jit(solution)/shard_map/ppermute | solution.py:195
  36.0 7.2 %all-to-all-start = ((bf16[32,16,384]{2,1,0:T(8,128)(2,1)}), bf16[32,16,384]{2,1,0:T(8,128)(2,1)S(1)}, u32[]{:S(2)}, u32[]{:S(2)}) async-start(bf16[32,16,384]{2,1,0:T(8,128)(2,1)} %get-tuple-element.41), calls=%async_computation | async-start | bytes 786432 | tf_op jit(solution)/shard_map/all_to_all | solution.py:219
  43.2 0.0 collective-permute-done.4.got
  43.2 5.7 %collective-permute-start.5 = (bf16[32,512]{1,0:T(8,128)(2,1)S(1)}, bf16[32,512]{1,0:T(8,128)(2,1)S(1)}, u32[]{:S(2)}, u32[]{:S(2)}) collective-permute-start(bf16[32,512]{1,0:T(8,128)(2,1)S(1)} %get-tuple-element.40), channel_id=1, source_target_pairs={{0,256},{16,272},{48,304},{32,288},{64,320},{80,336},{112,368},{96... | collective-permute-start | bytes 98312 | tf_op jit(solution)/shard_map/ppermute | solution.py:195
  48.9 4.3 %all-to-all-done = bf16[32,16,384]{2,1,0:T(8,128)(2,1)S(1)} async-done(((bf16[32,16,384]{2,1,0:T(8,128)(2,1)}), bf16[32,16,384]{2,1,0:T(8,128)(2,1)S(1)}, u32[]{:S(2)}, u32[]{:S(2)}) %all-to-all-start) | async-done | bytes 393248 | tf_op jit(solution)/shard_map/all_to_all | solution.py:219
  53.1 3.7 %all-to-all-start.1 = ((bf16[16,128,512]{2,1,0:T(8,128)(2,1)}), bf16[16,128,512]{2,1,0:T(8,128)(2,1)S(1)}, u32[]{:S(2)}, u32[]{:S(2)}) async-start(bf16[16,128,512]{2,1,0:T(8,128)(2,1)} %copy-done.1), calls=%async_computation.1 | async-start | bytes 4194304 | tf_op jit(solution)/shard_map/all_to_all | solution.py:227
  56.9 0.4 collective-permute-done.5.got
  57.3 0.1 shard_map.60
  57.4 31.0 %all_gather.3.gathered = bf16[512,896]{1,0:T(8,128)(2,1)S(1)} all-gather(bf16[32,896]{1,0:T(8,128)(2,1)S(1)} %shard_map.60), channel_id=1, replica_groups={{0,48,64,112,128,176,192,240,256,304,320,368,384,432,448,496},{16,32,80..., dimensions={0}, use_global_device_ids=true | all-gather | bytes 974848 | tf_op jit(solution)/shard_map/all_gather | solution.py:234
  88.4 0.0 all-to-all-done.1.rights
  88.4 1.3 %shard_map.61 = bf16[8,32,128]{2,1,0:T(8,128)(2,1)S(1)} custom-call(s32[1,32]{1,0:T(1,128)S(1)} %bitcast.5, bf16[512,896]{1,0:T(8,128)(2,1)S(1)} %all_gather.3.gathered, bf16[16,128,512]{2,1,0:T(8,128)(2,1)S(1)} %all-to-all-done.1.rights), custom_call_target="tpu_custom_call" | custom-call | tf_op jit(solution)/shard_map/pallas_call | solution.py:28
  89.7 8.1 %all_to_all.15.got = bf16[8,32,128]{2,1,0:T(8,128)(2,1)S(1)} all-to-all(bf16[8,32,128]{2,1,0:T(8,128)(2,1)S(1)} %shard_map.61), channel_id=1, replica_groups=mesh['zh'=4,'zl'=4,'core'=2,'owner'=16] {'zl','core'}, dimensions={0} | all-to-all | bytes 131072 | tf_op jit(solution)/shard_map/all_to_all | solution.py:240
  97.8 0.7 shard_map.62
  (5 shorter events, 0.0 us)
Async XLA Ops:
  0.0 11.9 %copy-start.4 = (bf16[1024,1024]{1,0:T(8,128)(2,1)S(1)}, bf16[1024,1024]{1,0:T(8,128)(2,1)}, u32[]{:S(2)}) copy-start(bf16[1024,1024]{1,0:T(8,128)(2,1)} %cots.1) | copy-start | bytes 6291460
  3.1 11.0 %collective-permute-start = (bf16[512,512]{1,0:T(8,128)(2,1)}, bf16[512,512]{1,0:T(8,128)(2,1)S(1)}, u32[]{:S(2)}, u32[]{:S(2)}) collective-permute-start(bf16[512,512]{1,0:T(8,128)(2,1)} %shard_map.55), channel_id=1, source_target_pairs={{0,16},{16,0},{1,17},{17,1},{2,18},{18,2},{3,19},{19,3},{4,20},{20... | collective-permute-start | bytes 1572872 | tf_op jit(solution)/shard_map/ppermute | solution.py:185
  11.9 14.1 %copy-start = (bf16[4,512,512]{2,1,0:T(8,128)(2,1)S(1)}, bf16[4,512,512]{2,1,0:T(8,128)(2,1)}, u32[]{:S(2)}) copy-start(bf16[4,512,512]{2,1,0:T(8,128)(2,1)} %right.1) | copy-start | bytes 6291460
  11.9 14.1 %copy-start.2 = (bf16[4,16,512]{2,1,0:T(8,128)(2,1)S(1)}, bf16[4,16,512]{2,1,0:T(8,128)(2,1)}, u32[]{:S(2)}) copy-start(bf16[4,16,512]{2,1,0:T(8,128)(2,1)} %left.1) | copy-start | bytes 196612
  11.9 14.1 %copy-start.3 = (s32[32]{0:T(128)S(1)}, s32[32]{0:T(128)}, u32[]{:S(2)}) copy-start(s32[32]{0:T(128)} %owners) | copy-start | bytes 388
  14.2 13.4 %collective-permute-start.1 = (bf16[128,512]{1,0:T(8,128)(2,1)S(1)}, bf16[128,512]{1,0:T(8,128)(2,1)S(1)}, u32[]{:S(2)}, u32[]{:S(2)}) collective-permute-start(bf16[128,512]{1,0:T(8,128)(2,1)S(1)} %get-tuple-element.30), channel_id=1, source_target_pairs={{0,48},{16,464},{48,64},{32,480},{64,112},{80,16},{112,128},{96,32... | collective-permute-start | bytes 393224 | tf_op jit(solution)/shard_map/ppermute | solution.py:195
  20.4 7.2 %collective-permute-start.2 = (bf16[128,512]{1,0:T(8,128)(2,1)S(1)}, bf16[128,512]{1,0:T(8,128)(2,1)S(1)}, u32[]{:S(2)}, u32[]{:S(2)}) collective-permute-start(bf16[128,512]{1,0:T(8,128)(2,1)S(1)} %get-tuple-element.31), channel_id=1, source_target_pairs={{0,64},{16,480},{48,112},{32,16},{64,128},{80,32},{112,176},{96,80... | collective-permute-start | bytes 393224 | tf_op jit(solution)/shard_map/ppermute | solution.py:195
  23.2 7.5 %collective-permute-start.3 = (bf16[128,512]{1,0:T(8,128)(2,1)S(1)}, bf16[128,512]{1,0:T(8,128)(2,1)S(1)}, u32[]{:S(2)}, u32[]{:S(2)}) collective-permute-start(bf16[128,512]{1,0:T(8,128)(2,1)S(1)} %get-tuple-element.32), channel_id=1, source_target_pairs={{0,496},{16,32},{48,0},{32,80},{64,48},{80,96},{112,64},{96,144},{... | collective-permute-start | bytes 393224 | tf_op jit(solution)/shard_map/ppermute | solution.py:195
  27.6 3.2 %copy-start.1 = (bf16[16,128,512]{2,1,0:T(8,128)(2,1)}, bf16[16,128,512]{2,1,0:T(8,128)(2,1)S(1)}, u32[]{:S(2)}) copy-start(bf16[16,128,512]{2,1,0:T(8,128)(2,1)S(1)} %get-tuple-element.42) | copy-start | bytes 6291460
  30.8 12.4 %collective-permute-start.4 = (bf16[64,512]{1,0:T(8,128)(2,1)S(1)}, bf16[64,512]{1,0:T(8,128)(2,1)S(1)}, u32[]{:S(2)}, u32[]{:S(2)}) collective-permute-start(bf16[64,512]{1,0:T(8,128)(2,1)S(1)} %get-tuple-element.36), channel_id=1, source_target_pairs={{0,128},{16,400},{48,176},{32,416},{64,192},{80,464},{112,240},{96... | collective-permute-start | bytes 196616 | tf_op jit(solution)/shard_map/ppermute | solution.py:195
  36.0 17.2 %all-to-all-start = ((bf16[32,16,384]{2,1,0:T(8,128)(2,1)}), bf16[32,16,384]{2,1,0:T(8,128)(2,1)S(1)}, u32[]{:S(2)}, u32[]{:S(2)}) async-start(bf16[32,16,384]{2,1,0:T(8,128)(2,1)} %get-tuple-element.41), calls=%async_computation | async-start | bytes 786432 | tf_op jit(solution)/shard_map/all_to_all | solution.py:219
  43.2 14.0 %collective-permute-start.5 = (bf16[32,512]{1,0:T(8,128)(2,1)S(1)}, bf16[32,512]{1,0:T(8,128)(2,1)S(1)}, u32[]{:S(2)}, u32[]{:S(2)}) collective-permute-start(bf16[32,512]{1,0:T(8,128)(2,1)S(1)} %get-tuple-element.40), channel_id=1, source_target_pairs={{0,256},{16,272},{48,304},{32,288},{64,320},{80,336},{112,368},{96... | collective-permute-start | bytes 98312 | tf_op jit(solution)/shard_map/ppermute | solution.py:195
  53.1 35.3 %all-to-all-start.1 = ((bf16[16,128,512]{2,1,0:T(8,128)(2,1)}), bf16[16,128,512]{2,1,0:T(8,128)(2,1)S(1)}, u32[]{:S(2)}, u32[]{:S(2)}) async-start(bf16[16,128,512]{2,1,0:T(8,128)(2,1)} %copy-done.1), calls=%async_computation.1 | async-start | bytes 4194304 | tf_op jit(solution)/shard_map/all_to_all | solution.py:227

commit v10 on v8

--- a/solution.py
+++ b/solution.py
@@ -199,7 +199,7 @@
         split_kernel, (mine, swapped), (1,), [whole(512, 512)] * 2,
         [whole(128, 512)] * 4, [quarter] * 3 + [shape_of((128, 512), F32)],
     )
-    a, b, c = shift(up, 1), shift(across, 2), shift(down, -1)
+    a, b, c = shift(up, 1), shift(across, -2), shift(down, -1)
 
     owner_row = block_owner.reshape(1, 32)
     own, block_owner = lax.optimization_barrier((own, block_owner))

time: 98.4 us -> 98.2 us (level)
  starting transfers between devices: 43.8 us -> 42.6 us
    ppermute x5, starting transfers between devices: 24.1 us -> 22.4 us  [shift(): return lax.ppermute(x, ('zh', 'zl', 'core'), moves)]
    ppermute x5, waiting for transfers between devices: 2.98 us -> 4.13 us  [shift(): return lax.ppermute(x, ('zh', 'zl', 'core'), moves)]
where the time goes in v10:
time: 98.2 us; the launch traced here: 97.7 us
  starting transfers between devices  42.6 us (43%)
  blocking collectives  39.2 us (40%)
  Pallas kernels  6.93 us (7%)
  waiting for transfers between devices  6.66 us (7%)
  matrix products  2.12 us (2%)
    all_gather x1, blocking collectives, shards(): lax.all_gather(part, ('zh', 'zl', 'core'), axis=0, tiled=True, axis_index...  30.9 us
    ppermute x5, starting transfers between devices, shift(): return lax.ppermute(x, ('zh', 'zl', 'core'), moves)  22.4 us
    ppermute x1, starting transfers between devices, shards(): swapped = lax.ppermute(theirs, 'core', [(0, 1), (1, 0)])  8.79 us
    all_to_all x1, blocking collectives, shards(): got = lax.all_to_all(results, ('zl', 'core'), 0, 0, tiled=True)  8.32 us
    all_to_all x1, starting transfers between devices, shards(): lax.all_to_all(left_sends, ('core', 'owner'), 0, 0, tiled=True)  7.22 us
    all_to_all x1, starting transfers between devices, shards(): rights = lax.all_to_all(right_sends, 'owner', 0, 0, tiled=True)  4.19 us
    ppermute x5, waiting for transfers between devices, shift(): return lax.ppermute(x, ('zh', 'zl', 'core'), moves)  4.13 us
    pallas_call x7, Pallas kernels, call(): pl.pallas_call(kernel, grid_spec=pltpu.PrefetchScalarGridSpec(num_scalar_...  3.89 us
  transfers between devices with their start and end apart: 8, of which 3 were waited for; matrix products, arithmetic and copies ran while one was open for 2% of the time, Pallas kernels for 2%

profile of v10, /device:TPU:1, one launch (start us, length us, event | category | flops | bytes accessed | tf_op | source)
XLA Modules:
  0.0 97.7 jit_solution(6019965671241145290)
XLA Ops:
  0.0 3.0 %shard_map.55 = bf16[512,512]{1,0:T(8,128)(2,1)} custom-call(bf16[1024,512]{1,0:T(8,128)(2,1)} %acts.1, bf16[1024,1024]{1,0:T(8,128)(2,1)} %cots.1), custom_call_target="tpu_custom_call" | custom-call | tf_op jit(solution)/shard_map/pallas_call | solution.py:178
  3.1 8.8 %collective-permute-start = (bf16[512,512]{1,0:T(8,128)(2,1)}, bf16[512,512]{1,0:T(8,128)(2,1)S(1)}, u32[]{:S(2)}, u32[]{:S(2)}) collective-permute-start(bf16[512,512]{1,0:T(8,128)(2,1)} %shard_map.55), channel_id=1, source_target_pairs={{0,16},{16,0},{1,17},{17,1},{2,18},{18,2},{3,19},{19,3},{4,20},{20... | collective-permute-start | bytes 1572872 | tf_op jit(solution)/shard_map/ppermute | solution.py:185
  11.9 0.0 copy-done.4
  11.9 0.0 copy-start
  11.9 0.0 copy-start.2
  11.9 0.0 copy-start.3
  11.9 2.1 %fusion.mine = f32[512,512]{1,0:T(8,128)S(1)} fusion(bf16[1024,512]{1,0:T(8,128)(2,1)} %acts.1, bf16[1024,1024]{1,0:T(8,128)(2,1)S(1)} %copy-done.4, s32[]{:T(128)S(6)} %select_n.3), kind=kOutput, calls=%fused_computation | convolution fusion | flops 536870912 | bytes 3145732 | tf_op jit(solution)/shard_map/dot_general | solution.py:187
  14.0 0.0 collective-permute-done.swapped
  14.0 0.1 shard_map.56
  14.2 5.6 %collective-permute-start.1 = (bf16[128,512]{1,0:T(8,128)(2,1)S(1)}, bf16[128,512]{1,0:T(8,128)(2,1)S(1)}, u32[]{:S(2)}, u32[]{:S(2)}) collective-permute-start(bf16[128,512]{1,0:T(8,128)(2,1)S(1)} %get-tuple-element.30), channel_id=1, source_target_pairs={{0,48},{16,480},{48,64},{32,16},{64,112},{80,32},{112,128},{96,80}... | collective-permute-start | bytes 393224 | tf_op jit(solution)/shard_map/ppermute | solution.py:195
  19.8 1.9 %collective-permute-start.2 = (bf16[128,512]{1,0:T(8,128)(2,1)S(1)}, bf16[128,512]{1,0:T(8,128)(2,1)S(1)}, u32[]{:S(2)}, u32[]{:S(2)}) collective-permute-start(bf16[128,512]{1,0:T(8,128)(2,1)S(1)} %get-tuple-element.31), channel_id=1, source_target_pairs={{0,448},{16,80},{48,496},{32,96},{64,0},{80,144},{112,48},{96,160}... | collective-permute-start | bytes 393224 | tf_op jit(solution)/shard_map/ppermute | solution.py:195
  21.7 1.9 %collective-permute-start.3 = (bf16[128,512]{1,0:T(8,128)(2,1)S(1)}, bf16[128,512]{1,0:T(8,128)(2,1)S(1)}, u32[]{:S(2)}, u32[]{:S(2)}) collective-permute-start(bf16[128,512]{1,0:T(8,128)(2,1)S(1)} %get-tuple-element.32), channel_id=1, source_target_pairs={{0,496},{16,32},{48,0},{32,80},{64,48},{80,96},{112,64},{96,144},{... | collective-permute-start | bytes 393224 | tf_op jit(solution)/shard_map/ppermute | solution.py:195
  23.7 0.0 copy-done
  23.7 1.6 %shard_map.57 = (bf16[32,16,384]{2,1,0:T(8,128)(2,1)}, bf16[16,128,512]{2,1,0:T(8,128)(2,1)S(1)}) custom-call(s32[32]{0:T(128)S(1)} %copy-done.3, bf16[4,16,512]{2,1,0:T(8,128)(2,1)S(1)} %copy-done.2, bf16[4,512,512]{2,1,0:T(8,128)(2,1)S(1)} %copy-done), custom_call_target="tpu_custom_call" | custom-call | tf_op jit(solution)/shard_map/pallas_call | solution.py:28
  25.3 0.0 collective-permute-done.1.a
  25.3 3.8 %collective-permute-done.2.b = bf16[128,512]{1,0:T(8,128)(2,1)S(1)} collective-permute-done((bf16[128,512]{1,0:T(8,128)(2,1)S(1)}, bf16[128,512]{1,0:T(8,128)(2,1)S(1)}, u32[]{:S(2)}, u32[]{:S(2)}) %collective-permute-start.2) | collective-permute-done | bytes 131104 | tf_op jit(solution)/shard_map/ppermute | solution.py:195
  29.1 0.3 collective-permute-done.3.c
  29.4 0.1 shard_map.58
  29.5 0.0 copy-done.1
  29.5 5.5 %collective-permute-start.4 = (bf16[64,512]{1,0:T(8,128)(2,1)S(1)}, bf16[64,512]{1,0:T(8,128)(2,1)S(1)}, u32[]{:S(2)}, u32[]{:S(2)}) collective-permute-start(bf16[64,512]{1,0:T(8,128)(2,1)S(1)} %get-tuple-element.36), channel_id=1, source_target_pairs={{0,128},{16,400},{48,176},{32,416},{64,192},{80,464},{112,240},{96... | collective-permute-start | bytes 196616 | tf_op jit(solution)/shard_map/ppermute | solution.py:195
  35.0 7.2 %all-to-all-start = ((bf16[32,16,384]{2,1,0:T(8,128)(2,1)}), bf16[32,16,384]{2,1,0:T(8,128)(2,1)S(1)}, u32[]{:S(2)}, u32[]{:S(2)}) async-start(bf16[32,16,384]{2,1,0:T(8,128)(2,1)} %get-tuple-element.41), calls=%async_computation | async-start | bytes 786432 | tf_op jit(solution)/shard_map/all_to_all | solution.py:219
  42.3 0.0 collective-permute-done.4.got
  42.3 7.4 %collective-permute-start.5 = (bf16[32,512]{1,0:T(8,128)(2,1)S(1)}, bf16[32,512]{1,0:T(8,128)(2,1)S(1)}, u32[]{:S(2)}, u32[]{:S(2)}) collective-permute-start(bf16[32,512]{1,0:T(8,128)(2,1)S(1)} %get-tuple-element.40), channel_id=1, source_target_pairs={{0,256},{16,272},{48,304},{32,288},{64,320},{80,336},{112,368},{96... | collective-permute-start | bytes 98312 | tf_op jit(solution)/shard_map/ppermute | solution.py:195
  49.7 2.5 %all-to-all-done = bf16[32,16,384]{2,1,0:T(8,128)(2,1)S(1)} async-done(((bf16[32,16,384]{2,1,0:T(8,128)(2,1)}), bf16[32,16,384]{2,1,0:T(8,128)(2,1)S(1)}, u32[]{:S(2)}, u32[]{:S(2)}) %all-to-all-start) | async-done | bytes 393248 | tf_op jit(solution)/shard_map/all_to_all | solution.py:219
  52.2 4.2 %all-to-all-start.1 = ((bf16[16,128,512]{2,1,0:T(8,128)(2,1)}), bf16[16,128,512]{2,1,0:T(8,128)(2,1)S(1)}, u32[]{:S(2)}, u32[]{:S(2)}) async-start(bf16[16,128,512]{2,1,0:T(8,128)(2,1)} %copy-done.1), calls=%async_computation.1 | async-start | bytes 4194304 | tf_op jit(solution)/shard_map/all_to_all | solution.py:227
  56.4 0.0 collective-permute-done.5.got
  56.4 0.1 shard_map.60
  56.6 30.9 %all_gather.3.gathered = bf16[512,896]{1,0:T(8,128)(2,1)S(1)} all-gather(bf16[32,896]{1,0:T(8,128)(2,1)S(1)} %shard_map.60), channel_id=1, replica_groups={{0,48,64,112,128,176,192,240,256,304,320,368,384,432,448,496},{16,32,80..., dimensions={0}, use_global_device_ids=true | all-gather | bytes 974848 | tf_op jit(solution)/shard_map/all_gather | solution.py:234
  87.5 0.0 all-to-all-done.1.rights
  87.5 1.3 %shard_map.61 = bf16[8,32,128]{2,1,0:T(8,128)(2,1)S(1)} custom-call(s32[1,32]{1,0:T(1,128)S(1)} %bitcast.5, bf16[512,896]{1,0:T(8,128)(2,1)S(1)} %all_gather.3.gathered, bf16[16,128,512]{2,1,0:T(8,128)(2,1)S(1)} %all-to-all-done.1.rights), custom_call_target="tpu_custom_call" | custom-call | tf_op jit(solution)/shard_map/pallas_call | solution.py:28
  88.8 8.3 %all_to_all.15.got = bf16[8,32,128]{2,1,0:T(8,128)(2,1)S(1)} all-to-all(bf16[8,32,128]{2,1,0:T(8,128)(2,1)S(1)} %shard_map.61), channel_id=1, replica_groups=mesh['zh'=4,'zl'=4,'core'=2,'owner'=16] {'zl','core'}, dimensions={0} | all-to-all | bytes 131072 | tf_op jit(solution)/shard_map/all_to_all | solution.py:240
  97.1 0.7 shard_map.62
  (5 shorter events, 0.0 us)
Async XLA Ops:
  0.0 11.9 %copy-start.4 = (bf16[1024,1024]{1,0:T(8,128)(2,1)S(1)}, bf16[1024,1024]{1,0:T(8,128)(2,1)}, u32[]{:S(2)}) copy-start(bf16[1024,1024]{1,0:T(8,128)(2,1)} %cots.1) | copy-start | bytes 6291460
  3.1 11.0 %collective-permute-start = (bf16[512,512]{1,0:T(8,128)(2,1)}, bf16[512,512]{1,0:T(8,128)(2,1)S(1)}, u32[]{:S(2)}, u32[]{:S(2)}) collective-permute-start(bf16[512,512]{1,0:T(8,128)(2,1)} %shard_map.55), channel_id=1, source_target_pairs={{0,16},{16,0},{1,17},{17,1},{2,18},{18,2},{3,19},{19,3},{4,20},{20... | collective-permute-start | bytes 1572872 | tf_op jit(solution)/shard_map/ppermute | solution.py:185
  11.9 11.8 %copy-start = (bf16[4,512,512]{2,1,0:T(8,128)(2,1)S(1)}, bf16[4,512,512]{2,1,0:T(8,128)(2,1)}, u32[]{:S(2)}) copy-start(bf16[4,512,512]{2,1,0:T(8,128)(2,1)} %right.1) | copy-start | bytes 6291460
  11.9 11.8 %copy-start.2 = (bf16[4,16,512]{2,1,0:T(8,128)(2,1)S(1)}, bf16[4,16,512]{2,1,0:T(8,128)(2,1)}, u32[]{:S(2)}) copy-start(bf16[4,16,512]{2,1,0:T(8,128)(2,1)} %left.1) | copy-start | bytes 196612
  11.9 11.8 %copy-start.3 = (s32[32]{0:T(128)S(1)}, s32[32]{0:T(128)}, u32[]{:S(2)}) copy-start(s32[32]{0:T(128)} %owners) | copy-start | bytes 388
  14.2 11.1 %collective-permute-start.1 = (bf16[128,512]{1,0:T(8,128)(2,1)S(1)}, bf16[128,512]{1,0:T(8,128)(2,1)S(1)}, u32[]{:S(2)}, u32[]{:S(2)}) collective-permute-start(bf16[128,512]{1,0:T(8,128)(2,1)S(1)} %get-tuple-element.30), channel_id=1, source_target_pairs={{0,48},{16,480},{48,64},{32,16},{64,112},{80,32},{112,128},{96,80}... | collective-permute-start | bytes 393224 | tf_op jit(solution)/shard_map/ppermute | solution.py:195
  19.8 9.3 %collective-permute-start.2 = (bf16[128,512]{1,0:T(8,128)(2,1)S(1)}, bf16[128,512]{1,0:T(8,128)(2,1)S(1)}, u32[]{:S(2)}, u32[]{:S(2)}) collective-permute-start(bf16[128,512]{1,0:T(8,128)(2,1)S(1)} %get-tuple-element.31), channel_id=1, source_target_pairs={{0,448},{16,80},{48,496},{32,96},{64,0},{80,144},{112,48},{96,160}... | collective-permute-start | bytes 393224 | tf_op jit(solution)/shard_map/ppermute | solution.py:195
  21.7 7.7 %collective-permute-start.3 = (bf16[128,512]{1,0:T(8,128)(2,1)S(1)}, bf16[128,512]{1,0:T(8,128)(2,1)S(1)}, u32[]{:S(2)}, u32[]{:S(2)}) collective-permute-start(bf16[128,512]{1,0:T(8,128)(2,1)S(1)} %get-tuple-element.32), channel_id=1, source_target_pairs={{0,496},{16,32},{48,0},{32,80},{64,48},{80,96},{112,64},{96,144},{... | collective-permute-start | bytes 393224 | tf_op jit(solution)/shard_map/ppermute | solution.py:195
  25.3 4.2 %copy-start.1 = (bf16[16,128,512]{2,1,0:T(8,128)(2,1)}, bf16[16,128,512]{2,1,0:T(8,128)(2,1)S(1)}, u32[]{:S(2)}) copy-start(bf16[16,128,512]{2,1,0:T(8,128)(2,1)S(1)} %get-tuple-element.42) | copy-start | bytes 6291460
  29.5 12.7 %collective-permute-start.4 = (bf16[64,512]{1,0:T(8,128)(2,1)S(1)}, bf16[64,512]{1,0:T(8,128)(2,1)S(1)}, u32[]{:S(2)}, u32[]{:S(2)}) collective-permute-start(bf16[64,512]{1,0:T(8,128)(2,1)S(1)} %get-tuple-element.36), channel_id=1, source_target_pairs={{0,128},{16,400},{48,176},{32,416},{64,192},{80,464},{112,240},{96... | collective-permute-start | bytes 196616 | tf_op jit(solution)/shard_map/ppermute | solution.py:195
  35.0 17.2 %all-to-all-start = ((bf16[32,16,384]{2,1,0:T(8,128)(2,1)}), bf16[32,16,384]{2,1,0:T(8,128)(2,1)S(1)}, u32[]{:S(2)}, u32[]{:S(2)}) async-start(bf16[32,16,384]{2,1,0:T(8,128)(2,1)} %get-tuple-element.41), calls=%async_computation | async-start | bytes 786432 | tf_op jit(solution)/shard_map/all_to_all | solution.py:219
  42.3 14.1 %collective-permute-start.5 = (bf16[32,512]{1,0:T(8,128)(2,1)S(1)}, bf16[32,512]{1,0:T(8,128)(2,1)S(1)}, u32[]{:S(2)}, u32[]{:S(2)}) collective-permute-start(bf16[32,512]{1,0:T(8,128)(2,1)S(1)} %get-tuple-element.40), channel_id=1, source_target_pairs={{0,256},{16,272},{48,304},{32,288},{64,320},{80,336},{112,368},{96... | collective-permute-start | bytes 98312 | tf_op jit(solution)/shard_map/ppermute | solution.py:195
  52.2 35.3 %all-to-all-start.1 = ((bf16[16,128,512]{2,1,0:T(8,128)(2,1)}), bf16[16,128,512]{2,1,0:T(8,128)(2,1)S(1)}, u32[]{:S(2)}, u32[]{:S(2)}) async-start(bf16[16,128,512]{2,1,0:T(8,128)(2,1)} %copy-done.1), calls=%async_computation.1 | async-start | bytes 4194304 | tf_op jit(solution)/shard_map/all_to_all | solution.py:227
